TPU v7x, 32 devices: a whole 2x2x4 slice. The times are simulated.
32 devices in a mesh: groups: 2 (over y), ex: 4 (over z), feat: 2 (over x), pb: 2 (over core).
Axes of the slice: x: 2, y: 2, z: 4, core: 2. Of those that a mesh axis runs over, the one named last changes fastest.
Arguments:
- activations: bfloat16 [8, 4, 128, 4096], P(('groups', 'ex'), ('feat', 'pb')), parts along dimension 0, may hold values from -6 to 6
- out_grads: bfloat16 [8, 4, 128, 7168], P(('groups', 'ex'), ('feat', 'pb')), parts along dimension 0
- act_proj: bfloat16 [4096, 64], replicated
- grad_proj: bfloat16 [7168, 64], replicated
- tok_counts: int32 [8, 4], P(('groups', 'ex'), ('feat', 'pb')), parts along dimension 0, may hold values from 1 to 128, as said below
- example_ids: int32 [8, 4], P('groups', ('feat', 'pb')), parts along dimension 0, may hold values from 0 to 15, as said below
- query_sketch: bfloat16 [2048, 4096], P(('groups', 'pb'), 'ex'), parts along dimension 0, may hold values from -6 to 6
- query_ids: int32 [2048], P('groups'), parts along dimension 0, may hold values from 0 to 31
Outputs:
- gram: float32 [8192, 4096], P(('groups', 'ex'), ('feat', 'pb')), parts along dimension 0
- scores: float32 [2048, 4, 4], P(('groups', 'ex'), None, ('feat', 'pb')), parts along dimension 0
There are 2 independent parts, one for each index of `groups`. A program takes and returns all parts, laid end to end along the dimension named above; an argument that names none is the same for every part. Nothing has to cross between parts.
Inputs may be any that keep to these rules, and one draw needn't show every extreme that they name: `tok_counts`: some example has all 128 tokens live. `example_ids`: all different.
All inputs are finite; a program needn't handle non-finite values.
Results may differ from a plain program's by a relative error of at most 0.0075.
Values may be sent and summed in bfloat16 or wider, within the bound.
No kernel may reach another device: no remote copies, remote signals or barrier semaphores. Data moves between devices by JAX's collectives and lax.ppermute only.
A program may use at most 64 MiB of HBM per device.

v0:
```python
import math

import jax
import jax.numpy as jnp
from jax import lax
from jax.sharding import PartitionSpec as P

DAMPING = 0.1


def shards(
    activations, out_grads, act_proj, grad_proj, tok_counts, example_ids, query_sketch, query_ids
):
    seq_len = activations.shape[2]
    proj_rank = act_proj.shape[1]
    sketch_width = proj_rank * proj_rank
    ex_count = lax.axis_size("ex")
    fp_count = lax.axis_size(("feat", "pb"))
    examples_all = ex_count * fp_count
    block_width = sketch_width // ex_count
    fp_width = sketch_width // fp_count
    act_low = jnp.dot(activations[0, 0], act_proj, preferred_element_type=jnp.float32).astype(
        jnp.bfloat16
    )
    grad_low = jnp.dot(out_grads[0, 0], grad_proj, preferred_element_type=jnp.float32).astype(
        jnp.bfloat16
    )
    keep_mask = (jnp.arange(seq_len, dtype=jnp.int32) < tok_counts[0, 0]).astype(jnp.bfloat16)
    kept = grad_low * keep_mask[:, None]
    outer_sum = jnp.dot(kept.T, act_low, preferred_element_type=jnp.float32) * (
        1.0 / math.sqrt(seq_len)
    )
    sketch_row = outer_sum.reshape(1, sketch_width).astype(jnp.bfloat16)
    feat_block = lax.all_to_all(sketch_row, "ex", split_axis=1, concat_axis=0, tiled=True)
    columns = lax.all_gather(feat_block[:, None, :], ("feat", "pb"), axis=1, tiled=True)
    flat_cols = columns.reshape(examples_all, block_width)
    offset_fp = lax.axis_index(("feat", "pb")) * fp_width
    right_cols = lax.dynamic_slice_in_dim(
        lax.all_gather(sketch_row, ("ex", "feat", "pb"), axis=0, tiled=True), offset_fp, fp_width, 1
    )
    gram_sum = jnp.dot(flat_cols.T, right_cols, preferred_element_type=jnp.float32)
    gram = gram_sum / examples_all
    squares = sketch_row[0].astype(jnp.float32)
    all_squares = lax.psum(squares * squares, ("ex", "feat", "pb"))
    diag_block = (
        lax.dynamic_slice_in_dim(all_squares, lax.axis_index("ex") * block_width, block_width, 0)
        / examples_all
    )
    all_queries = lax.all_gather(query_sketch, "pb", axis=0, tiled=True)
    scaled = (
        all_queries.astype(jnp.float32) / (math.sqrt(sketch_width) * (diag_block + DAMPING))
    ).astype(jnp.bfloat16)
    query_rows = scaled.shape[0] // ex_count
    score_part = lax.psum_scatter(
        jnp.dot(scaled, feat_block.T, preferred_element_type=jnp.float32),
        "ex",
        scatter_dimension=0,
        tiled=True,
    )
    query_here = lax.dynamic_slice_in_dim(
        query_ids, lax.axis_index("ex") * query_rows, query_rows, 0
    )
    self_pair = query_here[:, None] == example_ids[:, 0][None, :]
    scores = jnp.where(self_pair, jnp.float32(0.0), score_part)[:, :, None]
    return (gram, scores)


def solution(mesh):
    return jax.shard_map(
        shards,
        mesh=mesh,
        in_specs=(
            P(("groups", "ex"), ("feat", "pb"), None, None),
            P(("groups", "ex"), ("feat", "pb"), None, None),
            P(),
            P(),
            P(("groups", "ex"), ("feat", "pb")),
            P("groups", ("feat", "pb")),
            P(("groups", "pb"), "ex"),
            P("groups"),
        ),
        out_specs=(P(("groups", "ex"), ("feat", "pb")), P(("groups", "ex"), None, ("feat", "pb"))),
        check_vma=False,
    )
```

profile of v0, /device:TPU:0, one launch (start us, length us, event | category | flops | bytes accessed | tf_op | source)
XLA Modules:
  0.0 137.4 jit_solution(17156239788834478004)
XLA Ops:
  7.2 0.0 copy-start
  7.2 0.0 copy-start.1
  7.2 0.0 all-gather.4.cloned.1.call-start
  7.2 0.7 all-gather.4.cloned.1.call-update
  8.7 1.8 %convolution_convert_fusion = bf16[128,64]{0,1:T(8,128)(2,1)S(1)} fusion(bf16[4096,64]{0,1:T(8,128)(2,1)} %param.10, bf16[1,1,128,4096]{3,2,1,0:T(8,128)(2,1)} %param.8), kind=kOutput, calls=%fused_computation.6 | convolution fusion | flops 67117056 | bytes 1589248 | tf_op jit(solution)/shard_map/dot_general | solution.py:22
  10.5 0.0 copy-done
  10.5 0.0 copy-done.1
  10.5 0.9 convert_multiply_fusion
  11.4 0.1 convert_element_type.58
  11.5 0.5 broadcast.9
  12.0 0.7 reduce.1
  12.7 0.6 reshape.63
  13.3 6.3 %all-to-all-start = ((bf16[4,2,512]{2,1,0:T(2,128)(2,1)}), bf16[4,2,512]{2,1,0:T(2,128)(2,1)S(1)}, u32[]{:S(2)}, u32[]{:S(2)}) async-start(bf16[4,2,512]{2,1,0:T(2,128)(2,1)} %reshape.63), calls=%async_computation | async-start | bytes 16384 | tf_op jit(solution)/shard_map/all_to_all | solution.py:34
  19.6 0.0 reduce-scatter.4.cloned.1.call-start
  19.6 0.1 reshape.56
  19.7 0.1 mul.46
  19.8 61.1 %psum.7 = f32[4096]{0:T(1024)S(1)} all-reduce(f32[4096]{0:T(1024)S(1)} %mul.46), channel_id=1, replica_groups=mesh['groups'=2,'ex'=4,'feat'=2,'pb'=2] {'ex','feat','pb'}, use_global_device_ids=true, to_apply=%region_0.0 | all-reduce | flops 4096 | bytes 32768 | tf_op jit(solution)/shard_map/psum | solution.py:44
  80.9 17.8 %all-gather.1 = bf16[16,1,4096]{2,1,0:T(2,128)(2,1)S(1)} all-gather(bf16[1,1,4096]{2,1,0:T(2,128)(2,1)S(1)} %reshape.56), channel_id=1, replica_groups=mesh['groups'=2,'ex'=4,'feat'=2,'pb'=2] {'ex','feat','pb'}, dimensions={0}, use_global_device_ids=true | all-gather | bytes 139264 | tf_op jit(solution)/shard_map/all_gather | solution.py:39
  98.8 0.1 constant_dynamic-slice_fusion
  98.8 0.8 dynamic_slice.10
  99.6 0.0 all-to-all-done
  99.6 5.5 %all-gather = bf16[1,4,4096]{2,0,1:T(2,128)(2,1)S(1)} all-gather(bf16[1,4,1024]{2,0,1:T(2,128)(2,1)S(1)} %bitcast.32), channel_id=2, replica_groups=mesh['groups'=2,'ex'=4,'feat'=2,'pb'=2] {'feat','pb'}, dimensions={2}, use_global_device_ids=true | all-gather | bytes 40960 | tf_op jit(solution)/shard_map/all_gather | solution.py:35
  105.2 0.2 reduce
  105.4 0.0 all-gather.4.cloned.1.call-done
  105.4 3.1 %fusion = f32[1024,4]{1,0:T(8,128)} fusion(bf16[1024,1024]{1,0:T(8,128)(2,1)} %all-gather.4.cloned.1.call-done, f32[1024]{0:T(1024)S(1)} %add_multiply_fusion, bf16[1,4,1024]{2,0,1:T(2,128)(2,1)S(1)} %bitcast.33), kind=kOutput, calls=%fused_computation.2 | convolution fusion | flops 11534336 | bytes 2125824
  108.5 0.0 reduce-scatter.4.cloned.1.call-update
  108.5 0.0 copy-start.2
  108.5 2.7 %convolution_multiply_fusion = f32[1024,1024]{1,0:T(8,128)} fusion(bf16[16,1024]{1,0:T(8,128)(2,1)S(1)} %reshape.53, bf16[16,1,1024]{2,1,0:T(2,128)(2,1)S(1)} %constant_dynamic-slice_fusion), kind=kOutput, calls=%fused_computation.1 | convolution fusion | flops 34603008 | bytes 4259840 | tf_op jit(solution)/shard_map/dot_general | solution.py:41
  111.3 17.6 %reduce-scatter.4.cloned.1.call-done = f32[256,4]{1,0:T(8,128)} async-done(((f32[1024,4]{1,0:T(8,128)}), f32[256,4]{1,0:T(8,128)}) %reduce-scatter.4.cloned.1.call-update) | async-done | bytes 4112
  128.9 1.0 copy.20
  129.9 0.1 select_bitcast_fusion
  129.9 0.6 copy.18
  (5 shorter events, 0.1 us)
Async XLA Ops:
  7.2 3.3 %copy-start = (bf16[1,1,128,7168]{3,2,1,0:T(8,128)(2,1)S(1)}, bf16[1,1,128,7168]{3,2,1,0:T(8,128)(2,1)}, u32[]{:S(2)}) copy-start(bf16[1,1,128,7168]{3,2,1,0:T(8,128)(2,1)} %param.9) | copy-start | bytes 5505028
  7.2 3.3 %copy-start.1 = (bf16[7168,64]{0,1:T(8,128)(2,1)S(1)}, bf16[7168,64]{0,1:T(8,128)(2,1)}, u32[]{:S(2)}) copy-start(bf16[7168,64]{0,1:T(8,128)(2,1)} %param.11) | copy-start | bytes 2752516
  7.2 98.2 %all-gather.4.cloned.1.call-start = ((), (), s32[]{:S(2)}) async-start(), calls=%async_computation.2 | async-start | bytes 3145728 | tf_op jit(solution)/shard_map/all_gather | solution.py:49
  13.3 86.3 %all-to-all-start = ((bf16[4,2,512]{2,1,0:T(2,128)(2,1)}), bf16[4,2,512]{2,1,0:T(2,128)(2,1)S(1)}, u32[]{:S(2)}, u32[]{:S(2)}) async-start(bf16[4,2,512]{2,1,0:T(2,128)(2,1)} %reshape.63), calls=%async_computation | async-start | bytes 16384 | tf_op jit(solution)/shard_map/all_to_all | solution.py:34
  19.6 109.2 %reduce-scatter.4.cloned.1.call-start = ((), (), s32[]{:S(2)}) async-start(), calls=%async_computation.3 | async-start | bytes 655360
  108.5 21.4 %copy-start.2 = (s32[4,1]{0,1:T(1,128)S(1)}, s32[4,1]{0,1:T(1,128)}, u32[]{:S(2)}) copy-start(s32[4,1]{0,1:T(1,128)} %param.13) | copy-start | bytes 52
Sparse Core Ops, SparseCore 0:
  9.6 13.2 all-gather.3
  108.6 20.2 reduce-scatter.3
where the time goes:
time: 138 us; the launch traced here: 137 us
  blocking collectives  84.5 us (61%)
  waiting for transfers between devices  18.3 us (13%)
  between operations  14.9 us (11%)
  matrix products  8.53 us (6%)
  starting transfers between devices  6.36 us (5%)
  local copies, waits for them, and re-layouts  3.86 us (3%)
    psum x1, blocking collectives, shards(): all_squares = lax.psum(squares * squares, ('ex', 'feat', 'pb'))  61.1 us
    unnamed x3, waiting for transfers between devices  18.3 us
    all_gather x1, blocking collectives, shards(): lax.all_gather(sketch_row, ('ex', 'feat', 'pb'), axis=0, tiled=True)  17.8 us
    all_to_all x1, starting transfers between devices, shards(): lax.all_to_all(sketch_row, 'ex', split_axis=1, concat_axis=0, tiled=True)  6.32 us
    all_gather x1, blocking collectives, shards(): lax.all_gather(feat_block[:, None, :], ('feat', 'pb'), axis=1, tiled=True)  5.52 us
    unnamed x1, matrix products  3.08 us
    unnamed x12, local copies, waits for them, and re-layouts  2.84 us
  transfers between devices with their start and end apart: 3, of which 1 were waited for; matrix products, arithmetic and copies ran while one was open for 6% of the time, Pallas kernels for 0%

commit v1 on v0

v1 whole, which is shorter than its diff:
```python
import functools
import math

import jax
import jax.numpy as jnp
from jax import lax
from jax.experimental import pallas as pl
from jax.experimental.pallas import tpu as pltpu
from jax.sharding import PartitionSpec as P

DAMPING = 0.1
ACT_CUTS = 2
GRAD_CUTS = 4
NT = (((1,), (1,)), ((), ()))


def partner(index, step, count):
    if count & (count - 1) == 0:
        return index ^ step
    return (index + step) % count


def source(index, step, count):
    if count & (count - 1) == 0:
        return index ^ step
    return lax.rem(index + count - step, count)


def exchange(block, axis, step):
    count = lax.axis_size(axis)
    return lax.ppermute(block, axis, [(i, partner(i, step, count)) for i in range(count)])


def sketch_kernel(
    acts_hbm, grads_hbm, act_proj_hbm, grad_proj_hbm, count_ref, out_ref,
    acts, grads, act_proj, grad_proj, turned, act_sems, grad_sems,
):
    seq_len = acts.shape[0]
    rank = act_proj.shape[0]

    def copies(source_hbm, target, sems, slot, cuts):
        width = target.shape[1] // cuts
        return [
            pltpu.make_async_copy(
                source_hbm.at[:, pl.ds(c * width, width)],
                target.at[:, pl.ds(c * width, width)],
                sems.at[slot, c],
            )
            for c in range(cuts)
        ]

    act_copies = list(
        zip(
            copies(act_proj_hbm, act_proj, act_sems, 0, ACT_CUTS),
            copies(acts_hbm, acts, act_sems, 1, ACT_CUTS),
        )
    )
    grad_copies = list(
        zip(
            copies(grad_proj_hbm, grad_proj, grad_sems, 0, GRAD_CUTS),
            copies(grads_hbm, grads, grad_sems, 1, GRAD_CUTS),
        )
    )
    for pair in act_copies + grad_copies:
        for copy in pair:
            copy.start()
    act_width = acts.shape[1] // ACT_CUTS
    act_sum = jnp.zeros((seq_len, rank), jnp.float32)
    for c, pair in enumerate(act_copies):
        for copy in pair:
            copy.wait()
        cols = pl.ds(c * act_width, act_width)
        act_sum += lax.dot_general(
            acts[:, cols], act_proj[:, cols], NT, preferred_element_type=jnp.float32
        )
    grad_width = grads.shape[1] // GRAD_CUTS
    grad_sum = jnp.zeros((rank, seq_len), jnp.float32)
    for c, pair in enumerate(grad_copies):
        for copy in pair:
            copy.wait()
        cols = pl.ds(c * grad_width, grad_width)
        grad_sum += lax.dot_general(
            grad_proj[:, cols], grads[:, cols], NT, preferred_element_type=jnp.float32
        )
    live = lax.broadcasted_iota(jnp.int32, (rank, seq_len), 1) < count_ref[0, 0]
    turned[...] = jnp.where(live, grad_sum, 0.0)
    act_low = act_sum.astype(jnp.bfloat16)
    halves = [
        jnp.dot(
            turned[pl.ds(side, rank // 2, stride=2), :].astype(jnp.bfloat16),
            act_low,
            preferred_element_type=jnp.float32,
        )
        for side in range(2)
    ]
    outer = jnp.concatenate(halves, axis=1) * (1.0 / math.sqrt(seq_len))
    out_ref[...] = outer.astype(jnp.bfloat16)


def make_sketch(acts, grads, act_proj, grad_proj, tok_count):
    seq_len, width = acts.shape
    hidden = grads.shape[1]
    rank = act_proj.shape[0]
    return pl.pallas_call(
        sketch_kernel,
        out_shape=jax.ShapeDtypeStruct((rank // 2, 2 * rank), jnp.bfloat16),
        in_specs=[pl.BlockSpec(memory_space=pl.ANY)] * 4
        + [pl.BlockSpec(memory_space=pltpu.SMEM)],
        out_specs=pl.BlockSpec(memory_space=pltpu.VMEM),
        scratch_shapes=[
            pltpu.VMEM((seq_len, width), jnp.bfloat16),
            pltpu.VMEM((seq_len, hidden), jnp.bfloat16),
            pltpu.VMEM((rank, width), jnp.bfloat16),
            pltpu.VMEM((rank, hidden), jnp.bfloat16),
            pltpu.VMEM((rank, seq_len), jnp.float32),
            pltpu.SemaphoreType.DMA((2, ACT_CUTS)),
            pltpu.SemaphoreType.DMA((2, GRAD_CUTS)),
        ],
        compiler_params=pltpu.CompilerParams(vmem_limit_bytes=16 * 2**20),
        name="sketch",
    )(acts, grads, act_proj, grad_proj, tok_count)


def place_rows(sizes, pieces, rows):
    ex_count, feat_count, pb_count = sizes
    ex, feat, pb = lax.axis_index("ex"), lax.axis_index("feat"), lax.axis_index("pb")
    for k in range(ex_count):
        for s in range(feat_count * pb_count):
            column = (
                source(feat, s // pb_count, feat_count) * pb_count
                + source(pb, s % pb_count, pb_count)
            )
            rows[column * ex_count + source(ex, k, ex_count)] = pieces[k][s].astype(jnp.float32)


def score_kernel(sizes, query_ref, *refs):
    ex_count, feat_count, pb_count = sizes
    pieces, refs = refs[:ex_count], refs[ex_count:]
    outs, (rows, scaled, result, chunks) = refs[:-4], refs[-4:]
    ex, feat, pb = lax.axis_index("ex"), lax.axis_index("feat"), lax.axis_index("pb")
    fp_count = feat_count * pb_count
    examples = ex_count * fp_count
    lines, lanes = rows.shape[1:]
    block_lines = lines // ex_count
    place_rows(sizes, pieces, rows)
    block = rows[:, pl.ds(ex * block_lines, block_lines), :]
    diag = jnp.sum(block * block, axis=0) / examples
    weight = 1.0 / (math.sqrt(lines * lanes) * (diag + DAMPING))
    scaled[...] = (block * weight[None]).reshape(examples * block_lines, lanes)
    parts = [scaled[pl.ds(j, examples, stride=block_lines), :] for j in range(block_lines)]
    wide = jnp.concatenate(parts, axis=1)
    high = wide.astype(jnp.bfloat16)
    low = (wide - high.astype(jnp.float32)).astype(jnp.bfloat16)
    both = jnp.concatenate([high, low], axis=0)
    products = lax.dot_general(both, query_ref[...], NT, preferred_element_type=jnp.float32)
    result[...] = (products[:examples] + products[examples:]).reshape(result.shape)
    width = query_ref.shape[0] // (ex_count // pb_count)
    for t in range(ex_count):
        column = feat * pb_count + t % pb_count
        chunks[t] = result[column, :, pl.ds((t // pb_count) * width, width)]
    for j in range(ex_count):
        outs[j][...] = chunks[partner(ex, j, ex_count)]


def partial_scores(sizes, queries, pieces):
    ex_count, feat_count, pb_count = sizes
    examples = ex_count * feat_count * pb_count
    lines, lanes = pieces[0].shape[1:]
    chunk = (ex_count, queries.shape[0] * pb_count // ex_count)
    vmem = pl.BlockSpec(memory_space=pltpu.VMEM)
    return pl.pallas_call(
        functools.partial(score_kernel, sizes),
        out_shape=[jax.ShapeDtypeStruct(chunk, jnp.float32)] * ex_count,
        in_specs=[vmem] * (1 + ex_count),
        out_specs=[vmem] * ex_count,
        scratch_shapes=[
            pltpu.VMEM((examples, lines, lanes), jnp.float32),
            pltpu.VMEM((examples * (lines // ex_count), lanes), jnp.float32),
            pltpu.VMEM((feat_count * pb_count, ex_count, queries.shape[0]), jnp.float32),
            pltpu.VMEM((ex_count, *chunk), jnp.float32),
        ],
        compiler_params=pltpu.CompilerParams(vmem_limit_bytes=24 * 2**20),
        name="scores",
    )(queries, *pieces)


def gram_kernel(sizes, *refs):
    ex_count, feat_count, pb_count = sizes
    pieces, (out_ref, rows, left, right) = refs[:ex_count], refs[ex_count:]
    ex = lax.axis_index("ex")
    fp_count = feat_count * pb_count
    examples = ex_count * fp_count
    lines, lanes = rows.shape[1:]
    left_lines, right_lines = lines // ex_count, lines // fp_count

    @pl.when(pl.program_id(0) == 0)
    def _():
        fp = lax.axis_index("feat") * pb_count + lax.axis_index("pb")
        place_rows(sizes, pieces, rows)
        left_block = rows[:, pl.ds(ex * left_lines, left_lines), :]
        left[...] = left_block.reshape(examples * left_lines, lanes)
        right_block = rows[:, pl.ds(fp * right_lines, right_lines), :]
        right[...] = right_block.reshape(examples * right_lines, lanes)

    here = left[pl.ds(pl.program_id(0), examples, stride=left_lines), :].T.astype(jnp.bfloat16)
    across = jnp.concatenate(
        [right[pl.ds(j, examples, stride=right_lines), :] for j in range(right_lines)], axis=1
    ).astype(jnp.bfloat16)
    out_ref[...] = jnp.dot(here, across, preferred_element_type=jnp.float32) * (1.0 / examples)


def make_gram(sizes, pieces):
    ex_count, feat_count, pb_count = sizes
    fp_count = feat_count * pb_count
    examples = ex_count * fp_count
    lines, lanes = pieces[0].shape[1:]
    left_lines, right_lines = lines // ex_count, lines // fp_count
    whole = pl.BlockSpec(memory_space=pltpu.VMEM)
    return pl.pallas_call(
        functools.partial(gram_kernel, sizes),
        grid=(left_lines,),
        out_shape=jax.ShapeDtypeStruct((left_lines * lanes, right_lines * lanes), jnp.float32),
        in_specs=[whole] * ex_count,
        out_specs=pl.BlockSpec((lanes, right_lines * lanes), lambda i: (i, 0)),
        scratch_shapes=[
            pltpu.VMEM((examples, lines, lanes), jnp.float32),
            pltpu.VMEM((examples * left_lines, lanes), jnp.float32),
            pltpu.VMEM((examples * right_lines, lanes), jnp.float32),
        ],
        compiler_params=pltpu.CompilerParams(vmem_limit_bytes=24 * 2**20),
        cost_estimate=pl.CostEstimate(
            flops=2 * 256 * left_lines * lanes * right_lines * lanes,
            bytes_accessed=4 * left_lines * lanes * right_lines * lanes,
            transcendentals=0,
        ),
        name="gram",
    )(*pieces)


def shards(
    activations, out_grads, act_proj, grad_proj, tok_counts, example_ids, query_sketch, query_ids
):
    ex_count, feat_count, pb_count = (lax.axis_size(axis) for axis in ("ex", "feat", "pb"))
    sizes = (ex_count, feat_count, pb_count)
    sketch = make_sketch(
        activations[0, 0], out_grads[0, 0], act_proj.T, grad_proj.T, tok_counts
    )
    block = sketch[None]
    for axis, count in (("pb", pb_count), ("feat", feat_count)):
        block = jnp.concatenate([block] + [exchange(block, axis, k) for k in range(1, count)])
    pieces = [block] + [exchange(block, "ex", k) for k in range(1, ex_count)]
    chunks = partial_scores(sizes, query_sketch, pieces)
    half = ex_count // pb_count
    arrived = [
        lax.ppermute(
            chunk,
            ("ex", "pb"),
            [
                (
                    e * pb_count + p,
                    (p * half + partner(e, j, ex_count) // pb_count) * pb_count
                    + partner(e, j, ex_count) % pb_count,
                )
                for e in range(ex_count)
                for p in range(pb_count)
            ],
        )
        for j, chunk in enumerate(chunks)
    ]
    gram = make_gram(sizes, pieces)
    width = query_ids.shape[0] // ex_count
    query_here = lax.dynamic_slice_in_dim(query_ids, lax.axis_index("ex") * width, width, 0)
    self_pair = example_ids == query_here[None, :]
    scores = jnp.where(self_pair, jnp.float32(0.0), sum(arrived))
    return gram, scores.T[:, :, None]


def solution(mesh):
    return jax.shard_map(
        shards,
        mesh=mesh,
        in_specs=(
            P(("groups", "ex"), ("feat", "pb"), None, None),
            P(("groups", "ex"), ("feat", "pb"), None, None),
            P(),
            P(),
            P(("groups", "ex"), ("feat", "pb")),
            P("groups", ("feat", "pb")),
            P(("groups", "pb"), "ex"),
            P("groups"),
        ),
        out_specs=(P(("groups", "ex"), ("feat", "pb")), P(("groups", "ex"), None, ("feat", "pb"))),
        check_vma=False,
    )
```

time: 138 us -> 37.1 us (0.27)
  the two profiles are of different devices: /device:TPU:0 before, /device:TPU:11 now
where the time goes in v1:
time: 37.1 us; the launch traced here: 36.7 us
  starting transfers between devices  17 us (46%)
  Pallas kernels  7.58 us (20%)
  local copies, waits for them, and re-layouts  6.3 us (17%)
  waiting for transfers between devices  4.41 us (12%)
  between operations  1.34 us (4%)
    ppermute x4, starting transfers between devices, shards(): lax.ppermute(chunk, ('ex', 'pb'), [(e * pb_count + p, (p * half + partner...  12.5 us
    unnamed x13, local copies, waits for them, and re-layouts  5.54 us
    pallas_call x1, Pallas kernels, make_gram(): pl.pallas_call(functools.partial(gram_kernel, sizes), grid=(left_lines,),...  4.63 us
    ppermute x5, starting transfers between devices, exchange(): lax.ppermute(block, axis, [(i, partner(i, step, count)) for i in range(co...  4.49 us
    ppermute x5, waiting for transfers between devices, exchange(): lax.ppermute(block, axis, [(i, partner(i, step, count)) for i in range(co...  4.4 us
    pallas_call x1, Pallas kernels, make_sketch(): pl.pallas_call(sketch_kernel, out_shape=jax.ShapeDtypeStruct((rank // 2,...  2.55 us
    dynamic_slice x1, local copies, waits for them, and re-layouts, shards(): lax.dynamic_slice_in_dim(query_ids, lax.axis_index('ex') * width, width, 0)  0.76 us
  transfers between devices with their start and end apart: 9, of which 4 were waited for; matrix products, arithmetic and copies ran while one was open for 2% of the time, Pallas kernels for 13%

profile of v1, /device:TPU:11, one launch (start us, length us, event | category | flops | bytes accessed | tf_op | source)
XLA Modules:
  0.0 36.7 jit_solution(12419006343402253087)
XLA Ops:
  1.3 0.0 copy-start
  1.3 1.5 %copy-done = bf16[1,1,128,7168]{3,2,1,0:T(8,128)(2,1)S(1)} copy-done((bf16[1,1,128,7168]{3,2,1,0:T(8,128)(2,1)S(1)}, bf16[1,1,128,7168]{3,2,1,0:T(8,128)(2,1)}, u32[]{:S(2)}) %copy-start) | copy-done | bytes 1835032
  2.8 0.0 copy-start.1
  2.8 1.2 %copy-done.1 = bf16[1,1,128,4096]{3,2,1,0:T(8,128)(2,1)S(1)} copy-done((bf16[1,1,128,4096]{3,2,1,0:T(8,128)(2,1)S(1)}, bf16[1,1,128,4096]{3,2,1,0:T(8,128)(2,1)}, u32[]{:S(2)}) %copy-start.1) | copy-done | bytes 1048600
  4.0 1.2 %copy-done.3 = bf16[7168,64]{0,1:T(8,128)(2,1)S(1)} copy-done((bf16[7168,64]{0,1:T(8,128)(2,1)S(1)}, bf16[7168,64]{0,1:T(8,128)(2,1)}, u32[]{:S(2)}) %copy-start.3) | copy-done | bytes 917528
  5.2 1.0 %copy-done.4 = bf16[4096,64]{0,1:T(8,128)(2,1)S(1)} copy-done((bf16[4096,64]{0,1:T(8,128)(2,1)S(1)}, bf16[4096,64]{0,1:T(8,128)(2,1)}, u32[]{:S(2)}) %copy-start.4) | copy-done | bytes 524312
  6.2 2.5 %sketch.1 = bf16[32,128]{1,0:T(8,128)(2,1)S(1)} custom-call(bf16[128,4096]{1,0:T(8,128)(2,1)S(1)} %bitcast.11, bf16[128,7168]{1,0:T(8,128)(2,1)S(1)} %bitcast.10, bf16[64,4096]{1,0:T(8,128)(2,1)S(1)} %bitcast.13, bf16[64,7168]{1,0:T(8,128)(2,1)S(1)} %bitcast.12, s32[1,1]{1,0:T(1,128)S(6)} %copy.11.count_ref), custom_call_target="tpu_custom_call" | custom-call | tf_op jit(solution)/shard_map/sketch/pallas_call | solution.py:104
  8.8 0.7 %collective-permute-start = (bf16[1,32,128]{2,1,0:T(8,128)(2,1)S(1)}, bf16[1,32,128]{2,1,0:T(8,128)(2,1)S(1)}, u32[]{:S(2)}, u32[]{:S(2)}) collective-permute-start(bf16[1,32,128]{2,1,0:T(8,128)(2,1)S(1)} %bitcast.14), channel_id=1, source_target_pairs={{0,1},{1,0},{2,3},{3,2},{4,5},{5,4},{6,7},{7,6},{8,9},{9,8},{10,11... | collective-permute-start | bytes 24584 | tf_op jit(solution)/shard_map/ppermute | solution.py:31
  9.5 0.8 %collective-permute-done = bf16[1,32,128]{2,1,0:T(8,128)(2,1)S(1)} collective-permute-done((bf16[1,32,128]{2,1,0:T(8,128)(2,1)S(1)}, bf16[1,32,128]{2,1,0:T(8,128)(2,1)S(1)}, u32[]{:S(2)}, u32[]{:S(2)}) %collective-permute-start) | collective-permute-done | bytes 8224 | tf_op jit(solution)/shard_map/ppermute | solution.py:31
  10.4 0.3 collective-permute-start.1
  10.6 2.3 %collective-permute-done.1 = bf16[2,32,128]{2,1,0:T(8,128)(2,1)S(1)} collective-permute-done((bf16[2,32,128]{2,1,0:T(8,128)(2,1)S(1)}, bf16[2,32,128]{2,1,0:T(8,128)(2,1)S(1)}, u32[]{:S(2)}, u32[]{:S(2)}) %collective-permute-start.1) | collective-permute-done | bytes 16416 | tf_op jit(solution)/shard_map/ppermute | solution.py:31
  13.0 1.3 %collective-permute-start.4 = (bf16[4,32,128]{2,1,0:T(8,128)(2,1)S(1)}, bf16[4,32,128]{2,1,0:T(8,128)(2,1)S(1)}, u32[]{:S(2)}, u32[]{:S(2)}) collective-permute-start(bf16[4,32,128]{2,1,0:T(8,128)(2,1)S(1)} %pad_maximum_fusion.refs_0_), channel_id=1, source_target_pairs={{0,12},{4,8},{8,4},{12,0},{1,13},{5,9},{9,5},{13,1},{2,14},{6,10},... | collective-permute-start | bytes 98312 | tf_op jit(solution)/shard_map/ppermute | solution.py:31
  14.3 1.1 %collective-permute-start.3 = (bf16[4,32,128]{2,1,0:T(8,128)(2,1)S(1)}, bf16[4,32,128]{2,1,0:T(8,128)(2,1)S(1)}, u32[]{:S(2)}, u32[]{:S(2)}) collective-permute-start(bf16[4,32,128]{2,1,0:T(8,128)(2,1)S(1)} %pad_maximum_fusion.refs_0_), channel_id=1, source_target_pairs={{0,8},{4,12},{8,0},{12,4},{1,9},{5,13},{9,1},{13,5},{2,10},{6,14},... | collective-permute-start | bytes 98312 | tf_op jit(solution)/shard_map/ppermute | solution.py:31
  15.3 1.1 %collective-permute-start.2 = (bf16[4,32,128]{2,1,0:T(8,128)(2,1)S(1)}, bf16[4,32,128]{2,1,0:T(8,128)(2,1)S(1)}, u32[]{:S(2)}, u32[]{:S(2)}) collective-permute-start(bf16[4,32,128]{2,1,0:T(8,128)(2,1)S(1)} %pad_maximum_fusion.refs_0_), channel_id=1, source_target_pairs={{0,4},{4,0},{8,12},{12,8},{1,5},{5,1},{9,13},{13,9},{2,6},{6,2},{1... | collective-permute-start | bytes 98312 | tf_op jit(solution)/shard_map/ppermute | solution.py:31
  16.5 0.8 %dynamic_slice.3 = s32[256]{0:T(256)S(1)} dynamic-slice(s32[1024]{0:T(1024)} %param.15, s32[]{:T(128)S(6)} %select_n.7), dynamic_slice_sizes={256} | dynamic-slice | bytes 2052 | tf_op jit(solution)/shard_map/dynamic_slice | solution.py:272
  17.2 0.0 collective-permute-done.4.refs_3_
  17.2 0.8 %collective-permute-done.3.refs_2_ = bf16[4,32,128]{2,1,0:T(8,128)(2,1)S(1)} collective-permute-done((bf16[4,32,128]{2,1,0:T(8,128)(2,1)S(1)}, bf16[4,32,128]{2,1,0:T(8,128)(2,1)S(1)}, u32[]{:S(2)}, u32[]{:S(2)}) %collective-permute-start.3) | collective-permute-done | bytes 32800 | tf_op jit(solution)/shard_map/ppermute | solution.py:31
  18.0 0.4 %collective-permute-done.2.refs_1_ = bf16[4,32,128]{2,1,0:T(8,128)(2,1)S(1)} collective-permute-done((bf16[4,32,128]{2,1,0:T(8,128)(2,1)S(1)}, bf16[4,32,128]{2,1,0:T(8,128)(2,1)S(1)}, u32[]{:S(2)}, u32[]{:S(2)}) %collective-permute-start.2) | collective-permute-done | bytes 32800 | tf_op jit(solution)/shard_map/ppermute | solution.py:31
  18.4 0.0 copy-done.2
  18.5 0.4 %scores.1 = (f32[4,256]{1,0:T(4,128)S(1)}, f32[4,256]{1,0:T(4,128)S(1)}, f32[4,256]{1,0:T(4,128)S(1)}, f32[4,256]{1,0:T(4,128)S(1)}) custom-call(bf16[512,1024]{1,0:T(8,128)(2,1)S(1)} %copy-done.2, bf16[4,32,128]{2,1,0:T(8,128)(2,1)S(1)} %pad_maximum_fusion.refs_0_, bf16[4,32,128]{2,1,0:T(8,128)(2,1)S(1)} %collective-permute-done.2.refs_1_, ...), custom_call_target="tpu_custom_call" | custom-call | tf_op jit(solution)/shard_map/scores/pallas_call | solution.py:171
  18.9 4.2 %collective-permute-start.5 = (f32[4,256]{1,0:T(4,128)S(1)}, f32[4,256]{1,0:T(4,128)S(1)}, u32[]{:S(2)}, u32[]{:S(2)}) collective-permute-start(f32[4,256]{1,0:T(4,128)S(1)} %get-tuple-element.6), channel_id=1, source_target_pairs={{0,0},{1,8},{4,1},{5,9},{8,4},{9,12},{12,5},{13,13},{2,2},{3,10},{... | collective-permute-start | bytes 12296 | tf_op jit(solution)/shard_map/ppermute | solution.py:255
  23.1 2.8 %collective-permute-start.6 = (f32[4,256]{1,0:T(4,128)S(1)}, f32[4,256]{1,0:T(4,128)S(1)}, u32[]{:S(2)}, u32[]{:S(2)}) collective-permute-start(f32[4,256]{1,0:T(4,128)S(1)} %get-tuple-element.7), channel_id=1, source_target_pairs={{0,1},{1,9},{4,0},{5,8},{8,5},{9,13},{12,4},{13,12},{2,3},{3,11},{... | collective-permute-start | bytes 12296 | tf_op jit(solution)/shard_map/ppermute | solution.py:255
  25.9 0.0 collective-permute-start.7
  25.9 5.5 %collective-permute-start.8 = (f32[4,256]{1,0:T(4,128)S(1)}, f32[4,256]{1,0:T(4,128)S(1)}, u32[]{:S(2)}, u32[]{:S(2)}) collective-permute-start(f32[4,256]{1,0:T(4,128)S(1)} %get-tuple-element.9), channel_id=1, source_target_pairs={{0,5},{1,13},{4,4},{5,12},{8,1},{9,9},{12,0},{13,8},{2,7},{3,15},{... | collective-permute-start | bytes 12296 | tf_op jit(solution)/shard_map/ppermute | solution.py:255
  31.4 4.6 %gram.1 = f32[1024,1024]{1,0:T(8,128)} custom-call(bf16[4,32,128]{2,1,0:T(8,128)(2,1)S(1)} %pad_maximum_fusion.refs_0_, bf16[4,32,128]{2,1,0:T(8,128)(2,1)S(1)} %collective-permute-done.2.refs_1_, bf16[4,32,128]{2,1,0:T(8,128)(2,1)S(1)} %collective-permute-done.3.refs_2_, bf16[4,32,128]{2,1,0:T(8,128)(2,1)S(1)} %collective-permute-done.4.refs_3_), custom_call_target="tpu_custom_call" | custom-call | flops 536870912 | bytes 4194304 | tf_op jit(solution)/shard_map/gram/pallas_call | solution.py:219
  36.0 0.0 collective-permute-done.5
  36.0 0.0 collective-permute-done.6
  36.0 0.0 collective-permute-done.7
  36.1 0.0 collective-permute-done.8
  36.1 0.0 copy-done.5
  36.1 0.1 select_bitcast_fusion
  36.1 0.6 %copy.10 = f32[256,4,1]{0,2,1:T(1,128)} copy(f32[256,4,1]{0,1,2:T(4,128)S(1)} %select_bitcast_fusion) | data formatting | bytes 8192
  (6 shorter events, 0.0 us)
Async XLA Ops:
  1.3 1.5 %copy-start = (bf16[1,1,128,7168]{3,2,1,0:T(8,128)(2,1)S(1)}, bf16[1,1,128,7168]{3,2,1,0:T(8,128)(2,1)}, u32[]{:S(2)}) copy-start(bf16[1,1,128,7168]{3,2,1,0:T(8,128)(2,1)} %param.9) | copy-start | bytes 5505028
  2.8 1.2 %copy-start.1 = (bf16[1,1,128,4096]{3,2,1,0:T(8,128)(2,1)S(1)}, bf16[1,1,128,4096]{3,2,1,0:T(8,128)(2,1)}, u32[]{:S(2)}) copy-start(bf16[1,1,128,4096]{3,2,1,0:T(8,128)(2,1)} %param.8) | copy-start | bytes 3145732
  4.0 1.2 %copy-start.3 = (bf16[7168,64]{0,1:T(8,128)(2,1)S(1)}, bf16[7168,64]{0,1:T(8,128)(2,1)}, u32[]{:S(2)}) copy-start(bf16[7168,64]{0,1:T(8,128)(2,1)} %param.11) | copy-start | bytes 2752516
  5.2 1.0 %copy-start.4 = (bf16[4096,64]{0,1:T(8,128)(2,1)S(1)}, bf16[4096,64]{0,1:T(8,128)(2,1)}, u32[]{:S(2)}) copy-start(bf16[4096,64]{0,1:T(8,128)(2,1)} %param.10) | copy-start | bytes 1572868
  6.2 12.2 %copy-start.2 = (bf16[512,1024]{1,0:T(8,128)(2,1)S(1)}, bf16[512,1024]{1,0:T(8,128)(2,1)}, u32[]{:S(2)}) copy-start(bf16[512,1024]{1,0:T(8,128)(2,1)} %query_ref.1) | copy-start | bytes 3145732
  6.2 29.8 %copy-start.5 = (s32[4,1]{0,1:T(1,128)S(1)}, s32[4,1]{0,1:T(1,128)}, u32[]{:S(2)}) copy-start(s32[4,1]{0,1:T(1,128)} %param.13) | copy-start | bytes 52
  8.8 1.6 %collective-permute-start = (bf16[1,32,128]{2,1,0:T(8,128)(2,1)S(1)}, bf16[1,32,128]{2,1,0:T(8,128)(2,1)S(1)}, u32[]{:S(2)}, u32[]{:S(2)}) collective-permute-start(bf16[1,32,128]{2,1,0:T(8,128)(2,1)S(1)} %bitcast.14), channel_id=1, source_target_pairs={{0,1},{1,0},{2,3},{3,2},{4,5},{5,4},{6,7},{7,6},{8,9},{9,8},{10,11... | collective-permute-start | bytes 24584 | tf_op jit(solution)/shard_map/ppermute | solution.py:31
  10.4 2.6 %collective-permute-start.1 = (bf16[2,32,128]{2,1,0:T(8,128)(2,1)S(1)}, bf16[2,32,128]{2,1,0:T(8,128)(2,1)S(1)}, u32[]{:S(2)}, u32[]{:S(2)}) collective-permute-start(bf16[2,32,128]{2,1,0:T(8,128)(2,1)S(1)} %pad_maximum_fusion.1), channel_id=1, source_target_pairs={{0,2},{2,0},{1,3},{3,1},{4,6},{6,4},{5,7},{7,5},{8,10},{10,8},{9,1... | collective-permute-start | bytes 49160 | tf_op jit(solution)/shard_map/ppermute | solution.py:31
  13.0 4.3 %collective-permute-start.4 = (bf16[4,32,128]{2,1,0:T(8,128)(2,1)S(1)}, bf16[4,32,128]{2,1,0:T(8,128)(2,1)S(1)}, u32[]{:S(2)}, u32[]{:S(2)}) collective-permute-start(bf16[4,32,128]{2,1,0:T(8,128)(2,1)S(1)} %pad_maximum_fusion.refs_0_), channel_id=1, source_target_pairs={{0,12},{4,8},{8,4},{12,0},{1,13},{5,9},{9,5},{13,1},{2,14},{6,10},... | collective-permute-start | bytes 98312 | tf_op jit(solution)/shard_map/ppermute | solution.py:31
  14.3 3.8 %collective-permute-start.3 = (bf16[4,32,128]{2,1,0:T(8,128)(2,1)S(1)}, bf16[4,32,128]{2,1,0:T(8,128)(2,1)S(1)}, u32[]{:S(2)}, u32[]{:S(2)}) collective-permute-start(bf16[4,32,128]{2,1,0:T(8,128)(2,1)S(1)} %pad_maximum_fusion.refs_0_), channel_id=1, source_target_pairs={{0,8},{4,12},{8,0},{12,4},{1,9},{5,13},{9,1},{13,5},{2,10},{6,14},... | collective-permute-start | bytes 98312 | tf_op jit(solution)/shard_map/ppermute | solution.py:31
  15.3 3.1 %collective-permute-start.2 = (bf16[4,32,128]{2,1,0:T(8,128)(2,1)S(1)}, bf16[4,32,128]{2,1,0:T(8,128)(2,1)S(1)}, u32[]{:S(2)}, u32[]{:S(2)}) collective-permute-start(bf16[4,32,128]{2,1,0:T(8,128)(2,1)S(1)} %pad_maximum_fusion.refs_0_), channel_id=1, source_target_pairs={{0,4},{4,0},{8,12},{12,8},{1,5},{5,1},{9,13},{13,9},{2,6},{6,2},{1... | collective-permute-start | bytes 98312 | tf_op jit(solution)/shard_map/ppermute | solution.py:31
  18.9 17.2 %collective-permute-start.5 = (f32[4,256]{1,0:T(4,128)S(1)}, f32[4,256]{1,0:T(4,128)S(1)}, u32[]{:S(2)}, u32[]{:S(2)}) collective-permute-start(f32[4,256]{1,0:T(4,128)S(1)} %get-tuple-element.6), channel_id=1, source_target_pairs={{0,0},{1,8},{4,1},{5,9},{8,4},{9,12},{12,5},{13,13},{2,2},{3,10},{... | collective-permute-start | bytes 12296 | tf_op jit(solution)/shard_map/ppermute | solution.py:255
  23.1 13.0 %collective-permute-start.6 = (f32[4,256]{1,0:T(4,128)S(1)}, f32[4,256]{1,0:T(4,128)S(1)}, u32[]{:S(2)}, u32[]{:S(2)}) collective-permute-start(f32[4,256]{1,0:T(4,128)S(1)} %get-tuple-element.7), channel_id=1, source_target_pairs={{0,1},{1,9},{4,0},{5,8},{8,5},{9,13},{12,4},{13,12},{2,3},{3,11},{... | collective-permute-start | bytes 12296 | tf_op jit(solution)/shard_map/ppermute | solution.py:255
  25.9 10.2 %collective-permute-start.7 = (f32[4,256]{1,0:T(4,128)S(1)}, f32[4,256]{1,0:T(4,128)S(1)}, u32[]{:S(2)}, u32[]{:S(2)}) collective-permute-start(f32[4,256]{1,0:T(4,128)S(1)} %get-tuple-element.8), channel_id=1, source_target_pairs={{0,4},{1,12},{4,5},{5,13},{8,0},{9,8},{12,1},{13,9},{2,6},{3,14},{... | collective-permute-start | bytes 12296 | tf_op jit(solution)/shard_map/ppermute | solution.py:255
  25.9 10.2 %collective-permute-start.8 = (f32[4,256]{1,0:T(4,128)S(1)}, f32[4,256]{1,0:T(4,128)S(1)}, u32[]{:S(2)}, u32[]{:S(2)}) collective-permute-start(f32[4,256]{1,0:T(4,128)S(1)} %get-tuple-element.9), channel_id=1, source_target_pairs={{0,5},{1,13},{4,4},{5,12},{8,1},{9,9},{12,0},{13,8},{2,7},{3,15},{... | collective-permute-start | bytes 12296 | tf_op jit(solution)/shard_map/ppermute | solution.py:255

commit v2 on v1

v2 whole, which is shorter than its diff:
```python
import functools
import math

import jax
import jax.numpy as jnp
from jax import lax
from jax.experimental import pallas as pl
from jax.experimental.pallas import tpu as pltpu
from jax.sharding import PartitionSpec as P

DAMPING = 0.1
ACT_CUTS = 2
GRAD_CUTS = 4
NT = (((1,), (1,)), ((), ()))


def exchange(block, axis, step):
    return lax.ppermute(block, axis, [(i, i ^ step) for i in range(lax.axis_size(axis))])


def sketch_kernel(
    acts_hbm, grads_hbm, act_proj_hbm, grad_proj_hbm, count_ref, out_ref,
    acts, grads, act_proj, grad_proj, turned, act_sems, grad_sems,
):
    seq_len = acts.shape[0]
    rank = act_proj.shape[0]

    def copies(source_hbm, target, sems, slot, cuts):
        width = target.shape[1] // cuts
        return [
            pltpu.make_async_copy(
                source_hbm.at[:, pl.ds(c * width, width)],
                target.at[:, pl.ds(c * width, width)],
                sems.at[slot, c],
            )
            for c in range(cuts)
        ]

    act_copies = list(
        zip(
            copies(act_proj_hbm, act_proj, act_sems, 0, ACT_CUTS),
            copies(acts_hbm, acts, act_sems, 1, ACT_CUTS),
        )
    )
    grad_copies = list(
        zip(
            copies(grad_proj_hbm, grad_proj, grad_sems, 0, GRAD_CUTS),
            copies(grads_hbm, grads, grad_sems, 1, GRAD_CUTS),
        )
    )
    for pair in act_copies + grad_copies:
        for copy in pair:
            copy.start()
    act_width = acts.shape[1] // ACT_CUTS
    act_sum = jnp.zeros((seq_len, rank), jnp.float32)
    for c, pair in enumerate(act_copies):
        for copy in pair:
            copy.wait()
        cols = pl.ds(c * act_width, act_width)
        act_sum += lax.dot_general(
            acts[:, cols], act_proj[:, cols], NT, preferred_element_type=jnp.float32
        )
    grad_width = grads.shape[1] // GRAD_CUTS
    grad_sum = jnp.zeros((rank, seq_len), jnp.float32)
    for c, pair in enumerate(grad_copies):
        for copy in pair:
            copy.wait()
        cols = pl.ds(c * grad_width, grad_width)
        grad_sum += lax.dot_general(
            grad_proj[:, cols], grads[:, cols], NT, preferred_element_type=jnp.float32
        )
    live = lax.broadcasted_iota(jnp.int32, (rank, seq_len), 1) < count_ref[...]
    turned[...] = jnp.where(live, grad_sum, 0.0)
    act_low = act_sum.astype(jnp.bfloat16)
    halves = [
        jnp.dot(
            turned[pl.ds(side, rank // 2, stride=2), :].astype(jnp.bfloat16),
            act_low,
            preferred_element_type=jnp.float32,
        )
        for side in range(2)
    ]
    outer = jnp.concatenate(halves, axis=1) * (1.0 / math.sqrt(seq_len))
    out_ref[...] = outer.astype(jnp.bfloat16)


def make_sketch(acts, grads, act_proj, grad_proj, tok_count):
    seq_len, width = acts.shape
    hidden = grads.shape[1]
    rank = act_proj.shape[0]
    return pl.pallas_call(
        sketch_kernel,
        out_shape=jax.ShapeDtypeStruct((rank // 2, 2 * rank), jnp.bfloat16),
        in_specs=[pl.BlockSpec(memory_space=pl.ANY)] * 4
        + [pl.BlockSpec(memory_space=pltpu.VMEM)],
        out_specs=pl.BlockSpec(memory_space=pltpu.VMEM),
        scratch_shapes=[
            pltpu.VMEM((seq_len, width), jnp.bfloat16),
            pltpu.VMEM((seq_len, hidden), jnp.bfloat16),
            pltpu.VMEM((rank, width), jnp.bfloat16),
            pltpu.VMEM((rank, hidden), jnp.bfloat16),
            pltpu.VMEM((rank, seq_len), jnp.float32),
            pltpu.SemaphoreType.DMA((2, ACT_CUTS)),
            pltpu.SemaphoreType.DMA((2, GRAD_CUTS)),
        ],
        compiler_params=pltpu.CompilerParams(vmem_limit_bytes=60 * 2**20),
        name="sketch",
    )(acts, grads, act_proj, grad_proj, tok_count)


def place_rows(sizes, pieces, rows):
    ex_count, fp_count = sizes[0], sizes[1] * sizes[2]
    ex = lax.axis_index("ex")
    fp = lax.axis_index("feat") * sizes[2] + lax.axis_index("pb")
    for k in range(ex_count):
        for s in range(fp_count):
            rows[(fp ^ s) * ex_count + (ex ^ k)] = pieces[k][s].astype(jnp.float32)


def score_kernel(sizes, query_ref, *refs):
    ex_count, feat_count, pb_count = sizes
    half = ex_count // pb_count
    pieces, outs = refs[:ex_count], refs[ex_count : ex_count + half]
    rows, scaled, chunks = refs[-3:]
    ex, feat = lax.axis_index("ex"), lax.axis_index("feat")
    examples, lines, lanes = rows.shape
    block_lines = lines // ex_count
    mine = ex_count * pb_count
    place_rows(sizes, pieces, rows)
    block = rows[:, pl.ds(ex * block_lines, block_lines), :]
    diag = jnp.sum(block * block, axis=0) / examples
    weight = 1.0 / (math.sqrt(lines * lanes) * (diag + DAMPING))
    own = rows[pl.ds(feat * mine, mine), pl.ds(ex * block_lines, block_lines), :]
    scaled[...] = (own * weight[None]).reshape(mine * block_lines, lanes)
    parts = [scaled[pl.ds(j, mine, stride=block_lines), :] for j in range(block_lines)]
    wide = jnp.concatenate(parts, axis=1)
    high = wide.astype(jnp.bfloat16)
    low = (wide - high.astype(jnp.float32)).astype(jnp.bfloat16)
    both = jnp.concatenate([high, low], axis=0)
    products = lax.dot_general(both, query_ref[...], NT, preferred_element_type=jnp.float32)
    result = products[:mine] + products[mine:]
    width = chunks.shape[2]
    for t in range(half):
        chunks[t] = result[:, t * width : (t + 1) * width]
    for i in range(half):
        outs[i][...] = chunks[lax.rem(ex, half) ^ i]


def partial_scores(sizes, queries, pieces):
    ex_count, feat_count, pb_count = sizes
    examples = ex_count * feat_count * pb_count
    lines, lanes = pieces[0].shape[1:]
    half = ex_count // pb_count
    chunk = (pb_count * ex_count, queries.shape[0] // half)
    vmem = pl.BlockSpec(memory_space=pltpu.VMEM)
    return pl.pallas_call(
        functools.partial(score_kernel, sizes),
        out_shape=[jax.ShapeDtypeStruct(chunk, jnp.float32)] * half,
        in_specs=[vmem] * (1 + ex_count),
        out_specs=[vmem] * half,
        scratch_shapes=[
            pltpu.VMEM((examples, lines, lanes), jnp.float32),
            pltpu.VMEM((pb_count * lines, lanes), jnp.float32),
            pltpu.VMEM((half, *chunk), jnp.float32),
        ],
        compiler_params=pltpu.CompilerParams(vmem_limit_bytes=24 * 2**20),
        name="scores",
    )(queries, *pieces)


def gram_kernel(sizes, *refs):
    ex_count, fp_count = sizes[0], sizes[1] * sizes[2]
    pieces, (out_hbm, rows, left, right, result, sems) = refs[:ex_count], refs[ex_count:]
    ex = lax.axis_index("ex")
    fp = lax.axis_index("feat") * sizes[2] + lax.axis_index("pb")
    examples, lines, lanes = rows.shape
    left_lines, right_lines = lines // ex_count, lines // fp_count
    place_rows(sizes, pieces, rows)
    block = rows[:, pl.ds(ex * left_lines, left_lines), :]
    left[...] = block.reshape(examples * left_lines, lanes)
    block = rows[:, pl.ds(fp * right_lines, right_lines), :]
    right[...] = block.reshape(examples * right_lines, lanes)
    across = jnp.concatenate(
        [right[pl.ds(j, examples, stride=right_lines), :] for j in range(right_lines)], axis=1
    ).astype(jnp.bfloat16)
    copies = []
    for i in range(left_lines):
        here = left[pl.ds(i, examples, stride=left_lines), :].T.astype(jnp.bfloat16)
        band = pl.ds(i * lanes, lanes)
        total = jnp.dot(here, across, preferred_element_type=jnp.float32)
        result[band, :] = total * (1.0 / examples)
        copies.append(
            pltpu.make_async_copy(result.at[band, :], out_hbm.at[band, :], sems.at[i])
        )
        copies[-1].start()
    for copy in copies:
        copy.wait()


def make_gram(sizes, pieces):
    ex_count, fp_count = sizes[0], sizes[1] * sizes[2]
    examples = ex_count * fp_count
    lines, lanes = pieces[0].shape[1:]
    left_lines, right_lines = lines // ex_count, lines // fp_count
    shape = (left_lines * lanes, right_lines * lanes)
    return pl.pallas_call(
        functools.partial(gram_kernel, sizes),
        out_shape=jax.ShapeDtypeStruct(shape, jnp.float32),
        in_specs=[pl.BlockSpec(memory_space=pltpu.VMEM)] * ex_count,
        out_specs=pl.BlockSpec(memory_space=pl.ANY),
        scratch_shapes=[
            pltpu.VMEM((examples, lines, lanes), jnp.float32),
            pltpu.VMEM((examples * left_lines, lanes), jnp.float32),
            pltpu.VMEM((examples * right_lines, lanes), jnp.float32),
            pltpu.VMEM(shape, jnp.float32),
            pltpu.SemaphoreType.DMA((left_lines,)),
        ],
        compiler_params=pltpu.CompilerParams(vmem_limit_bytes=24 * 2**20),
        cost_estimate=pl.CostEstimate(
            flops=2 * 256 * shape[0] * shape[1],
            bytes_accessed=4 * shape[0] * shape[1],
            transcendentals=0,
        ),
        name="gram",
    )(*pieces)


def to_owners(chunks, ex_count, pb_count):
    half = ex_count // pb_count
    pairs = [
        [
            (e * pb_count + p, (e ^ (((e // half) ^ p) * half + i)) * pb_count + e // half)
            for e in range(ex_count)
            for p in range(pb_count)
        ]
        for i in range(half)
    ]
    return sum(lax.ppermute(chunk, ("ex", "pb"), pairs[i]) for i, chunk in enumerate(chunks))


def shards(
    activations, out_grads, act_proj, grad_proj, tok_counts, example_ids, query_sketch, query_ids
):
    ex_count, feat_count, pb_count = (lax.axis_size(axis) for axis in ("ex", "feat", "pb"))
    sizes = (ex_count, feat_count, pb_count)
    sketch = make_sketch(
        activations[0, 0], out_grads[0, 0], act_proj.T, grad_proj.T, tok_counts
    )
    block = sketch[None]
    for axis, count in (("pb", pb_count), ("feat", feat_count)):
        block = jnp.concatenate([block] + [exchange(block, axis, k) for k in range(1, count)])
    pieces = [block] + [exchange(block, "ex", k) for k in range(1, ex_count)]
    part = to_owners(partial_scores(sizes, query_sketch, pieces), ex_count, pb_count)
    gram = make_gram(sizes, pieces)
    part = part.reshape(pb_count, ex_count, -1)
    pb = lax.axis_index("pb")
    total = lax.dynamic_index_in_dim(part, pb, 0, keepdims=False)
    for k in range(1, pb_count):
        theirs = lax.dynamic_index_in_dim(part, pb ^ k, 0, keepdims=False)
        total += exchange(theirs, "pb", k)
    width = query_ids.shape[0] // ex_count
    query_here = lax.dynamic_slice_in_dim(query_ids, lax.axis_index("ex") * width, width, 0)
    self_pair = example_ids == query_here[None, :]
    scores = jnp.where(self_pair, jnp.float32(0.0), total)
    return gram, scores.T[:, :, None]


def solution(mesh):
    return jax.shard_map(
        shards,
        mesh=mesh,
        in_specs=(
            P(("groups", "ex"), ("feat", "pb"), None, None),
            P(("groups", "ex"), ("feat", "pb"), None, None),
            P(),
            P(),
            P(("groups", "ex"), ("feat", "pb")),
            P("groups", ("feat", "pb")),
            P(("groups", "pb"), "ex"),
            P("groups"),
        ),
        out_specs=(P(("groups", "ex"), ("feat", "pb")), P(("groups", "ex"), None, ("feat", "pb"))),
        check_vma=False,
    )
```

time: 37.1 us -> 35.5 us (0.957)
  the two profiles are of different devices: /device:TPU:11 before, /device:TPU:0 now
where the time goes in v2:
time: 35.5 us; the launch traced here: 35.2 us
  starting transfers between devices  13.5 us (38%)
  waiting for transfers between devices  9.81 us (28%)
  Pallas kernels  7.51 us (21%)
  other arithmetic  1.48 us (4%)
  between operations  1.46 us (4%)
  local copies, waits for them, and re-layouts  1.39 us (4%)
    ppermute x6, starting transfers between devices, exchange(): lax.ppermute(block, axis, [(i, i ^ step) for i in range(lax.axis_size(axi...  12.8 us
    ppermute x6, waiting for transfers between devices, exchange(): lax.ppermute(block, axis, [(i, i ^ step) for i in range(lax.axis_size(axi...  6.94 us
    pallas_call x1, Pallas kernels, make_sketch(): pl.pallas_call(sketch_kernel, out_shape=jax.ShapeDtypeStruct((rank // 2,...  4.76 us
    ppermute x2, waiting for transfers between devices, to_owners(): lax.ppermute(chunk, ('ex', 'pb'), pairs[i])  2.86 us
    pallas_call x1, Pallas kernels, make_gram(): pl.pallas_call(functools.partial(gram_kernel, sizes), out_shape=jax.Shape...  2.38 us
    concatenate x2, other arithmetic, shards(): jnp.concatenate([block] + [exchange(block, axis, k) for k in range(1, cou...  1.4 us
    dynamic_slice x1, local copies, waits for them, and re-layouts, shards(): lax.dynamic_slice_in_dim(query_ids, lax.axis_index('ex') * width, width, 0)  0.76 us
    ppermute x2, starting transfers between devices, to_owners(): lax.ppermute(chunk, ('ex', 'pb'), pairs[i])  0.75 us
  transfers between devices with their start and end apart: 8, of which 5 were waited for; matrix products, arithmetic and copies ran while one was open for 2% of the time, Pallas kernels for 7%

profile of v2, /device:TPU:0, one launch (start us, length us, event | category | flops | bytes accessed | tf_op | source)
XLA Modules:
  0.0 35.2 jit_solution(10353719444148145525)
XLA Ops:
  0.6 0.0 copy-start
  1.4 0.0 copy-start.1
  1.4 4.8 %sketch.1 = bf16[32,128]{1,0:T(8,128)(2,1)} custom-call(bf16[128,4096]{1,0:T(8,128)(2,1)} %bitcast.19, bf16[128,7168]{1,0:T(8,128)(2,1)} %bitcast.18, bf16[64,4096]{1,0:T(8,128)(2,1)} %bitcast.21, bf16[64,7168]{1,0:T(8,128)(2,1)} %bitcast.20, s32[1,1]{1,0:T(1,128)S(6)} %copy.10.count_ref), custom_call_target="tpu_custom_call" | custom-call | tf_op jit(solution)/shard_map/sketch/pallas_call | solution.py:91
  6.2 0.5 %collective-permute-start = (bf16[1,32,128]{2,1,0:T(8,128)(2,1)}, bf16[1,32,128]{2,1,0:T(8,128)(2,1)S(1)}, u32[]{:S(2)}, u32[]{:S(2)}) collective-permute-start(bf16[1,32,128]{2,1,0:T(8,128)(2,1)} %bitcast.22), channel_id=1, source_target_pairs={{0,1},{1,0},{2,3},{3,2},{4,5},{5,4},{6,7},{7,6},{8,9},{9,8},{10,11... | collective-permute-start | bytes 24584 | tf_op jit(solution)/shard_map/ppermute | solution.py:18
  6.7 1.0 %collective-permute-done = bf16[1,32,128]{2,1,0:T(8,128)(2,1)S(1)} collective-permute-done((bf16[1,32,128]{2,1,0:T(8,128)(2,1)}, bf16[1,32,128]{2,1,0:T(8,128)(2,1)S(1)}, u32[]{:S(2)}, u32[]{:S(2)}) %collective-permute-start) | collective-permute-done | bytes 8224 | tf_op jit(solution)/shard_map/ppermute | solution.py:18
  7.7 0.7 %pad_maximum_fusion.1 = bf16[2,32,128]{2,1,0:T(8,128)(2,1)S(1)} fusion(bf16[1,32,128]{2,1,0:T(8,128)(2,1)S(1)} %collective-permute-done, bf16[1,32,128]{2,1,0:T(8,128)(2,1)} %bitcast.23), kind=kLoop, calls=%fused_computation.1 | loop fusion | flops 8192 | bytes 32768 | tf_op jit(solution)/shard_map/concatenate | solution.py:251
  8.4 2.8 %collective-permute-start.1 = (bf16[2,32,128]{2,1,0:T(8,128)(2,1)S(1)}, bf16[2,32,128]{2,1,0:T(8,128)(2,1)S(1)}, u32[]{:S(2)}, u32[]{:S(2)}) collective-permute-start(bf16[2,32,128]{2,1,0:T(8,128)(2,1)S(1)} %pad_maximum_fusion.1), channel_id=1, source_target_pairs={{0,2},{2,0},{1,3},{3,1},{4,6},{6,4},{5,7},{7,5},{8,10},{10,8},{9,1... | collective-permute-start | bytes 49160 | tf_op jit(solution)/shard_map/ppermute | solution.py:18
  11.2 1.7 %collective-permute-done.1 = bf16[2,32,128]{2,1,0:T(8,128)(2,1)S(1)} collective-permute-done((bf16[2,32,128]{2,1,0:T(8,128)(2,1)S(1)}, bf16[2,32,128]{2,1,0:T(8,128)(2,1)S(1)}, u32[]{:S(2)}, u32[]{:S(2)}) %collective-permute-start.1) | collective-permute-done | bytes 16416 | tf_op jit(solution)/shard_map/ppermute | solution.py:18
  13.0 0.7 %pad_maximum_fusion.refs_0_ = bf16[4,32,128]{2,1,0:T(8,128)(2,1)S(1)} fusion(bf16[2,32,128]{2,1,0:T(8,128)(2,1)S(1)} %collective-permute-done.1, bf16[1,32,128]{2,1,0:T(8,128)(2,1)S(1)} %collective-permute-done, bf16[1,32,128]{2,1,0:T(8,128)(2,1)} %bitcast.24), kind=kLoop, calls=%fused_computation | loop fusion | flops 32768 | bytes 65536 | tf_op jit(solution)/shard_map/concatenate | solution.py:251
  13.7 4.1 %collective-permute-start.4 = (bf16[4,32,128]{2,1,0:T(8,128)(2,1)S(1)}, bf16[4,32,128]{2,1,0:T(8,128)(2,1)S(1)}, u32[]{:S(2)}, u32[]{:S(2)}) collective-permute-start(bf16[4,32,128]{2,1,0:T(8,128)(2,1)S(1)} %pad_maximum_fusion.refs_0_), channel_id=1, source_target_pairs={{0,12},{4,8},{8,4},{12,0},{1,13},{5,9},{9,5},{13,1},{2,14},{6,10},... | collective-permute-start | bytes 98312 | tf_op jit(solution)/shard_map/ppermute | solution.py:18
  17.8 0.0 collective-permute-start.3
  17.8 0.6 %collective-permute-start.2 = (bf16[4,32,128]{2,1,0:T(8,128)(2,1)S(1)}, bf16[4,32,128]{2,1,0:T(8,128)(2,1)S(1)}, u32[]{:S(2)}, u32[]{:S(2)}) collective-permute-start(bf16[4,32,128]{2,1,0:T(8,128)(2,1)S(1)} %pad_maximum_fusion.refs_0_), channel_id=1, source_target_pairs={{0,4},{4,0},{8,12},{12,8},{1,5},{5,1},{9,13},{13,9},{2,6},{6,2},{1... | collective-permute-start | bytes 98312 | tf_op jit(solution)/shard_map/ppermute | solution.py:18
  18.4 1.4 %collective-permute-done.4.refs_3_ = bf16[4,32,128]{2,1,0:T(8,128)(2,1)S(1)} collective-permute-done((bf16[4,32,128]{2,1,0:T(8,128)(2,1)S(1)}, bf16[4,32,128]{2,1,0:T(8,128)(2,1)S(1)}, u32[]{:S(2)}, u32[]{:S(2)}) %collective-permute-start.4) | collective-permute-done | bytes 32800 | tf_op jit(solution)/shard_map/ppermute | solution.py:18
  19.8 2.8 %collective-permute-done.3.refs_2_ = bf16[4,32,128]{2,1,0:T(8,128)(2,1)S(1)} collective-permute-done((bf16[4,32,128]{2,1,0:T(8,128)(2,1)S(1)}, bf16[4,32,128]{2,1,0:T(8,128)(2,1)S(1)}, u32[]{:S(2)}, u32[]{:S(2)}) %collective-permute-start.3) | collective-permute-done | bytes 32800 | tf_op jit(solution)/shard_map/ppermute | solution.py:18
  22.6 0.0 collective-permute-done.2.refs_1_
  22.6 0.0 copy-done
  22.6 0.4 %scores.1 = (f32[8,256]{1,0:T(8,128)S(1)}, f32[8,256]{1,0:T(8,128)S(1)}) custom-call(bf16[512,1024]{1,0:T(8,128)(2,1)S(1)} %copy-done, bf16[4,32,128]{2,1,0:T(8,128)(2,1)S(1)} %pad_maximum_fusion.refs_0_, bf16[4,32,128]{2,1,0:T(8,128)(2,1)S(1)} %collective-permute-done.2.refs_1_, bf16[4,32,128]{2,1,0:T(8,128)(2,1)S(1)} %collective-permute-done.3.refs_2_, ...), custom_call_target="tpu_custom_call" | custom-call | tf_op jit(solution)/shard_map/scores/pallas_call | solution.py:156
  23.0 0.7 %collective-permute-start.5 = (f32[8,256]{1,0:T(8,128)S(1)}, f32[8,256]{1,0:T(8,128)S(1)}, u32[]{:S(2)}, u32[]{:S(2)}) collective-permute-start(f32[8,256]{1,0:T(8,128)S(1)} %get-tuple-element.4), channel_id=1, source_target_pairs={{0,0},{1,8},{4,4},{5,12},{8,1},{9,9},{12,5},{13,13},{2,2},{3,10},{... | collective-permute-start | bytes 24584 | tf_op jit(solution)/shard_map/ppermute | solution.py:238
  23.7 0.1 collective-permute-start.6
  23.8 0.8 %dynamic_slice.10 = s32[256]{0:T(256)S(1)} dynamic-slice(s32[1024]{0:T(1024)} %param.15, s32[]{:T(128)S(6)} %select_n.14), dynamic_slice_sizes={256} | dynamic-slice | bytes 2052 | tf_op jit(solution)/shard_map/dynamic_slice | solution.py:262
  24.5 0.0 collective-permute-done.5
  24.5 2.9 %collective-permute-done.6 = f32[8,256]{1,0:T(8,128)S(1)} collective-permute-done((f32[8,256]{1,0:T(8,128)S(1)}, f32[8,256]{1,0:T(8,128)S(1)}, u32[]{:S(2)}, u32[]{:S(2)}) %collective-permute-start.6) | collective-permute-done | bytes 8224 | tf_op jit(solution)/shard_map/ppermute | solution.py:238
  27.4 4.7 %collective-permute-start.7 = (f32[4,256]{1,0:T(4,128)S(1)}, f32[4,256]{1,0:T(4,128)S(1)}, u32[]{:S(2)}, u32[]{:S(2)}) collective-permute-start(f32[4,256]{1,0:T(4,128)S(1)} %dynamic-slice_bitcast_fusion), channel_id=1, source_target_pairs={{0,1},{1,0},{2,3},{3,2},{4,5},{5,4},{6,7},{7,6},{8,9},{9,8},{10,11... | collective-permute-start | bytes 12296 | tf_op jit(solution)/shard_map/ppermute | solution.py:18
  32.1 2.4 %gram.1 = f32[1024,1024]{1,0:T(8,128)} custom-call(bf16[4,32,128]{2,1,0:T(8,128)(2,1)S(1)} %pad_maximum_fusion.refs_0_, bf16[4,32,128]{2,1,0:T(8,128)(2,1)S(1)} %collective-permute-done.2.refs_1_, bf16[4,32,128]{2,1,0:T(8,128)(2,1)S(1)} %collective-permute-done.3.refs_2_, bf16[4,32,128]{2,1,0:T(8,128)(2,1)S(1)} %collective-permute-done.4.refs_3_), custom_call_target="tpu_custom_call" | custom-call | flops 536870912 | bytes 4194304 | tf_op jit(solution)/shard_map/gram/pallas_call | solution.py:206
  34.5 0.0 collective-permute-done.7
  34.5 0.0 copy-done.1
  34.5 0.1 fusion.1
  34.6 0.6 %broadcast_in_dim.13 = f32[256,4,1]{0,2,1:T(1,128)} reshape(f32[256,4]{0,1:T(4,128)S(1)} %fusion.1) | data formatting | bytes 8192 | tf_op jit(solution)/shard_map/broadcast_in_dim | solution.py:265
  (3 shorter events, 0.0 us)
Async XLA Ops:
  0.6 22.0 %copy-start = (bf16[512,1024]{1,0:T(8,128)(2,1)S(1)}, bf16[512,1024]{1,0:T(8,128)(2,1)}, u32[]{:S(2)}) copy-start(bf16[512,1024]{1,0:T(8,128)(2,1)} %query_ref.1) | copy-start | bytes 3145732
  1.4 33.1 %copy-start.1 = (s32[4,1]{0,1:T(1,128)S(1)}, s32[4,1]{0,1:T(1,128)}, u32[]{:S(2)}) copy-start(s32[4,1]{0,1:T(1,128)} %param.13) | copy-start | bytes 52
  6.2 1.6 %collective-permute-start = (bf16[1,32,128]{2,1,0:T(8,128)(2,1)}, bf16[1,32,128]{2,1,0:T(8,128)(2,1)S(1)}, u32[]{:S(2)}, u32[]{:S(2)}) collective-permute-start(bf16[1,32,128]{2,1,0:T(8,128)(2,1)} %bitcast.22), channel_id=1, source_target_pairs={{0,1},{1,0},{2,3},{3,2},{4,5},{5,4},{6,7},{7,6},{8,9},{9,8},{10,11... | collective-permute-start | bytes 24584 | tf_op jit(solution)/shard_map/ppermute | solution.py:18
  8.4 4.5 %collective-permute-start.1 = (bf16[2,32,128]{2,1,0:T(8,128)(2,1)S(1)}, bf16[2,32,128]{2,1,0:T(8,128)(2,1)S(1)}, u32[]{:S(2)}, u32[]{:S(2)}) collective-permute-start(bf16[2,32,128]{2,1,0:T(8,128)(2,1)S(1)} %pad_maximum_fusion.1), channel_id=1, source_target_pairs={{0,2},{2,0},{1,3},{3,1},{4,6},{6,4},{5,7},{7,5},{8,10},{10,8},{9,1... | collective-permute-start | bytes 49160 | tf_op jit(solution)/shard_map/ppermute | solution.py:18
  13.7 6.2 %collective-permute-start.4 = (bf16[4,32,128]{2,1,0:T(8,128)(2,1)S(1)}, bf16[4,32,128]{2,1,0:T(8,128)(2,1)S(1)}, u32[]{:S(2)}, u32[]{:S(2)}) collective-permute-start(bf16[4,32,128]{2,1,0:T(8,128)(2,1)S(1)} %pad_maximum_fusion.refs_0_), channel_id=1, source_target_pairs={{0,12},{4,8},{8,4},{12,0},{1,13},{5,9},{9,5},{13,1},{2,14},{6,10},... | collective-permute-start | bytes 98312 | tf_op jit(solution)/shard_map/ppermute | solution.py:18
  17.8 4.8 %collective-permute-start.3 = (bf16[4,32,128]{2,1,0:T(8,128)(2,1)S(1)}, bf16[4,32,128]{2,1,0:T(8,128)(2,1)S(1)}, u32[]{:S(2)}, u32[]{:S(2)}) collective-permute-start(bf16[4,32,128]{2,1,0:T(8,128)(2,1)S(1)} %pad_maximum_fusion.refs_0_), channel_id=1, source_target_pairs={{0,8},{4,12},{8,0},{12,4},{1,9},{5,13},{9,1},{13,5},{2,10},{6,14},... | collective-permute-start | bytes 98312 | tf_op jit(solution)/shard_map/ppermute | solution.py:18
  17.8 4.8 %collective-permute-start.2 = (bf16[4,32,128]{2,1,0:T(8,128)(2,1)S(1)}, bf16[4,32,128]{2,1,0:T(8,128)(2,1)S(1)}, u32[]{:S(2)}, u32[]{:S(2)}) collective-permute-start(bf16[4,32,128]{2,1,0:T(8,128)(2,1)S(1)} %pad_maximum_fusion.refs_0_), channel_id=1, source_target_pairs={{0,4},{4,0},{8,12},{12,8},{1,5},{5,1},{9,13},{13,9},{2,6},{6,2},{1... | collective-permute-start | bytes 98312 | tf_op jit(solution)/shard_map/ppermute | solution.py:18
  23.0 1.5 %collective-permute-start.5 = (f32[8,256]{1,0:T(8,128)S(1)}, f32[8,256]{1,0:T(8,128)S(1)}, u32[]{:S(2)}, u32[]{:S(2)}) collective-permute-start(f32[8,256]{1,0:T(8,128)S(1)} %get-tuple-element.4), channel_id=1, source_target_pairs={{0,0},{1,8},{4,4},{5,12},{8,1},{9,9},{12,5},{13,13},{2,2},{3,10},{... | collective-permute-start | bytes 24584 | tf_op jit(solution)/shard_map/ppermute | solution.py:238
  23.7 3.7 %collective-permute-start.6 = (f32[8,256]{1,0:T(8,128)S(1)}, f32[8,256]{1,0:T(8,128)S(1)}, u32[]{:S(2)}, u32[]{:S(2)}) collective-permute-start(f32[8,256]{1,0:T(8,128)S(1)} %get-tuple-element.5), channel_id=1, source_target_pairs={{0,4},{1,12},{4,0},{5,8},{8,5},{9,13},{12,1},{13,9},{2,6},{3,14},{... | collective-permute-start | bytes 24584 | tf_op jit(solution)/shard_map/ppermute | solution.py:238
  27.4 7.1 %collective-permute-start.7 = (f32[4,256]{1,0:T(4,128)S(1)}, f32[4,256]{1,0:T(4,128)S(1)}, u32[]{:S(2)}, u32[]{:S(2)}) collective-permute-start(f32[4,256]{1,0:T(4,128)S(1)} %dynamic-slice_bitcast_fusion), channel_id=1, source_target_pairs={{0,1},{1,0},{2,3},{3,2},{4,5},{5,4},{6,7},{7,6},{8,9},{9,8},{10,11... | collective-permute-start | bytes 12296 | tf_op jit(solution)/shard_map/ppermute | solution.py:18

commit v3 on v2

--- a/solution.py
+++ b/solution.py
@@ -108,25 +108,53 @@
     )(acts, grads, act_proj, grad_proj, tok_count)
 
 
-def place_rows(sizes, pieces, rows):
+def spread(block, distances):
+    pairs = [
+        (e * len(distances) + p, (e ^ k) * len(distances) + p)
+        for e in range(lax.axis_size("ex"))
+        for p, k in enumerate(distances)
+    ]
+    return lax.ppermute(block, ("ex", "pb"), pairs)
+
+
+def gather_rows(sketch):
+    ex_count = lax.axis_size("ex")
+    fp_count = lax.axis_size(("feat", "pb"))
+    own = sketch[None]
+    block = jnp.concatenate([own] + [exchange(own, ("feat", "pb"), s) for s in range(1, fp_count)])
+    pieces = [(block, (0, 0), 0)]
+    for k in range(1, ex_count, 2):
+        distances = (k, min(k + 1, ex_count - 1))
+        near = spread(block, distances)
+        pieces.append((near, distances, 0))
+        if distances[0] != distances[1]:
+            pieces.append((exchange(near, "pb", 1), distances, 1))
+    return pieces
+
+
+def place_rows(sizes, sources, pieces, rows):
     ex_count, fp_count = sizes[0], sizes[1] * sizes[2]
-    ex = lax.axis_index("ex")
-    fp = lax.axis_index("feat") * sizes[2] + lax.axis_index("pb")
-    for k in range(ex_count):
+    ex, pb = lax.axis_index("ex"), lax.axis_index("pb")
+    fp = lax.axis_index("feat") * sizes[2] + pb
+    for piece, (distances, core) in zip(pieces, sources):
+        first, step = distances[core], distances[1 - core] - distances[core]
+        where = ex ^ (first + step * pb)
         for s in range(fp_count):
-            rows[(fp ^ s) * ex_count + (ex ^ k)] = pieces[k][s].astype(jnp.float32)
-
-
-def score_kernel(sizes, query_ref, *refs):
+            rows[(fp ^ core ^ s) * ex_count + where] = piece[s].astype(jnp.float32)
+
+
+def score_kernel(sizes, sources, query_ref, *refs):
     ex_count, feat_count, pb_count = sizes
     half = ex_count // pb_count
-    pieces, outs = refs[:ex_count], refs[ex_count : ex_count + half]
-    rows, scaled, chunks = refs[-3:]
+    pieces, outs = refs[: len(sources)], refs[len(sources) : len(sources) + half]
+    own_ref, rows, scaled, chunks = refs[-4:]
     ex, feat = lax.axis_index("ex"), lax.axis_index("feat")
+    near = lax.div(ex, half) == lax.axis_index("pb")
+    here = lax.rem(ex, half)
     examples, lines, lanes = rows.shape
     block_lines = lines // ex_count
     mine = ex_count * pb_count
-    place_rows(sizes, pieces, rows)
+    place_rows(sizes, sources, pieces, rows)
     block = rows[:, pl.ds(ex * block_lines, block_lines), :]
     diag = jnp.sum(block * block, axis=0) / examples
     weight = 1.0 / (math.sqrt(lines * lanes) * (diag + DAMPING))
@@ -142,22 +170,25 @@
     width = chunks.shape[2]
     for t in range(half):
         chunks[t] = result[:, t * width : (t + 1) * width]
-    for i in range(half):
-        outs[i][...] = chunks[lax.rem(ex, half) ^ i]
+    shift = near.astype(jnp.int32)
+    for i in range(half - 1):
+        outs[i][...] = chunks[here ^ (i + shift)]
+    outs[half - 1][...] = jnp.where(near, 0.0, chunks[here ^ (half - 1)])
+    own_ref[...] = jnp.where(near, chunks[here], 0.0)
 
 
 def partial_scores(sizes, queries, pieces):
     ex_count, feat_count, pb_count = sizes
     examples = ex_count * feat_count * pb_count
-    lines, lanes = pieces[0].shape[1:]
+    lines, lanes = pieces[0][0].shape[1:]
     half = ex_count // pb_count
     chunk = (pb_count * ex_count, queries.shape[0] // half)
     vmem = pl.BlockSpec(memory_space=pltpu.VMEM)
     return pl.pallas_call(
-        functools.partial(score_kernel, sizes),
-        out_shape=[jax.ShapeDtypeStruct(chunk, jnp.float32)] * half,
-        in_specs=[vmem] * (1 + ex_count),
-        out_specs=[vmem] * half,
+        functools.partial(score_kernel, sizes, [piece[1:] for piece in pieces]),
+        out_shape=[jax.ShapeDtypeStruct(chunk, jnp.float32)] * (half + 1),
+        in_specs=[vmem] * (1 + len(pieces)),
+        out_specs=[vmem] * (half + 1),
         scratch_shapes=[
             pltpu.VMEM((examples, lines, lanes), jnp.float32),
             pltpu.VMEM((pb_count * lines, lanes), jnp.float32),
@@ -165,17 +196,19 @@
         ],
         compiler_params=pltpu.CompilerParams(vmem_limit_bytes=24 * 2**20),
         name="scores",
-    )(queries, *pieces)
-
-
-def gram_kernel(sizes, *refs):
+    )(queries, *[piece[0] for piece in pieces])
+
+
+def gram_kernel(sizes, sources, kept_ref, *refs):
     ex_count, fp_count = sizes[0], sizes[1] * sizes[2]
-    pieces, (out_hbm, rows, left, right, result, sems) = refs[:ex_count], refs[ex_count:]
+    pieces = refs[: len(sources)]
+    out_hbm, kept_out_ref, rows, left, right, result, sems = refs[len(sources) :]
     ex = lax.axis_index("ex")
     fp = lax.axis_index("feat") * sizes[2] + lax.axis_index("pb")
     examples, lines, lanes = rows.shape
     left_lines, right_lines = lines // ex_count, lines // fp_count
-    place_rows(sizes, pieces, rows)
+    kept_out_ref[...] = kept_ref[...]
+    place_rows(sizes, sources, pieces, rows)
     block = rows[:, pl.ds(ex * left_lines, left_lines), :]
     left[...] = block.reshape(examples * left_lines, lanes)
     block = rows[:, pl.ds(fp * right_lines, right_lines), :]
@@ -197,17 +230,20 @@
         copy.wait()
 
 
-def make_gram(sizes, pieces):
+def make_gram(sizes, pieces, kept):
     ex_count, fp_count = sizes[0], sizes[1] * sizes[2]
     examples = ex_count * fp_count
-    lines, lanes = pieces[0].shape[1:]
+    lines, lanes = pieces[0][0].shape[1:]
     left_lines, right_lines = lines // ex_count, lines // fp_count
     shape = (left_lines * lanes, right_lines * lanes)
     return pl.pallas_call(
-        functools.partial(gram_kernel, sizes),
-        out_shape=jax.ShapeDtypeStruct(shape, jnp.float32),
-        in_specs=[pl.BlockSpec(memory_space=pltpu.VMEM)] * ex_count,
-        out_specs=pl.BlockSpec(memory_space=pl.ANY),
+        functools.partial(gram_kernel, sizes, [piece[1:] for piece in pieces]),
+        out_shape=[
+            jax.ShapeDtypeStruct(shape, jnp.float32),
+            jax.ShapeDtypeStruct(kept.shape, kept.dtype),
+        ],
+        in_specs=[pl.BlockSpec(memory_space=pltpu.VMEM)] * (1 + len(pieces)),
+        out_specs=[pl.BlockSpec(memory_space=pl.ANY), pl.BlockSpec(memory_space=pltpu.VMEM)],
         scratch_shapes=[
             pltpu.VMEM((examples, lines, lanes), jnp.float32),
             pltpu.VMEM((examples * left_lines, lanes), jnp.float32),
@@ -222,20 +258,20 @@
             transcendentals=0,
         ),
         name="gram",
-    )(*pieces)
-
-
-def to_owners(chunks, ex_count, pb_count):
-    half = ex_count // pb_count
-    pairs = [
-        [
-            (e * pb_count + p, (e ^ (((e // half) ^ p) * half + i)) * pb_count + e // half)
-            for e in range(ex_count)
-            for p in range(pb_count)
-        ]
-        for i in range(half)
-    ]
-    return sum(lax.ppermute(chunk, ("ex", "pb"), pairs[i]) for i, chunk in enumerate(chunks))
+    )(kept, *[piece[0] for piece in pieces])
+
+
+def to_owners(chunks, ex_count):
+    half = ex_count // 2
+    arrived = []
+    for i, chunk in enumerate(chunks):
+        pairs = []
+        for e in range(ex_count):
+            near, far = e // half, 1 - e // half
+            pairs.append((e * 2 + near, (e ^ (i + 1 if i < half - 1 else 1)) * 2 + near))
+            pairs.append((e * 2 + far, (e ^ (half + i)) * 2 + near))
+        arrived.append(lax.ppermute(chunk, ("ex", "pb"), pairs))
+    return sum(arrived)
 
 
 def shards(
@@ -246,18 +282,14 @@
     sketch = make_sketch(
         activations[0, 0], out_grads[0, 0], act_proj.T, grad_proj.T, tok_counts
     )
-    block = sketch[None]
-    for axis, count in (("pb", pb_count), ("feat", feat_count)):
-        block = jnp.concatenate([block] + [exchange(block, axis, k) for k in range(1, count)])
-    pieces = [block] + [exchange(block, "ex", k) for k in range(1, ex_count)]
-    part = to_owners(partial_scores(sizes, query_sketch, pieces), ex_count, pb_count)
-    gram = make_gram(sizes, pieces)
-    part = part.reshape(pb_count, ex_count, -1)
+    pieces = gather_rows(sketch)
+    *chunks, own = partial_scores(sizes, query_sketch, pieces)
+    part = to_owners(chunks, ex_count)
+    gram, own = make_gram(sizes, pieces, own)
+    part = (part + own).reshape(pb_count, ex_count, -1)
     pb = lax.axis_index("pb")
-    total = lax.dynamic_index_in_dim(part, pb, 0, keepdims=False)
-    for k in range(1, pb_count):
-        theirs = lax.dynamic_index_in_dim(part, pb ^ k, 0, keepdims=False)
-        total += exchange(theirs, "pb", k)
+    theirs = lax.dynamic_index_in_dim(part, 1 - pb, 0, keepdims=False)
+    total = lax.dynamic_index_in_dim(part, pb, 0, keepdims=False) + exchange(theirs, "pb", 1)
     width = query_ids.shape[0] // ex_count
     query_here = lax.dynamic_slice_in_dim(query_ids, lax.axis_index("ex") * width, width, 0)
     self_pair = example_ids == query_here[None, :]

time: 35.5 us -> 28.5 us (0.80)
  starting transfers between devices: 13.5 us -> 10.4 us
  waiting for transfers between devices: 9.81 us -> 6.8 us
  other arithmetic: 1.48 us -> 0.78 us
    ppermute x6 -> x5, starting transfers between devices: 12.8 us -> 4.26 us  [exchange(): lax.ppermute(block, axis, [(i, i ^ step) for i in range(lax.axis_size(axi...]
    ppermute x2 -> x4, starting transfers between devices: 0.75 us -> 6.1 us  [the longest x2 4.05 us: spread(): return lax.ppermute(block, ('ex', 'pb'), pairs)]
    ppermute x6 -> x5, waiting for transfers between devices: 6.94 us -> 3.28 us  [exchange(): lax.ppermute(block, axis, [(i, i ^ step) for i in range(lax.axis_size(axi...]
    concatenate x2 -> x1, other arithmetic: 1.4 us -> 0.7 us  [gather_rows(): jnp.concatenate([own] + [exchange(own, ('feat', 'pb'), s) for s in range(...]
    ppermute x2 -> x4, waiting for transfers between devices: 2.86 us -> 3.52 us  [the longest x2 3.51 us: spread(): return lax.ppermute(block, ('ex', 'pb'), pairs)]
  transfers between devices with their start and end apart: 8 -> 9, of which waited for: 5 -> 5; matrix products, arithmetic and copies ran while one was open for 2% -> 3% of each run, Pallas kernels for 7% -> 8%
where the time goes in v3:
time: 28.5 us; the launch traced here: 28.3 us
  starting transfers between devices  10.4 us (36%)
  Pallas kernels  7.52 us (26%)
  waiting for transfers between devices  6.8 us (24%)
  between operations  1.45 us (5%)
  local copies, waits for them, and re-layouts  1.39 us (5%)
  other arithmetic  0.78 us (3%)
    pallas_call x1, Pallas kernels, make_sketch(): pl.pallas_call(sketch_kernel, out_shape=jax.ShapeDtypeStruct((rank // 2,...  4.77 us
    ppermute x5, starting transfers between devices, exchange(): lax.ppermute(block, axis, [(i, i ^ step) for i in range(lax.axis_size(axi...  4.26 us
    ppermute x2, starting transfers between devices, spread(): return lax.ppermute(block, ('ex', 'pb'), pairs)  4.05 us
    ppermute x2, waiting for transfers between devices, spread(): return lax.ppermute(block, ('ex', 'pb'), pairs)  3.51 us
    ppermute x5, waiting for transfers between devices, exchange(): lax.ppermute(block, axis, [(i, i ^ step) for i in range(lax.axis_size(axi...  3.28 us
    pallas_call x1, Pallas kernels, make_gram(): pl.pallas_call(functools.partial(gram_kernel, sizes, [piece[1:] for piece...  2.38 us
    ppermute x2, starting transfers between devices, to_owners(): arrived.append(lax.ppermute(chunk, ('ex', 'pb'), pairs))  2.05 us
    dynamic_slice x1, local copies, waits for them, and re-layouts, shards(): lax.dynamic_slice_in_dim(query_ids, lax.axis_index('ex') * width, width, 0)  0.76 us
  transfers between devices with their start and end apart: 9, of which 5 were waited for; matrix products, arithmetic and copies ran while one was open for 3% of the time, Pallas kernels for 8%

profile of v3, /device:TPU:0, one launch (start us, length us, event | category | flops | bytes accessed | tf_op | source)
XLA Modules:
  0.0 28.3 jit_solution(5904140600649562982)
XLA Ops:
  0.6 0.0 copy-start
  0.6 0.0 copy-start.1
  1.4 4.8 %sketch.1 = bf16[32,128]{1,0:T(8,128)(2,1)} custom-call(bf16[128,4096]{1,0:T(8,128)(2,1)} %bitcast.19, bf16[128,7168]{1,0:T(8,128)(2,1)} %bitcast.18, bf16[64,4096]{1,0:T(8,128)(2,1)} %bitcast.21, bf16[64,7168]{1,0:T(8,128)(2,1)} %bitcast.20, s32[1,1]{1,0:T(1,128)S(6)} %copy.10.count_ref), custom_call_target="tpu_custom_call" | custom-call | tf_op jit(solution)/shard_map/sketch/pallas_call | solution.py:91
  6.2 0.5 %collective-permute-start = (bf16[1,32,128]{2,1,0:T(8,128)(2,1)}, bf16[1,32,128]{2,1,0:T(8,128)(2,1)S(1)}, u32[]{:S(2)}, u32[]{:S(2)}) collective-permute-start(bf16[1,32,128]{2,1,0:T(8,128)(2,1)} %bitcast.22), channel_id=1, source_target_pairs={{0,1},{1,0},{2,3},{3,2},{4,5},{5,4},{6,7},{7,6},{8,9},{9,8},{10,11... | collective-permute-start | bytes 24584 | tf_op jit(solution)/shard_map/ppermute | solution.py:18
  6.7 2.6 %collective-permute-start.1 = (bf16[1,32,128]{2,1,0:T(8,128)(2,1)}, bf16[1,32,128]{2,1,0:T(8,128)(2,1)S(1)}, u32[]{:S(2)}, u32[]{:S(2)}) collective-permute-start(bf16[1,32,128]{2,1,0:T(8,128)(2,1)} %bitcast.23), channel_id=1, source_target_pairs={{0,2},{1,3},{2,0},{3,1},{4,6},{5,7},{6,4},{7,5},{8,10},{9,11},{10,... | collective-permute-start | bytes 24584 | tf_op jit(solution)/shard_map/ppermute | solution.py:18
  9.2 0.1 collective-permute-start.2
  9.3 0.0 collective-permute-done
  9.3 1.8 %collective-permute-done.1 = bf16[1,32,128]{2,1,0:T(8,128)(2,1)S(1)} collective-permute-done((bf16[1,32,128]{2,1,0:T(8,128)(2,1)}, bf16[1,32,128]{2,1,0:T(8,128)(2,1)S(1)}, u32[]{:S(2)}, u32[]{:S(2)}) %collective-permute-start.1) | collective-permute-done | bytes 8224 | tf_op jit(solution)/shard_map/ppermute | solution.py:18
  11.1 1.4 %collective-permute-done.2 = bf16[1,32,128]{2,1,0:T(8,128)(2,1)S(1)} collective-permute-done((bf16[1,32,128]{2,1,0:T(8,128)(2,1)}, bf16[1,32,128]{2,1,0:T(8,128)(2,1)S(1)}, u32[]{:S(2)}, u32[]{:S(2)}) %collective-permute-start.2) | collective-permute-done | bytes 8224 | tf_op jit(solution)/shard_map/ppermute | solution.py:18
  12.5 0.7 %pad_maximum_fusion.refs_0_ = bf16[4,32,128]{2,1,0:T(8,128)(2,1)S(1)} fusion(bf16[1,32,128]{2,1,0:T(8,128)(2,1)S(1)} %collective-permute-done.2, bf16[1,32,128]{2,1,0:T(8,128)(2,1)S(1)} %collective-permute-done.1, bf16[1,32,128]{2,1,0:T(8,128)(2,1)S(1)} %collective-permute-done, bf16[1,32,128]{2,1,0:T(8,128)(2,1)} %bitcast.25), kind=kLoop, calls=%fused_computation | loop fusion | flops 49152 | bytes 65536 | tf_op jit(solution)/shard_map/concatenate | solution.py:124
  13.2 1.6 %collective-permute-start.3 = (bf16[4,32,128]{2,1,0:T(8,128)(2,1)S(1)}, bf16[4,32,128]{2,1,0:T(8,128)(2,1)S(1)}, u32[]{:S(2)}, u32[]{:S(2)}) collective-permute-start(bf16[4,32,128]{2,1,0:T(8,128)(2,1)S(1)} %pad_maximum_fusion.refs_0_), channel_id=1, source_target_pairs={{0,4},{1,9},{4,0},{5,13},{8,12},{9,1},{12,8},{13,5},{2,6},{3,11},{... | collective-permute-start | bytes 98312 | tf_op jit(solution)/shard_map/ppermute | solution.py:117
  14.8 2.5 %collective-permute-start.5 = (bf16[4,32,128]{2,1,0:T(8,128)(2,1)S(1)}, bf16[4,32,128]{2,1,0:T(8,128)(2,1)S(1)}, u32[]{:S(2)}, u32[]{:S(2)}) collective-permute-start(bf16[4,32,128]{2,1,0:T(8,128)(2,1)S(1)} %pad_maximum_fusion.refs_0_), channel_id=1, source_target_pairs={{0,12},{1,13},{4,8},{5,9},{8,4},{9,5},{12,0},{13,1},{2,14},{3,15},... | collective-permute-start | bytes 98312 | tf_op jit(solution)/shard_map/ppermute | solution.py:117
  17.3 0.2 collective-permute-done.3.refs_1_
  17.5 0.0 collective-permute-start.4
  17.5 3.3 %collective-permute-done.5.refs_3_ = bf16[4,32,128]{2,1,0:T(8,128)(2,1)S(1)} collective-permute-done((bf16[4,32,128]{2,1,0:T(8,128)(2,1)S(1)}, bf16[4,32,128]{2,1,0:T(8,128)(2,1)S(1)}, u32[]{:S(2)}, u32[]{:S(2)}) %collective-permute-start.5) | collective-permute-done | bytes 32800 | tf_op jit(solution)/shard_map/ppermute | solution.py:117
  20.8 0.0 collective-permute-done.4.refs_2_
  20.8 0.0 copy-done
  20.8 0.4 %scores.1 = (f32[8,256]{1,0:T(8,128)S(1)}, f32[8,256]{1,0:T(8,128)S(1)}, f32[8,256]{1,0:T(8,128)S(1)}) custom-call(bf16[512,1024]{1,0:T(8,128)(2,1)S(1)} %copy-done, bf16[4,32,128]{2,1,0:T(8,128)(2,1)S(1)} %pad_maximum_fusion.refs_0_, bf16[4,32,128]{2,1,0:T(8,128)(2,1)S(1)} %collective-permute-done.3.refs_1_, ...), custom_call_target="tpu_custom_call" | custom-call | tf_op jit(solution)/shard_map/scores/pallas_call | solution.py:187
  21.2 0.0 collective-permute-start.6
  21.2 2.0 %collective-permute-start.7 = (f32[8,256]{1,0:T(8,128)S(1)}, f32[8,256]{1,0:T(8,128)S(1)}, u32[]{:S(2)}, u32[]{:S(2)}) collective-permute-start(f32[8,256]{1,0:T(8,128)S(1)} %get-tuple-element.10), channel_id=1, source_target_pairs={{0,4},{1,12},{4,0},{5,8},{9,13},{8,5},{13,9},{12,1},{2,6},{3,14},{... | collective-permute-start | bytes 24584 | tf_op jit(solution)/shard_map/ppermute | solution.py:273
  23.2 2.4 %gram.1 = (f32[1024,1024]{1,0:T(8,128)}, f32[8,256]{1,0:T(8,128)S(1)}) custom-call(f32[8,256]{1,0:T(8,128)S(1)} %get-tuple-element.7.kept_ref, bf16[4,32,128]{2,1,0:T(8,128)(2,1)S(1)} %pad_maximum_fusion.refs_0_, bf16[4,32,128]{2,1,0:T(8,128)(2,1)S(1)} %collective-permute-done.3.refs_1_, bf16[4,32,128]{2,1,0:T(8,128)(2,1)S(1)} %collective-permute-done.4.refs_2_, ...), custom_call_target="tpu_custom_call" | custom-call | flops 536870912 | bytes 4194304 | tf_op jit(solution)/shard_map/gram/pallas_call | solution.py:239
  25.6 0.0 collective-permute-done.6
  25.6 0.0 collective-permute-done.7
  25.7 1.1 %collective-permute-start.8 = (f32[4,256]{1,0:T(4,128)S(1)}, f32[4,256]{1,0:T(4,128)S(1)}, u32[]{:S(2)}, u32[]{:S(2)}) collective-permute-start(f32[4,256]{1,0:T(4,128)S(1)} %dynamic-slice_bitcast_fusion), channel_id=1, source_target_pairs={{0,1},{1,0},{2,3},{3,2},{4,5},{5,4},{6,7},{7,6},{8,9},{9,8},{10,11... | collective-permute-start | bytes 12296 | tf_op jit(solution)/shard_map/ppermute | solution.py:18
  26.8 0.8 %dynamic_slice.10 = s32[256]{0:T(256)S(1)} dynamic-slice(s32[1024]{0:T(1024)} %param.15, s32[]{:T(128)S(6)} %select_n.14), dynamic_slice_sizes={256} | dynamic-slice | bytes 2052 | tf_op jit(solution)/shard_map/dynamic_slice | solution.py:294
  27.6 0.1 collective-permute-done.8
  27.6 0.0 copy-done.1
  27.6 0.1 fusion.1
  27.7 0.6 %broadcast_in_dim.13 = f32[256,4,1]{0,2,1:T(1,128)} reshape(f32[256,4]{0,1:T(4,128)S(1)} %fusion.1) | data formatting | bytes 8192 | tf_op jit(solution)/shard_map/broadcast_in_dim | solution.py:297
  (3 shorter events, 0.0 us)
Async XLA Ops:
  0.6 20.2 %copy-start = (bf16[512,1024]{1,0:T(8,128)(2,1)S(1)}, bf16[512,1024]{1,0:T(8,128)(2,1)}, u32[]{:S(2)}) copy-start(bf16[512,1024]{1,0:T(8,128)(2,1)} %query_ref.1) | copy-start | bytes 3145732
  0.6 27.0 %copy-start.1 = (s32[4,1]{0,1:T(1,128)S(1)}, s32[4,1]{0,1:T(1,128)}, u32[]{:S(2)}) copy-start(s32[4,1]{0,1:T(1,128)} %param.13) | copy-start | bytes 52
  6.2 3.2 %collective-permute-start = (bf16[1,32,128]{2,1,0:T(8,128)(2,1)}, bf16[1,32,128]{2,1,0:T(8,128)(2,1)S(1)}, u32[]{:S(2)}, u32[]{:S(2)}) collective-permute-start(bf16[1,32,128]{2,1,0:T(8,128)(2,1)} %bitcast.22), channel_id=1, source_target_pairs={{0,1},{1,0},{2,3},{3,2},{4,5},{5,4},{6,7},{7,6},{8,9},{9,8},{10,11... | collective-permute-start | bytes 24584 | tf_op jit(solution)/shard_map/ppermute | solution.py:18
  6.7 4.4 %collective-permute-start.1 = (bf16[1,32,128]{2,1,0:T(8,128)(2,1)}, bf16[1,32,128]{2,1,0:T(8,128)(2,1)S(1)}, u32[]{:S(2)}, u32[]{:S(2)}) collective-permute-start(bf16[1,32,128]{2,1,0:T(8,128)(2,1)} %bitcast.23), channel_id=1, source_target_pairs={{0,2},{1,3},{2,0},{3,1},{4,6},{5,7},{6,4},{7,5},{8,10},{9,11},{10,... | collective-permute-start | bytes 24584 | tf_op jit(solution)/shard_map/ppermute | solution.py:18
  9.2 3.3 %collective-permute-start.2 = (bf16[1,32,128]{2,1,0:T(8,128)(2,1)}, bf16[1,32,128]{2,1,0:T(8,128)(2,1)S(1)}, u32[]{:S(2)}, u32[]{:S(2)}) collective-permute-start(bf16[1,32,128]{2,1,0:T(8,128)(2,1)} %bitcast.24), channel_id=1, source_target_pairs={{0,3},{1,2},{2,1},{3,0},{4,7},{5,6},{6,5},{7,4},{8,11},{9,10},{10,... | collective-permute-start | bytes 24584 | tf_op jit(solution)/shard_map/ppermute | solution.py:18
  13.2 4.3 %collective-permute-start.3 = (bf16[4,32,128]{2,1,0:T(8,128)(2,1)S(1)}, bf16[4,32,128]{2,1,0:T(8,128)(2,1)S(1)}, u32[]{:S(2)}, u32[]{:S(2)}) collective-permute-start(bf16[4,32,128]{2,1,0:T(8,128)(2,1)S(1)} %pad_maximum_fusion.refs_0_), channel_id=1, source_target_pairs={{0,4},{1,9},{4,0},{5,13},{8,12},{9,1},{12,8},{13,5},{2,6},{3,11},{... | collective-permute-start | bytes 98312 | tf_op jit(solution)/shard_map/ppermute | solution.py:117
  14.8 6.0 %collective-permute-start.5 = (bf16[4,32,128]{2,1,0:T(8,128)(2,1)S(1)}, bf16[4,32,128]{2,1,0:T(8,128)(2,1)S(1)}, u32[]{:S(2)}, u32[]{:S(2)}) collective-permute-start(bf16[4,32,128]{2,1,0:T(8,128)(2,1)S(1)} %pad_maximum_fusion.refs_0_), channel_id=1, source_target_pairs={{0,12},{1,13},{4,8},{5,9},{8,4},{9,5},{12,0},{13,1},{2,14},{3,15},... | collective-permute-start | bytes 98312 | tf_op jit(solution)/shard_map/ppermute | solution.py:117
  17.5 3.3 %collective-permute-start.4 = (bf16[4,32,128]{2,1,0:T(8,128)(2,1)S(1)}, bf16[4,32,128]{2,1,0:T(8,128)(2,1)S(1)}, u32[]{:S(2)}, u32[]{:S(2)}) collective-permute-start(bf16[4,32,128]{2,1,0:T(8,128)(2,1)S(1)} %collective-permute-done.3.refs_1_), channel_id=1, source_target_pairs={{0,1},{1,0},{2,3},{3,2},{4,5},{5,4},{6,7},{7,6},{8,9},{9,8},{10,11... | collective-permute-start | bytes 98312 | tf_op jit(solution)/shard_map/ppermute | solution.py:18
  21.2 4.5 %collective-permute-start.6 = (f32[8,256]{1,0:T(8,128)S(1)}, f32[8,256]{1,0:T(8,128)S(1)}, u32[]{:S(2)}, u32[]{:S(2)}) collective-permute-start(f32[8,256]{1,0:T(8,128)S(1)} %get-tuple-element.9), channel_id=1, source_target_pairs={{0,4},{1,8},{4,0},{5,12},{9,13},{8,1},{13,9},{12,5},{2,6},{3,10},{... | collective-permute-start | bytes 24584 | tf_op jit(solution)/shard_map/ppermute | solution.py:273
  21.2 4.4 %collective-permute-start.7 = (f32[8,256]{1,0:T(8,128)S(1)}, f32[8,256]{1,0:T(8,128)S(1)}, u32[]{:S(2)}, u32[]{:S(2)}) collective-permute-start(f32[8,256]{1,0:T(8,128)S(1)} %get-tuple-element.10), channel_id=1, source_target_pairs={{0,4},{1,12},{4,0},{5,8},{9,13},{8,5},{13,9},{12,1},{2,6},{3,14},{... | collective-permute-start | bytes 24584 | tf_op jit(solution)/shard_map/ppermute | solution.py:273
  25.7 1.9 %collective-permute-start.8 = (f32[4,256]{1,0:T(4,128)S(1)}, f32[4,256]{1,0:T(4,128)S(1)}, u32[]{:S(2)}, u32[]{:S(2)}) collective-permute-start(f32[4,256]{1,0:T(4,128)S(1)} %dynamic-slice_bitcast_fusion), channel_id=1, source_target_pairs={{0,1},{1,0},{2,3},{3,2},{4,5},{5,4},{6,7},{7,6},{8,9},{9,8},{10,11... | collective-permute-start | bytes 12296 | tf_op jit(solution)/shard_map/ppermute | solution.py:18

commit v4 on v3

--- a/solution.py
+++ b/solution.py
@@ -9,8 +9,6 @@
 from jax.sharding import PartitionSpec as P
 
 DAMPING = 0.1
-ACT_CUTS = 2
-GRAD_CUTS = 4
 NT = (((1,), (1,)), ((), ()))
 
 
@@ -18,94 +16,16 @@
     return lax.ppermute(block, axis, [(i, i ^ step) for i in range(lax.axis_size(axis))])
 
 
-def sketch_kernel(
-    acts_hbm, grads_hbm, act_proj_hbm, grad_proj_hbm, count_ref, out_ref,
-    acts, grads, act_proj, grad_proj, turned, act_sems, grad_sems,
-):
-    seq_len = acts.shape[0]
-    rank = act_proj.shape[0]
-
-    def copies(source_hbm, target, sems, slot, cuts):
-        width = target.shape[1] // cuts
-        return [
-            pltpu.make_async_copy(
-                source_hbm.at[:, pl.ds(c * width, width)],
-                target.at[:, pl.ds(c * width, width)],
-                sems.at[slot, c],
-            )
-            for c in range(cuts)
-        ]
-
-    act_copies = list(
-        zip(
-            copies(act_proj_hbm, act_proj, act_sems, 0, ACT_CUTS),
-            copies(acts_hbm, acts, act_sems, 1, ACT_CUTS),
-        )
-    )
-    grad_copies = list(
-        zip(
-            copies(grad_proj_hbm, grad_proj, grad_sems, 0, GRAD_CUTS),
-            copies(grads_hbm, grads, grad_sems, 1, GRAD_CUTS),
-        )
-    )
-    for pair in act_copies + grad_copies:
-        for copy in pair:
-            copy.start()
-    act_width = acts.shape[1] // ACT_CUTS
-    act_sum = jnp.zeros((seq_len, rank), jnp.float32)
-    for c, pair in enumerate(act_copies):
-        for copy in pair:
-            copy.wait()
-        cols = pl.ds(c * act_width, act_width)
-        act_sum += lax.dot_general(
-            acts[:, cols], act_proj[:, cols], NT, preferred_element_type=jnp.float32
-        )
-    grad_width = grads.shape[1] // GRAD_CUTS
-    grad_sum = jnp.zeros((rank, seq_len), jnp.float32)
-    for c, pair in enumerate(grad_copies):
-        for copy in pair:
-            copy.wait()
-        cols = pl.ds(c * grad_width, grad_width)
-        grad_sum += lax.dot_general(
-            grad_proj[:, cols], grads[:, cols], NT, preferred_element_type=jnp.float32
-        )
-    live = lax.broadcasted_iota(jnp.int32, (rank, seq_len), 1) < count_ref[...]
-    turned[...] = jnp.where(live, grad_sum, 0.0)
-    act_low = act_sum.astype(jnp.bfloat16)
-    halves = [
-        jnp.dot(
-            turned[pl.ds(side, rank // 2, stride=2), :].astype(jnp.bfloat16),
-            act_low,
-            preferred_element_type=jnp.float32,
-        )
-        for side in range(2)
-    ]
-    outer = jnp.concatenate(halves, axis=1) * (1.0 / math.sqrt(seq_len))
-    out_ref[...] = outer.astype(jnp.bfloat16)
-
-
 def make_sketch(acts, grads, act_proj, grad_proj, tok_count):
-    seq_len, width = acts.shape
-    hidden = grads.shape[1]
-    rank = act_proj.shape[0]
-    return pl.pallas_call(
-        sketch_kernel,
-        out_shape=jax.ShapeDtypeStruct((rank // 2, 2 * rank), jnp.bfloat16),
-        in_specs=[pl.BlockSpec(memory_space=pl.ANY)] * 4
-        + [pl.BlockSpec(memory_space=pltpu.VMEM)],
-        out_specs=pl.BlockSpec(memory_space=pltpu.VMEM),
-        scratch_shapes=[
-            pltpu.VMEM((seq_len, width), jnp.bfloat16),
-            pltpu.VMEM((seq_len, hidden), jnp.bfloat16),
-            pltpu.VMEM((rank, width), jnp.bfloat16),
-            pltpu.VMEM((rank, hidden), jnp.bfloat16),
-            pltpu.VMEM((rank, seq_len), jnp.float32),
-            pltpu.SemaphoreType.DMA((2, ACT_CUTS)),
-            pltpu.SemaphoreType.DMA((2, GRAD_CUTS)),
-        ],
-        compiler_params=pltpu.CompilerParams(vmem_limit_bytes=60 * 2**20),
-        name="sketch",
-    )(acts, grads, act_proj, grad_proj, tok_count)
+    seq_len, rank = acts.shape[0], act_proj.shape[1]
+    act_low = jnp.dot(acts, act_proj, preferred_element_type=jnp.float32).astype(jnp.bfloat16)
+    grad_low = jnp.dot(grads, grad_proj, preferred_element_type=jnp.float32).astype(jnp.bfloat16)
+    keep_mask = (jnp.arange(seq_len, dtype=jnp.int32) < tok_count).astype(jnp.bfloat16)
+    kept = grad_low * keep_mask[:, None]
+    outer_sum = jnp.dot(kept.T, act_low, preferred_element_type=jnp.float32) * (
+        1.0 / math.sqrt(seq_len)
+    )
+    return outer_sum.astype(jnp.bfloat16).reshape(rank // 2, 2 * rank)
 
 
 def spread(block, distances):
@@ -143,11 +63,11 @@
             rows[(fp ^ core ^ s) * ex_count + where] = piece[s].astype(jnp.float32)
 
 
-def score_kernel(sizes, sources, query_ref, *refs):
+def score_kernel(sizes, sources, query_ref, query_ids_ref, example_ids_ref, *refs):
     ex_count, feat_count, pb_count = sizes
     half = ex_count // pb_count
     pieces, outs = refs[: len(sources)], refs[len(sources) : len(sources) + half]
-    own_ref, rows, scaled, chunks = refs[-4:]
+    own_ref, open_ref, rows, scaled, chunks = refs[-5:]
     ex, feat = lax.axis_index("ex"), lax.axis_index("feat")
     near = lax.div(ex, half) == lax.axis_index("pb")
     here = lax.rem(ex, half)
@@ -175,9 +95,10 @@
         outs[i][...] = chunks[here ^ (i + shift)]
     outs[half - 1][...] = jnp.where(near, 0.0, chunks[here ^ (half - 1)])
     own_ref[...] = jnp.where(near, chunks[here], 0.0)
-
-
-def partial_scores(sizes, queries, pieces):
+    open_ref[...] = jnp.where(example_ids_ref[...] == query_ids_ref[...], 0.0, 1.0)
+
+
+def partial_scores(sizes, queries, query_ids, example_ids, pieces):
     ex_count, feat_count, pb_count = sizes
     examples = ex_count * feat_count * pb_count
     lines, lanes = pieces[0][0].shape[1:]
@@ -186,9 +107,10 @@
     vmem = pl.BlockSpec(memory_space=pltpu.VMEM)
     return pl.pallas_call(
         functools.partial(score_kernel, sizes, [piece[1:] for piece in pieces]),
-        out_shape=[jax.ShapeDtypeStruct(chunk, jnp.float32)] * (half + 1),
-        in_specs=[vmem] * (1 + len(pieces)),
-        out_specs=[vmem] * (half + 1),
+        out_shape=[jax.ShapeDtypeStruct(chunk, jnp.float32)] * (half + 1)
+        + [jax.ShapeDtypeStruct((ex_count, chunk[1]), jnp.float32)],
+        in_specs=[vmem] * (3 + len(pieces)),
+        out_specs=[vmem] * (half + 2),
         scratch_shapes=[
             pltpu.VMEM((examples, lines, lanes), jnp.float32),
             pltpu.VMEM((pb_count * lines, lanes), jnp.float32),
@@ -196,7 +118,7 @@
         ],
         compiler_params=pltpu.CompilerParams(vmem_limit_bytes=24 * 2**20),
         name="scores",
-    )(queries, *[piece[0] for piece in pieces])
+    )(queries, query_ids, example_ids, *[piece[0] for piece in pieces])
 
 
 def gram_kernel(sizes, sources, kept_ref, *refs):
@@ -280,20 +202,21 @@
     ex_count, feat_count, pb_count = (lax.axis_size(axis) for axis in ("ex", "feat", "pb"))
     sizes = (ex_count, feat_count, pb_count)
     sketch = make_sketch(
-        activations[0, 0], out_grads[0, 0], act_proj.T, grad_proj.T, tok_counts
+        activations[0, 0], out_grads[0, 0], act_proj, grad_proj, tok_counts[0, 0]
     )
     pieces = gather_rows(sketch)
-    *chunks, own = partial_scores(sizes, query_sketch, pieces)
+    width = query_ids.shape[0] // ex_count
+    query_here = lax.dynamic_slice_in_dim(query_ids, lax.axis_index("ex") * width, width, 0)
+    *chunks, own, is_open = partial_scores(
+        sizes, query_sketch, query_here[None], example_ids, pieces
+    )
     part = to_owners(chunks, ex_count)
     gram, own = make_gram(sizes, pieces, own)
     part = (part + own).reshape(pb_count, ex_count, -1)
     pb = lax.axis_index("pb")
     theirs = lax.dynamic_index_in_dim(part, 1 - pb, 0, keepdims=False)
     total = lax.dynamic_index_in_dim(part, pb, 0, keepdims=False) + exchange(theirs, "pb", 1)
-    width = query_ids.shape[0] // ex_count
-    query_here = lax.dynamic_slice_in_dim(query_ids, lax.axis_index("ex") * width, width, 0)
-    self_pair = example_ids == query_here[None, :]
-    scores = jnp.where(self_pair, jnp.float32(0.0), total)
+    scores = jnp.where(is_open == 0.0, jnp.float32(0.0), total)
     return gram, scores.T[:, :, None]
 
 

time: 28.5 us -> 26.7 us (0.937)
  Pallas kernels: 7.52 us -> 2.76 us
  matrix products: 0 us -> 3.84 us
  other arithmetic: 0.78 us -> 0.01 us
  waiting for transfers between devices: 6.8 us -> 6.48 us
    pallas_call x1 -> x0, Pallas kernels: 4.77 us -> none  [make_sketch(): pl.pallas_call(sketch_kernel, out_shape=jax.ShapeDtypeStruct((rank // 2,...]
    dot_general x0 -> x2, matrix products: none -> 3.84 us  [the longest x1 2.06 us: make_sketch(): jnp.dot(kept.T, act_low, preferred_element_type=jnp.float32)]
    ppermute x2, waiting for transfers between devices: 3.51 us -> 2.66 us  [spread(): return lax.ppermute(block, ('ex', 'pb'), pairs)]
    unnamed x4 -> x11, local copies, waits for them, and re-layouts: 0.01 us -> 0.73 us
    concatenate x1 -> x0, other arithmetic: 0.7 us -> none  [gather_rows(): jnp.concatenate([own] + [exchange(own, ('feat', 'pb'), s) for s in range(...]
    broadcast_in_dim x1 -> x0, local copies, waits for them, and re-layouts: 0.6 us -> none  [shards(): return (gram, scores.T[:, :, None])]
    ppermute x5, waiting for transfers between devices: 3.28 us -> 3.81 us  [exchange(): lax.ppermute(block, axis, [(i, i ^ step) for i in range(lax.axis_size(axi...]
  transfers between devices with their start and end apart: 9 -> 9, of which waited for: 5 -> 5; matrix products, arithmetic and copies ran while one was open for 3% -> 3% of each run, Pallas kernels for 8% -> 9%
where the time goes in v4:
time: 26.7 us; the launch traced here: 26.5 us
  starting transfers between devices  10.3 us (39%)
  waiting for transfers between devices  6.48 us (24%)
  matrix products  3.84 us (14%)
  Pallas kernels  2.76 us (10%)
  local copies, waits for them, and re-layouts  1.61 us (6%)
  between operations  1.53 us (6%)
    ppermute x5, starting transfers between devices, exchange(): lax.ppermute(block, axis, [(i, i ^ step) for i in range(lax.axis_size(axi...  4.21 us
    ppermute x2, starting transfers between devices, spread(): return lax.ppermute(block, ('ex', 'pb'), pairs)  4.05 us
    ppermute x5, waiting for transfers between devices, exchange(): lax.ppermute(block, axis, [(i, i ^ step) for i in range(lax.axis_size(axi...  3.81 us
    ppermute x2, waiting for transfers between devices, spread(): return lax.ppermute(block, ('ex', 'pb'), pairs)  2.66 us
    pallas_call x1, Pallas kernels, make_gram(): pl.pallas_call(functools.partial(gram_kernel, sizes, [piece[1:] for piece...  2.38 us
    dot_general x1, matrix products, make_sketch(): jnp.dot(kept.T, act_low, preferred_element_type=jnp.float32)  2.06 us
    ppermute x2, starting transfers between devices, to_owners(): arrived.append(lax.ppermute(chunk, ('ex', 'pb'), pairs))  2.04 us
    dot_general x1, matrix products, make_sketch(): jnp.dot(acts, act_proj, preferred_element_type=jnp.float32)  1.78 us
  transfers between devices with their start and end apart: 9, of which 5 were waited for; matrix products, arithmetic and copies ran while one was open for 3% of the time, Pallas kernels for 9%

profile of v4, /device:TPU:0, one launch (start us, length us, event | category | flops | bytes accessed | tf_op | source)
XLA Modules:
  0.0 26.5 jit_solution(3317409182974170348)
XLA Ops:
  0.6 0.0 copy-start
  1.4 1.8 %convolution_convert_fusion = bf16[128,64]{1,0:T(8,128)(2,1)S(1)} fusion(bf16[4096,64]{0,1:T(8,128)(2,1)} %param.10, bf16[1,1,128,4096]{3,2,1,0:T(8,128)(2,1)} %param.8), kind=kOutput, calls=%fused_computation.2 | convolution fusion | flops 67117056 | bytes 1589248 | tf_op jit(solution)/shard_map/dot_general | solution.py:21
  3.2 0.0 copy-done
  3.2 0.0 copy-start.2
  3.2 0.0 copy-start.1
  3.3 2.1 %fusion.14 = bf16[64,64]{1,0:T(8,128)(2,1)S(1)} fusion(bf16[128,64]{1,0:T(8,128)(2,1)S(1)} %convolution_convert_fusion, bf16[7168,64]{0,1:T(8,128)(2,1)} %param.11, bf16[1,1,128,7168]{3,2,1,0:T(8,128)(2,1)S(1)} %copy-done, bf16[128]{0:T(256)(128)(2,1)S(1)} %compare_convert_fusion), kind=kOutput, calls=%fused_computation.7 | convolution fusion | flops 118513664 | bytes 2777344 | tf_op jit(solution)/shard_map/dot_general | solution.py:25
  5.3 0.1 broadcast_in_dim_reshape.3
  5.4 0.5 %collective-permute-start = (bf16[1,32,128]{2,1,0:T(8,128)(2,1)S(1)}, bf16[1,32,128]{2,1,0:T(8,128)(2,1)S(1)}, u32[]{:S(2)}, u32[]{:S(2)}) collective-permute-start(bf16[1,32,128]{2,1,0:T(8,128)(2,1)S(1)} %broadcast_in_dim_reshape.3), channel_id=1, source_target_pairs={{0,1},{1,0},{2,3},{3,2},{4,5},{5,4},{6,7},{7,6},{8,9},{9,8},{10,11... | collective-permute-start | bytes 24584 | tf_op jit(solution)/shard_map/ppermute | solution.py:16
  5.9 2.6 %collective-permute-start.1 = (bf16[1,32,128]{2,1,0:T(8,128)(2,1)S(1)}, bf16[1,32,128]{2,1,0:T(8,128)(2,1)S(1)}, u32[]{:S(2)}, u32[]{:S(2)}) collective-permute-start(bf16[1,32,128]{2,1,0:T(8,128)(2,1)S(1)} %broadcast_in_dim_reshape.3), channel_id=1, source_target_pairs={{0,2},{1,3},{2,0},{3,1},{4,6},{5,7},{6,4},{7,5},{8,10},{9,11},{10,... | collective-permute-start | bytes 24584 | tf_op jit(solution)/shard_map/ppermute | solution.py:16
  8.4 0.1 collective-permute-start.2
  8.5 0.0 collective-permute-done
  8.5 1.5 %collective-permute-done.1 = bf16[1,32,128]{2,1,0:T(8,128)(2,1)S(1)} collective-permute-done((bf16[1,32,128]{2,1,0:T(8,128)(2,1)S(1)}, bf16[1,32,128]{2,1,0:T(8,128)(2,1)S(1)}, u32[]{:S(2)}, u32[]{:S(2)}) %collective-permute-start.1) | collective-permute-done | bytes 8224 | tf_op jit(solution)/shard_map/ppermute | solution.py:16
  10.1 1.4 %collective-permute-done.2 = bf16[1,32,128]{2,1,0:T(8,128)(2,1)S(1)} collective-permute-done((bf16[1,32,128]{2,1,0:T(8,128)(2,1)S(1)}, bf16[1,32,128]{2,1,0:T(8,128)(2,1)S(1)}, u32[]{:S(2)}, u32[]{:S(2)}) %collective-permute-start.2) | collective-permute-done | bytes 8224 | tf_op jit(solution)/shard_map/ppermute | solution.py:16
  11.5 1.6 %collective-permute-start.3 = (bf16[4,32,128]{2,1,0:T(8,128)(2,1)S(1)}, bf16[4,32,128]{2,1,0:T(8,128)(2,1)S(1)}, u32[]{:S(2)}, u32[]{:S(2)}) collective-permute-start(bf16[4,32,128]{2,1,0:T(8,128)(2,1)S(1)} %constant_dynamic-update-slice_fusion.refs_0_), channel_id=1, source_target_pairs={{0,4},{1,9},{4,0},{5,13},{8,12},{9,1},{12,8},{13,5},{2,6},{3,11},{... | collective-permute-start | bytes 98312 | tf_op jit(solution)/shard_map/ppermute | solution.py:37
  13.1 2.5 %collective-permute-start.5 = (bf16[4,32,128]{2,1,0:T(8,128)(2,1)S(1)}, bf16[4,32,128]{2,1,0:T(8,128)(2,1)S(1)}, u32[]{:S(2)}, u32[]{:S(2)}) collective-permute-start(bf16[4,32,128]{2,1,0:T(8,128)(2,1)S(1)} %constant_dynamic-update-slice_fusion.refs_0_), channel_id=1, source_target_pairs={{0,12},{1,13},{4,8},{5,9},{8,4},{9,5},{12,0},{13,1},{2,14},{3,15},... | collective-permute-start | bytes 98312 | tf_op jit(solution)/shard_map/ppermute | solution.py:37
  15.6 0.2 collective-permute-done.3.refs_1_
  15.8 0.0 collective-permute-start.4
  15.8 0.0 copy-done.2
  15.8 0.1 copy.10.example_ids_ref
  15.9 0.8 %dynamic_slice.10 = s32[256]{0:T(256)S(1)} dynamic-slice(s32[1024]{0:T(1024)} %param.15, s32[]{:T(128)S(6)} %select_n.14), dynamic_slice_sizes={256} | dynamic-slice | bytes 2052 | tf_op jit(solution)/shard_map/dynamic_slice | solution.py:209
  16.6 2.4 %collective-permute-done.5.refs_3_ = bf16[4,32,128]{2,1,0:T(8,128)(2,1)S(1)} collective-permute-done((bf16[4,32,128]{2,1,0:T(8,128)(2,1)S(1)}, bf16[4,32,128]{2,1,0:T(8,128)(2,1)S(1)}, u32[]{:S(2)}, u32[]{:S(2)}) %collective-permute-start.5) | collective-permute-done | bytes 32800 | tf_op jit(solution)/shard_map/ppermute | solution.py:37
  19.1 0.0 collective-permute-done.4.refs_2_
  19.1 0.0 copy-done.1
  19.1 0.4 %scores.1 = (f32[8,256]{1,0:T(8,128)S(1)}, f32[8,256]{1,0:T(8,128)S(1)}, f32[8,256]{1,0:T(8,128)S(1)}, f32[4,256]{1,0:T(4,128)S(1)}) custom-call(bf16[512,1024]{1,0:T(8,128)(2,1)S(1)} %copy-done.1, s32[1,256]{1,0:T(1,128)S(1)} %bitcast.34, s32[4,1]{1,0:T(4,128)S(1)} %copy.10.example_ids_ref, ...), custom_call_target="tpu_custom_call" | custom-call | tf_op jit(solution)/shard_map/scores/pallas_call | solution.py:108
  19.5 0.0 collective-permute-start.6
  19.5 2.0 %collective-permute-start.7 = (f32[8,256]{1,0:T(8,128)S(1)}, f32[8,256]{1,0:T(8,128)S(1)}, u32[]{:S(2)}, u32[]{:S(2)}) collective-permute-start(f32[8,256]{1,0:T(8,128)S(1)} %get-tuple-element.12), channel_id=1, source_target_pairs={{0,4},{1,12},{4,0},{5,8},{9,13},{8,5},{13,9},{12,1},{2,6},{3,14},{... | collective-permute-start | bytes 24584 | tf_op jit(solution)/shard_map/ppermute | solution.py:195
  21.5 2.4 %gram.1 = (f32[1024,1024]{1,0:T(8,128)}, f32[8,256]{1,0:T(8,128)S(1)}) custom-call(f32[8,256]{1,0:T(8,128)S(1)} %get-tuple-element.8.kept_ref, bf16[4,32,128]{2,1,0:T(8,128)(2,1)S(1)} %constant_dynamic-update-slice_fusion.refs_0_, bf16[4,32,128]{2,1,0:T(8,128)(2,1)S(1)} %collective-permute-done.3.refs_1_, ...), custom_call_target="tpu_custom_call" | custom-call | flops 536870912 | bytes 4194304 | tf_op jit(solution)/shard_map/gram/pallas_call | solution.py:161
  23.9 0.0 collective-permute-done.6
  23.9 0.0 collective-permute-done.7
  24.0 1.1 %collective-permute-start.8 = (f32[4,256]{1,0:T(4,128)S(1)}, f32[4,256]{1,0:T(4,128)S(1)}, u32[]{:S(2)}, u32[]{:S(2)}) collective-permute-start(f32[4,256]{1,0:T(4,128)S(1)} %dynamic-slice_bitcast_fusion), channel_id=1, source_target_pairs={{0,1},{1,0},{2,3},{3,2},{4,5},{5,4},{6,7},{7,6},{8,9},{9,8},{10,11... | collective-permute-start | bytes 12296 | tf_op jit(solution)/shard_map/ppermute | solution.py:16
  25.1 0.8 %collective-permute-done.8 = f32[4,256]{1,0:T(4,128)S(1)} collective-permute-done((f32[4,256]{1,0:T(4,128)S(1)}, f32[4,256]{1,0:T(4,128)S(1)}, u32[]{:S(2)}, u32[]{:S(2)}) %collective-permute-start.8) | collective-permute-done | bytes 4128 | tf_op jit(solution)/shard_map/ppermute | solution.py:16
  25.9 0.6 %copy.11 = f32[256,4,1]{0,2,1:T(1,128)} copy(f32[256,4,1]{0,1,2:T(4,128)S(1)} %fusion.20) | data formatting | bytes 8192
  (9 shorter events, 0.1 us)
Async XLA Ops:
  0.6 2.6 %copy-start = (bf16[1,1,128,7168]{3,2,1,0:T(8,128)(2,1)S(1)}, bf16[1,1,128,7168]{3,2,1,0:T(8,128)(2,1)}, u32[]{:S(2)}) copy-start(bf16[1,1,128,7168]{3,2,1,0:T(8,128)(2,1)} %param.9) | copy-start | bytes 5505028
  3.2 12.6 %copy-start.2 = (s32[4,1]{0,1:T(1,128)S(1)}, s32[4,1]{0,1:T(1,128)}, u32[]{:S(2)}) copy-start(s32[4,1]{0,1:T(1,128)} %param.13) | copy-start | bytes 52
  3.2 15.9 %copy-start.1 = (bf16[512,1024]{1,0:T(8,128)(2,1)S(1)}, bf16[512,1024]{1,0:T(8,128)(2,1)}, u32[]{:S(2)}) copy-start(bf16[512,1024]{1,0:T(8,128)(2,1)} %query_ref.1) | copy-start | bytes 3145732
  5.4 3.1 %collective-permute-start = (bf16[1,32,128]{2,1,0:T(8,128)(2,1)S(1)}, bf16[1,32,128]{2,1,0:T(8,128)(2,1)S(1)}, u32[]{:S(2)}, u32[]{:S(2)}) collective-permute-start(bf16[1,32,128]{2,1,0:T(8,128)(2,1)S(1)} %broadcast_in_dim_reshape.3), channel_id=1, source_target_pairs={{0,1},{1,0},{2,3},{3,2},{4,5},{5,4},{6,7},{7,6},{8,9},{9,8},{10,11... | collective-permute-start | bytes 24584 | tf_op jit(solution)/shard_map/ppermute | solution.py:16
  5.9 4.2 %collective-permute-start.1 = (bf16[1,32,128]{2,1,0:T(8,128)(2,1)S(1)}, bf16[1,32,128]{2,1,0:T(8,128)(2,1)S(1)}, u32[]{:S(2)}, u32[]{:S(2)}) collective-permute-start(bf16[1,32,128]{2,1,0:T(8,128)(2,1)S(1)} %broadcast_in_dim_reshape.3), channel_id=1, source_target_pairs={{0,2},{1,3},{2,0},{3,1},{4,6},{5,7},{6,4},{7,5},{8,10},{9,11},{10,... | collective-permute-start | bytes 24584 | tf_op jit(solution)/shard_map/ppermute | solution.py:16
  8.4 3.1 %collective-permute-start.2 = (bf16[1,32,128]{2,1,0:T(8,128)(2,1)S(1)}, bf16[1,32,128]{2,1,0:T(8,128)(2,1)S(1)}, u32[]{:S(2)}, u32[]{:S(2)}) collective-permute-start(bf16[1,32,128]{2,1,0:T(8,128)(2,1)S(1)} %broadcast_in_dim_reshape.3), channel_id=1, source_target_pairs={{0,3},{1,2},{2,1},{3,0},{4,7},{5,6},{6,5},{7,4},{8,11},{9,10},{10,... | collective-permute-start | bytes 24584 | tf_op jit(solution)/shard_map/ppermute | solution.py:16
  11.5 4.3 %collective-permute-start.3 = (bf16[4,32,128]{2,1,0:T(8,128)(2,1)S(1)}, bf16[4,32,128]{2,1,0:T(8,128)(2,1)S(1)}, u32[]{:S(2)}, u32[]{:S(2)}) collective-permute-start(bf16[4,32,128]{2,1,0:T(8,128)(2,1)S(1)} %constant_dynamic-update-slice_fusion.refs_0_), channel_id=1, source_target_pairs={{0,4},{1,9},{4,0},{5,13},{8,12},{9,1},{12,8},{13,5},{2,6},{3,11},{... | collective-permute-start | bytes 98312 | tf_op jit(solution)/shard_map/ppermute | solution.py:37
  13.1 6.0 %collective-permute-start.5 = (bf16[4,32,128]{2,1,0:T(8,128)(2,1)S(1)}, bf16[4,32,128]{2,1,0:T(8,128)(2,1)S(1)}, u32[]{:S(2)}, u32[]{:S(2)}) collective-permute-start(bf16[4,32,128]{2,1,0:T(8,128)(2,1)S(1)} %constant_dynamic-update-slice_fusion.refs_0_), channel_id=1, source_target_pairs={{0,12},{1,13},{4,8},{5,9},{8,4},{9,5},{12,0},{13,1},{2,14},{3,15},... | collective-permute-start | bytes 98312 | tf_op jit(solution)/shard_map/ppermute | solution.py:37
  15.8 3.3 %collective-permute-start.4 = (bf16[4,32,128]{2,1,0:T(8,128)(2,1)S(1)}, bf16[4,32,128]{2,1,0:T(8,128)(2,1)S(1)}, u32[]{:S(2)}, u32[]{:S(2)}) collective-permute-start(bf16[4,32,128]{2,1,0:T(8,128)(2,1)S(1)} %collective-permute-done.3.refs_1_), channel_id=1, source_target_pairs={{0,1},{1,0},{2,3},{3,2},{4,5},{5,4},{6,7},{7,6},{8,9},{9,8},{10,11... | collective-permute-start | bytes 98312 | tf_op jit(solution)/shard_map/ppermute | solution.py:16
  19.5 4.4 %collective-permute-start.6 = (f32[8,256]{1,0:T(8,128)S(1)}, f32[8,256]{1,0:T(8,128)S(1)}, u32[]{:S(2)}, u32[]{:S(2)}) collective-permute-start(f32[8,256]{1,0:T(8,128)S(1)} %get-tuple-element.11), channel_id=1, source_target_pairs={{0,4},{1,8},{4,0},{5,12},{9,13},{8,1},{13,9},{12,5},{2,6},{3,10},{... | collective-permute-start | bytes 24584 | tf_op jit(solution)/shard_map/ppermute | solution.py:195
  19.5 4.4 %collective-permute-start.7 = (f32[8,256]{1,0:T(8,128)S(1)}, f32[8,256]{1,0:T(8,128)S(1)}, u32[]{:S(2)}, u32[]{:S(2)}) collective-permute-start(f32[8,256]{1,0:T(8,128)S(1)} %get-tuple-element.12), channel_id=1, source_target_pairs={{0,4},{1,12},{4,0},{5,8},{9,13},{8,5},{13,9},{12,1},{2,6},{3,14},{... | collective-permute-start | bytes 24584 | tf_op jit(solution)/shard_map/ppermute | solution.py:195
  24.0 1.9 %collective-permute-start.8 = (f32[4,256]{1,0:T(4,128)S(1)}, f32[4,256]{1,0:T(4,128)S(1)}, u32[]{:S(2)}, u32[]{:S(2)}) collective-permute-start(f32[4,256]{1,0:T(4,128)S(1)} %dynamic-slice_bitcast_fusion), channel_id=1, source_target_pairs={{0,1},{1,0},{2,3},{3,2},{4,5},{5,4},{6,7},{7,6},{8,9},{9,8},{10,11... | collective-permute-start | bytes 12296 | tf_op jit(solution)/shard_map/ppermute | solution.py:16

commit v5 on v4

--- a/solution.py
+++ b/solution.py
@@ -16,21 +16,51 @@
     return lax.ppermute(block, axis, [(i, i ^ step) for i in range(lax.axis_size(axis))])
 
 
+def project_kernel(acts_hbm, grads_hbm, act_proj_hbm, grad_proj_hbm, act_low_ref, grad_low_ref, acts, grads, act_proj, grad_proj, sems):
+    sources = (act_proj_hbm, acts_hbm, grad_proj_hbm, grads_hbm)
+    targets = (act_proj, acts, grad_proj, grads)
+    copies = [
+        pltpu.make_async_copy(s, t, sems.at[i]) for i, (s, t) in enumerate(zip(sources, targets))
+    ]
+    for copy in copies:
+        copy.start()
+    for copy in copies[:2]:
+        copy.wait()
+    act_sum = lax.dot_general(acts[...], act_proj[...], NT, preferred_element_type=jnp.float32)
+    for copy in copies[2:]:
+        copy.wait()
+    grad_sum = lax.dot_general(grad_proj[...], grads[...], NT, preferred_element_type=jnp.float32)
+    act_low_ref[...] = act_sum.astype(jnp.bfloat16)
+    grad_low_ref[...] = grad_sum.astype(jnp.bfloat16)
+
+
 def make_sketch(acts, grads, act_proj, grad_proj, tok_count):
-    seq_len, rank = acts.shape[0], act_proj.shape[1]
-    act_low = jnp.dot(acts, act_proj, preferred_element_type=jnp.float32).astype(jnp.bfloat16)
-    grad_low = jnp.dot(grads, grad_proj, preferred_element_type=jnp.float32).astype(jnp.bfloat16)
-    keep_mask = (jnp.arange(seq_len, dtype=jnp.int32) < tok_count).astype(jnp.bfloat16)
-    kept = grad_low * keep_mask[:, None]
-    outer_sum = jnp.dot(kept.T, act_low, preferred_element_type=jnp.float32) * (
-        1.0 / math.sqrt(seq_len)
-    )
-    return outer_sum.astype(jnp.bfloat16).reshape(rank // 2, 2 * rank)
+    seq_len, width = acts.shape
+    hidden, rank = grad_proj.shape
+    operands = (acts, grads, act_proj.T, grad_proj.T)
+    act_low, grad_low = pl.pallas_call(
+        project_kernel,
+        out_shape=[
+            jax.ShapeDtypeStruct((seq_len, rank), jnp.bfloat16),
+            jax.ShapeDtypeStruct((rank, seq_len), jnp.bfloat16),
+        ],
+        in_specs=[pl.BlockSpec(memory_space=pl.ANY)] * 4,
+        out_specs=[pl.BlockSpec(memory_space=pltpu.VMEM)] * 2,
+        scratch_shapes=[pltpu.VMEM(x.shape, x.dtype) for x in operands]
+        + [pltpu.SemaphoreType.DMA((4,))],
+        compiler_params=pltpu.CompilerParams(vmem_limit_bytes=16 * 2**20),
+        name="project",
+    )(*[pltpu.with_memory_space_constraint(x, pltpu.HBM) for x in operands])
+    mask = (jnp.arange(seq_len, dtype=jnp.int32) < tok_count).astype(jnp.bfloat16)
+    outer = jnp.dot(grad_low * mask[None, :], act_low, preferred_element_type=jnp.float32)
+    outer = outer * (1.0 / math.sqrt(seq_len))
+    return outer.astype(jnp.bfloat16).reshape(rank // 2, 2 * rank)
 
 
 def spread(block, distances):
+    crossed = int(distances[0] == distances[1])
     pairs = [
-        (e * len(distances) + p, (e ^ k) * len(distances) + p)
+        (e * len(distances) + p, (e ^ k) * len(distances) + (p ^ crossed))
         for e in range(lax.axis_size("ex"))
         for p, k in enumerate(distances)
     ]
@@ -46,7 +76,7 @@
     for k in range(1, ex_count, 2):
         distances = (k, min(k + 1, ex_count - 1))
         near = spread(block, distances)
-        pieces.append((near, distances, 0))
+        pieces.append((near, distances, int(distances[0] == distances[1])))
         if distances[0] != distances[1]:
             pieces.append((exchange(near, "pb", 1), distances, 1))
     return pieces
@@ -95,7 +125,12 @@
         outs[i][...] = chunks[here ^ (i + shift)]
     outs[half - 1][...] = jnp.where(near, 0.0, chunks[here ^ (half - 1)])
     own_ref[...] = jnp.where(near, chunks[here], 0.0)
-    open_ref[...] = jnp.where(example_ids_ref[...] == query_ids_ref[...], 0.0, 1.0)
+    spans = chunks.shape[2] // query_ids_ref.shape[1]
+    ids = [query_ids_ref[pl.ds(ex * spans + i, 1), :] for i in range(spans)]
+    ids = jnp.concatenate(ids, axis=1)
+    open_ref[...] = jnp.concatenate(
+        [jnp.where(example_ids_ref[:, a : a + 1] == ids, 0.0, 1.0) for a in range(ex_count)]
+    )
 
 
 def partial_scores(sizes, queries, query_ids, example_ids, pieces):
@@ -206,10 +241,8 @@
     )
     pieces = gather_rows(sketch)
     width = query_ids.shape[0] // ex_count
-    query_here = lax.dynamic_slice_in_dim(query_ids, lax.axis_index("ex") * width, width, 0)
-    *chunks, own, is_open = partial_scores(
-        sizes, query_sketch, query_here[None], example_ids, pieces
-    )
+    ids = query_ids.reshape(-1, min(width, 128))
+    *chunks, own, is_open = partial_scores(sizes, query_sketch, ids, example_ids.T, pieces)
     part = to_owners(chunks, ex_count)
     gram, own = make_gram(sizes, pieces, own)
     part = (part + own).reshape(pb_count, ex_count, -1)

time: 26.7 us -> 25.9 us (0.970)
  matrix products: 3.84 us -> 0.13 us
  Pallas kernels: 2.76 us -> 6.02 us
  local copies, waits for them, and re-layouts: 1.61 us -> 0.75 us
  waiting for transfers between devices: 6.48 us -> 7.1 us
    dot_general x2 -> x1, matrix products: 3.84 us -> 0.13 us  [make_sketch(): jnp.dot(grad_low * mask[None, :], act_low, preferred_element_type=jnp.flo...]
    pallas_call x0 -> x1, Pallas kernels: none -> 3.24 us  [make_sketch(): pl.pallas_call(project_kernel, out_shape=[jax.ShapeDtypeStruct((seq_len,...]
    dynamic_slice x1 -> x0, local copies, waits for them, and re-layouts: 0.76 us -> none  [shards(): lax.dynamic_slice_in_dim(query_ids, lax.axis_index('ex') * width, width, 0)]
    ppermute x2, starting transfers between devices: 4.05 us -> 3.42 us  [spread(): return lax.ppermute(block, ('ex', 'pb'), pairs)]
    ppermute x2, waiting for transfers between devices: 2.66 us -> 3.28 us  [spread(): return lax.ppermute(block, ('ex', 'pb'), pairs)]
    ppermute x5, starting transfers between devices: 4.21 us -> 4.78 us  [exchange(): lax.ppermute(block, axis, [(i, i ^ step) for i in range(lax.axis_size(axi...]
    unnamed x11 -> x10, local copies, waits for them, and re-layouts: 0.73 us -> 0.63 us
  transfers between devices with their start and end apart: 9 -> 9, of which waited for: 5 -> 5; matrix products, arithmetic and copies ran while one was open for 3% -> 0% of each run, Pallas kernels for 9% -> 9%
where the time goes in v5:
time: 25.9 us; the launch traced here: 25.7 us
  starting transfers between devices  10.2 us (39%)
  waiting for transfers between devices  7.1 us (27%)
  Pallas kernels  6.02 us (23%)
  between operations  1.47 us (6%)
  local copies, waits for them, and re-layouts  0.75 us (3%)
    ppermute x5, starting transfers between devices, exchange(): lax.ppermute(block, axis, [(i, i ^ step) for i in range(lax.axis_size(axi...  4.78 us
    ppermute x5, waiting for transfers between devices, exchange(): lax.ppermute(block, axis, [(i, i ^ step) for i in range(lax.axis_size(axi...  3.81 us
    ppermute x2, starting transfers between devices, spread(): return lax.ppermute(block, ('ex', 'pb'), pairs)  3.42 us
    ppermute x2, waiting for transfers between devices, spread(): return lax.ppermute(block, ('ex', 'pb'), pairs)  3.28 us
    pallas_call x1, Pallas kernels, make_sketch(): pl.pallas_call(project_kernel, out_shape=[jax.ShapeDtypeStruct((seq_len,...  3.24 us
    pallas_call x1, Pallas kernels, make_gram(): pl.pallas_call(functools.partial(gram_kernel, sizes, [piece[1:] for piece...  2.38 us
    ppermute x2, starting transfers between devices, to_owners(): arrived.append(lax.ppermute(chunk, ('ex', 'pb'), pairs))  2.04 us
    unnamed x10, local copies, waits for them, and re-layouts  0.63 us
  transfers between devices with their start and end apart: 9, of which 5 were waited for; matrix products, arithmetic and copies ran while one was open for 0% of the time, Pallas kernels for 9%

profile of v5, /device:TPU:0, one launch (start us, length us, event | category | flops | bytes accessed | tf_op | source)
XLA Modules:
  0.0 25.7 jit_solution(8220724785870229949)
XLA Ops:
  0.6 0.0 copy-start.1
  0.6 0.0 copy-start.2
  0.7 0.0 copy-start
  1.4 3.2 %project.1 = (bf16[128,64]{1,0:T(8,128)(2,1)S(1)}, bf16[64,128]{1,0:T(8,128)(2,1)S(1)}) custom-call(bf16[128,4096]{1,0:T(8,128)(2,1)} %bitcast.24, bf16[128,7168]{1,0:T(8,128)(2,1)} %bitcast.23, bf16[64,4096]{1,0:T(8,128)(2,1)} %bitcast.26, bf16[64,7168]{1,0:T(8,128)(2,1)} %bitcast.25), custom_call_target="tpu_custom_call" | custom-call | tf_op jit(solution)/shard_map/project/pallas_call | solution.py:41
  4.7 0.1 fusion
  4.8 0.1 broadcast_in_dim_reshape.3
  4.9 0.5 %collective-permute-start = (bf16[1,32,128]{2,1,0:T(8,128)(2,1)S(1)}, bf16[1,32,128]{2,1,0:T(8,128)(2,1)S(1)}, u32[]{:S(2)}, u32[]{:S(2)}) collective-permute-start(bf16[1,32,128]{2,1,0:T(8,128)(2,1)S(1)} %broadcast_in_dim_reshape.3), channel_id=1, source_target_pairs={{0,1},{1,0},{2,3},{3,2},{4,5},{5,4},{6,7},{7,6},{8,9},{9,8},{10,11... | collective-permute-start | bytes 24584 | tf_op jit(solution)/shard_map/ppermute | solution.py:16
  5.3 2.6 %collective-permute-start.1 = (bf16[1,32,128]{2,1,0:T(8,128)(2,1)S(1)}, bf16[1,32,128]{2,1,0:T(8,128)(2,1)S(1)}, u32[]{:S(2)}, u32[]{:S(2)}) collective-permute-start(bf16[1,32,128]{2,1,0:T(8,128)(2,1)S(1)} %broadcast_in_dim_reshape.3), channel_id=1, source_target_pairs={{0,2},{1,3},{2,0},{3,1},{4,6},{5,7},{6,4},{7,5},{8,10},{9,11},{10,... | collective-permute-start | bytes 24584 | tf_op jit(solution)/shard_map/ppermute | solution.py:16
  7.9 0.1 collective-permute-start.2
  8.0 0.0 collective-permute-done
  8.0 1.5 %collective-permute-done.1 = bf16[1,32,128]{2,1,0:T(8,128)(2,1)S(1)} collective-permute-done((bf16[1,32,128]{2,1,0:T(8,128)(2,1)S(1)}, bf16[1,32,128]{2,1,0:T(8,128)(2,1)S(1)}, u32[]{:S(2)}, u32[]{:S(2)}) %collective-permute-start.1) | collective-permute-done | bytes 8224 | tf_op jit(solution)/shard_map/ppermute | solution.py:16
  9.6 1.4 %collective-permute-done.2 = bf16[1,32,128]{2,1,0:T(8,128)(2,1)S(1)} collective-permute-done((bf16[1,32,128]{2,1,0:T(8,128)(2,1)S(1)}, bf16[1,32,128]{2,1,0:T(8,128)(2,1)S(1)}, u32[]{:S(2)}, u32[]{:S(2)}) %collective-permute-start.2) | collective-permute-done | bytes 8224 | tf_op jit(solution)/shard_map/ppermute | solution.py:16
  11.0 1.6 %collective-permute-start.3 = (bf16[4,32,128]{2,1,0:T(8,128)(2,1)S(1)}, bf16[4,32,128]{2,1,0:T(8,128)(2,1)S(1)}, u32[]{:S(2)}, u32[]{:S(2)}) collective-permute-start(bf16[4,32,128]{2,1,0:T(8,128)(2,1)S(1)} %constant_dynamic-update-slice_fusion.refs_0_), channel_id=1, source_target_pairs={{0,4},{1,9},{4,0},{5,13},{8,12},{9,1},{12,8},{13,5},{2,6},{3,11},{... | collective-permute-start | bytes 98312 | tf_op jit(solution)/shard_map/ppermute | solution.py:67
  12.6 1.9 %collective-permute-start.5 = (bf16[4,32,128]{2,1,0:T(8,128)(2,1)S(1)}, bf16[4,32,128]{2,1,0:T(8,128)(2,1)S(1)}, u32[]{:S(2)}, u32[]{:S(2)}) collective-permute-start(bf16[4,32,128]{2,1,0:T(8,128)(2,1)S(1)} %constant_dynamic-update-slice_fusion.refs_0_), channel_id=1, source_target_pairs={{0,13},{1,12},{4,9},{5,8},{8,5},{9,4},{12,1},{13,0},{2,15},{3,14},... | collective-permute-start | bytes 98312 | tf_op jit(solution)/shard_map/ppermute | solution.py:67
  14.4 0.8 %collective-permute-done.3.refs_1_ = bf16[4,32,128]{2,1,0:T(8,128)(2,1)S(1)} collective-permute-done((bf16[4,32,128]{2,1,0:T(8,128)(2,1)S(1)}, bf16[4,32,128]{2,1,0:T(8,128)(2,1)S(1)}, u32[]{:S(2)}, u32[]{:S(2)}) %collective-permute-start.3) | collective-permute-done | bytes 32800 | tf_op jit(solution)/shard_map/ppermute | solution.py:67
  15.3 0.0 collective-permute-start.4
  15.3 2.4 %collective-permute-done.5.refs_3_ = bf16[4,32,128]{2,1,0:T(8,128)(2,1)S(1)} collective-permute-done((bf16[4,32,128]{2,1,0:T(8,128)(2,1)S(1)}, bf16[4,32,128]{2,1,0:T(8,128)(2,1)S(1)}, u32[]{:S(2)}, u32[]{:S(2)}) %collective-permute-start.5) | collective-permute-done | bytes 32800 | tf_op jit(solution)/shard_map/ppermute | solution.py:67
  17.7 0.0 collective-permute-done.4.refs_2_
  17.7 0.0 copy-done.1
  17.7 0.0 copy-done.2
  17.7 0.0 copy-done
  17.7 0.4 %scores.1 = (f32[8,256]{1,0:T(8,128)S(1)}, f32[8,256]{1,0:T(8,128)S(1)}, f32[8,256]{1,0:T(8,128)S(1)}, f32[4,256]{1,0:T(4,128)S(1)}) custom-call(bf16[512,1024]{1,0:T(8,128)(2,1)S(1)} %copy-done, s32[8,128]{1,0:T(8,128)S(1)} %bitcast.21, s32[1,4]{1,0:T(1,128)S(1)} %bitcast.22, bf16[4,32,128]{2,1,0:T(8,128)(2,1)S(1)} %constant_dynamic-update-slice_fusion.refs_0_, ...), custom_call_target="tpu_custom_call" | custom-call | tf_op jit(solution)/shard_map/scores/pallas_call | solution.py:143
  18.1 0.1 collective-permute-start.6
  18.2 1.9 %collective-permute-start.7 = (f32[8,256]{1,0:T(8,128)S(1)}, f32[8,256]{1,0:T(8,128)S(1)}, u32[]{:S(2)}, u32[]{:S(2)}) collective-permute-start(f32[8,256]{1,0:T(8,128)S(1)} %get-tuple-element.16), channel_id=1, source_target_pairs={{0,4},{1,12},{4,0},{5,8},{9,13},{8,5},{13,9},{12,1},{2,6},{3,14},{... | collective-permute-start | bytes 24584 | tf_op jit(solution)/shard_map/ppermute | solution.py:230
  20.2 2.4 %gram.1 = (f32[1024,1024]{1,0:T(8,128)}, f32[8,256]{1,0:T(8,128)S(1)}) custom-call(f32[8,256]{1,0:T(8,128)S(1)} %get-tuple-element.12.kept_ref, bf16[4,32,128]{2,1,0:T(8,128)(2,1)S(1)} %constant_dynamic-update-slice_fusion.refs_0_, bf16[4,32,128]{2,1,0:T(8,128)(2,1)S(1)} %collective-permute-done.3.refs_1_, ...), custom_call_target="tpu_custom_call" | custom-call | flops 536870912 | bytes 4194304 | tf_op jit(solution)/shard_map/gram/pallas_call | solution.py:196
  22.5 0.0 collective-permute-done.6
  22.6 0.0 collective-permute-done.7
  22.6 1.7 %collective-permute-start.8 = (f32[4,256]{1,0:T(4,128)S(1)}, f32[4,256]{1,0:T(4,128)S(1)}, u32[]{:S(2)}, u32[]{:S(2)}) collective-permute-start(f32[4,256]{1,0:T(4,128)S(1)} %dynamic-slice_bitcast_fusion), channel_id=1, source_target_pairs={{0,1},{1,0},{2,3},{3,2},{4,5},{5,4},{6,7},{7,6},{8,9},{9,8},{10,11... | collective-permute-start | bytes 12296 | tf_op jit(solution)/shard_map/ppermute | solution.py:16
  24.3 0.8 %collective-permute-done.8 = f32[4,256]{1,0:T(4,128)S(1)} collective-permute-done((f32[4,256]{1,0:T(4,128)S(1)}, f32[4,256]{1,0:T(4,128)S(1)}, u32[]{:S(2)}, u32[]{:S(2)}) %collective-permute-start.8) | collective-permute-done | bytes 4128 | tf_op jit(solution)/shard_map/ppermute | solution.py:16
  25.1 0.6 %copy.10 = f32[256,4,1]{0,2,1:T(1,128)} copy(f32[256,4,1]{0,1,2:T(4,128)S(1)} %fusion.4) | data formatting | bytes 8192
  (9 shorter events, 0.1 us)
Async XLA Ops:
  0.6 17.1 %copy-start.1 = (s32[1024]{0:T(1024)S(1)}, s32[1024]{0:T(1024)}, u32[]{:S(2)}) copy-start(s32[1024]{0:T(1024)} %param.15) | copy-start | bytes 12292
  0.6 17.1 %copy-start.2 = (s32[4,1]{0,1:T(1,128)S(1)}, s32[4,1]{0,1:T(1,128)}, u32[]{:S(2)}) copy-start(s32[4,1]{0,1:T(1,128)} %param.13) | copy-start | bytes 52
  0.7 17.1 %copy-start = (bf16[512,1024]{1,0:T(8,128)(2,1)S(1)}, bf16[512,1024]{1,0:T(8,128)(2,1)}, u32[]{:S(2)}) copy-start(bf16[512,1024]{1,0:T(8,128)(2,1)} %query_ref.1) | copy-start | bytes 3145732
  4.9 3.1 %collective-permute-start = (bf16[1,32,128]{2,1,0:T(8,128)(2,1)S(1)}, bf16[1,32,128]{2,1,0:T(8,128)(2,1)S(1)}, u32[]{:S(2)}, u32[]{:S(2)}) collective-permute-start(bf16[1,32,128]{2,1,0:T(8,128)(2,1)S(1)} %broadcast_in_dim_reshape.3), channel_id=1, source_target_pairs={{0,1},{1,0},{2,3},{3,2},{4,5},{5,4},{6,7},{7,6},{8,9},{9,8},{10,11... | collective-permute-start | bytes 24584 | tf_op jit(solution)/shard_map/ppermute | solution.py:16
  5.3 4.2 %collective-permute-start.1 = (bf16[1,32,128]{2,1,0:T(8,128)(2,1)S(1)}, bf16[1,32,128]{2,1,0:T(8,128)(2,1)S(1)}, u32[]{:S(2)}, u32[]{:S(2)}) collective-permute-start(bf16[1,32,128]{2,1,0:T(8,128)(2,1)S(1)} %broadcast_in_dim_reshape.3), channel_id=1, source_target_pairs={{0,2},{1,3},{2,0},{3,1},{4,6},{5,7},{6,4},{7,5},{8,10},{9,11},{10,... | collective-permute-start | bytes 24584 | tf_op jit(solution)/shard_map/ppermute | solution.py:16
  7.9 3.1 %collective-permute-start.2 = (bf16[1,32,128]{2,1,0:T(8,128)(2,1)S(1)}, bf16[1,32,128]{2,1,0:T(8,128)(2,1)S(1)}, u32[]{:S(2)}, u32[]{:S(2)}) collective-permute-start(bf16[1,32,128]{2,1,0:T(8,128)(2,1)S(1)} %broadcast_in_dim_reshape.3), channel_id=1, source_target_pairs={{0,3},{1,2},{2,1},{3,0},{4,7},{5,6},{6,5},{7,4},{8,11},{9,10},{10,... | collective-permute-start | bytes 24584 | tf_op jit(solution)/shard_map/ppermute | solution.py:16
  11.0 4.3 %collective-permute-start.3 = (bf16[4,32,128]{2,1,0:T(8,128)(2,1)S(1)}, bf16[4,32,128]{2,1,0:T(8,128)(2,1)S(1)}, u32[]{:S(2)}, u32[]{:S(2)}) collective-permute-start(bf16[4,32,128]{2,1,0:T(8,128)(2,1)S(1)} %constant_dynamic-update-slice_fusion.refs_0_), channel_id=1, source_target_pairs={{0,4},{1,9},{4,0},{5,13},{8,12},{9,1},{12,8},{13,5},{2,6},{3,11},{... | collective-permute-start | bytes 98312 | tf_op jit(solution)/shard_map/ppermute | solution.py:67
  12.6 5.1 %collective-permute-start.5 = (bf16[4,32,128]{2,1,0:T(8,128)(2,1)S(1)}, bf16[4,32,128]{2,1,0:T(8,128)(2,1)S(1)}, u32[]{:S(2)}, u32[]{:S(2)}) collective-permute-start(bf16[4,32,128]{2,1,0:T(8,128)(2,1)S(1)} %constant_dynamic-update-slice_fusion.refs_0_), channel_id=1, source_target_pairs={{0,13},{1,12},{4,9},{5,8},{8,5},{9,4},{12,1},{13,0},{2,15},{3,14},... | collective-permute-start | bytes 98312 | tf_op jit(solution)/shard_map/ppermute | solution.py:67
  15.3 2.4 %collective-permute-start.4 = (bf16[4,32,128]{2,1,0:T(8,128)(2,1)S(1)}, bf16[4,32,128]{2,1,0:T(8,128)(2,1)S(1)}, u32[]{:S(2)}, u32[]{:S(2)}) collective-permute-start(bf16[4,32,128]{2,1,0:T(8,128)(2,1)S(1)} %collective-permute-done.3.refs_1_), channel_id=1, source_target_pairs={{0,1},{1,0},{2,3},{3,2},{4,5},{5,4},{6,7},{7,6},{8,9},{9,8},{10,11... | collective-permute-start | bytes 98312 | tf_op jit(solution)/shard_map/ppermute | solution.py:16
  18.1 4.4 %collective-permute-start.6 = (f32[8,256]{1,0:T(8,128)S(1)}, f32[8,256]{1,0:T(8,128)S(1)}, u32[]{:S(2)}, u32[]{:S(2)}) collective-permute-start(f32[8,256]{1,0:T(8,128)S(1)} %get-tuple-element.15), channel_id=1, source_target_pairs={{0,4},{1,8},{4,0},{5,12},{9,13},{8,1},{13,9},{12,5},{2,6},{3,10},{... | collective-permute-start | bytes 24584 | tf_op jit(solution)/shard_map/ppermute | solution.py:230
  18.2 4.3 %collective-permute-start.7 = (f32[8,256]{1,0:T(8,128)S(1)}, f32[8,256]{1,0:T(8,128)S(1)}, u32[]{:S(2)}, u32[]{:S(2)}) collective-permute-start(f32[8,256]{1,0:T(8,128)S(1)} %get-tuple-element.16), channel_id=1, source_target_pairs={{0,4},{1,12},{4,0},{5,8},{9,13},{8,5},{13,9},{12,1},{2,6},{3,14},{... | collective-permute-start | bytes 24584 | tf_op jit(solution)/shard_map/ppermute | solution.py:230
  22.6 2.5 %collective-permute-start.8 = (f32[4,256]{1,0:T(4,128)S(1)}, f32[4,256]{1,0:T(4,128)S(1)}, u32[]{:S(2)}, u32[]{:S(2)}) collective-permute-start(f32[4,256]{1,0:T(4,128)S(1)} %dynamic-slice_bitcast_fusion), channel_id=1, source_target_pairs={{0,1},{1,0},{2,3},{3,2},{4,5},{5,4},{6,7},{7,6},{8,9},{9,8},{10,11... | collective-permute-start | bytes 12296 | tf_op jit(solution)/shard_map/ppermute | solution.py:16

commit v6 on v5

--- a/solution.py
+++ b/solution.py
@@ -9,6 +9,7 @@
 from jax.sharding import PartitionSpec as P
 
 DAMPING = 0.1
+LANES = 128
 NT = (((1,), (1,)), ((), ()))
 
 
@@ -54,7 +55,7 @@
     mask = (jnp.arange(seq_len, dtype=jnp.int32) < tok_count).astype(jnp.bfloat16)
     outer = jnp.dot(grad_low * mask[None, :], act_low, preferred_element_type=jnp.float32)
     outer = outer * (1.0 / math.sqrt(seq_len))
-    return outer.astype(jnp.bfloat16).reshape(rank // 2, 2 * rank)
+    return outer.astype(jnp.bfloat16).reshape(rank * rank // LANES, LANES)
 
 
 def spread(block, distances):
@@ -67,56 +68,92 @@
     return lax.ppermute(block, ("ex", "pb"), pairs)
 
 
-def gather_rows(sketch):
-    ex_count = lax.axis_size("ex")
-    fp_count = lax.axis_size(("feat", "pb"))
-    own = sketch[None]
+def take(block, index):
+    return lax.dynamic_index_in_dim(block, index, 1, keepdims=False)
+
+
+def pairs_of_distances(ex_count):
+    return [(k, min(k + 1, ex_count - 1)) for k in range(1, ex_count, 2)]
+
+
+def gather_rows(sizes, sketch, queries):
+    ex_count, feat_count, pb_count = sizes
+    ex, feat, pb = (lax.axis_index(axis) for axis in ("ex", "feat", "pb"))
+    fp_count, fp = feat_count * pb_count, feat * pb_count + pb
+    ratio = ex_count // fp_count
+    sketch, queries = lax.optimization_barrier((sketch, queries))
+    own = sketch.reshape(1, ex_count, -1, LANES)
+    others = exchange(queries, "pb", 1)
     block = jnp.concatenate([own] + [exchange(own, ("feat", "pb"), s) for s in range(1, fp_count)])
+    by_fp = block.reshape(fp_count, fp_count, ratio, -1, LANES)
+
+    def columns(index):
+        return jnp.moveaxis(take(by_fp, index), 1, 0)
+
     pieces = [(block, (0, 0), 0)]
-    for k in range(1, ex_count, 2):
-        distances = (k, min(k + 1, ex_count - 1))
-        near = spread(block, distances)
-        pieces.append((near, distances, int(distances[0] == distances[1])))
-        if distances[0] != distances[1]:
-            pieces.append((exchange(near, "pb", 1), distances, 1))
-    return pieces
-
-
-def place_rows(sizes, sources, pieces, rows):
-    ex_count, fp_count = sizes[0], sizes[1] * sizes[2]
+    for near, far in pairs_of_distances(ex_count):
+        theirs = take(block, ex ^ (near + (far - near) * pb))[None]
+        for_other = jnp.concatenate([theirs, columns(fp ^ 1)])
+        if near == far:
+            pieces.append((spread(for_other, (near, far)), (near, far), 1))
+        else:
+            both = spread(jnp.concatenate([columns(fp), for_other]), (near, far))
+            pieces.append((both, (near, far), 0))
+            pieces.append((exchange(both[ratio:], "pb", 1), (far, near), 1))
+    return pieces, others
+
+
+def place_rows(sizes, origins, pieces, left_rows, right_rows=None):
+    ex_count, feat_count, pb_count = sizes
     ex, pb = lax.axis_index("ex"), lax.axis_index("pb")
-    fp = lax.axis_index("feat") * sizes[2] + pb
-    for piece, (distances, core) in zip(pieces, sources):
-        first, step = distances[core], distances[1 - core] - distances[core]
-        where = ex ^ (first + step * pb)
+    fp_count = feat_count * pb_count
+    ratio = ex_count // fp_count
+    fp = lax.axis_index("feat") * pb_count + pb
+    for piece, (distances, other) in zip(pieces, origins):
+        where = ex ^ (distances[0] + (distances[1] - distances[0]) * pb)
+        whole = distances == (0, 0)
+        left, right = (0, 1) if other else (ratio, 0)
         for s in range(fp_count):
-            rows[(fp ^ core ^ s) * ex_count + where] = piece[s].astype(jnp.float32)
-
-
-def score_kernel(sizes, sources, query_ref, query_ids_ref, example_ids_ref, *refs):
+            slot = (fp ^ other ^ s) * ex_count + where
+            block = piece[s, ex] if whole else piece[left, s]
+            left_rows[slot] = block.astype(jnp.float32)
+            if right_rows is not None:
+                block = piece[s, pl.ds(fp * ratio, ratio)] if whole else piece[right : right + ratio, s]
+                right_rows[slot] = block.astype(jnp.float32).reshape(right_rows.shape[1:])
+
+
+def score_kernel(
+    sizes, origins, query_ref, other_query_ref, query_ids_ref, example_ids_ref, *refs
+):
     ex_count, feat_count, pb_count = sizes
+    pieces, refs = refs[: len(origins)], refs[len(origins) :]
     half = ex_count // pb_count
-    pieces, outs = refs[: len(sources)], refs[len(sources) : len(sources) + half]
-    own_ref, open_ref, rows, scaled, chunks = refs[-5:]
+    outs = refs[:half]
+    own_ref, open_ref, rows, scaled, chunks, products = refs[-6:]
     ex, feat = lax.axis_index("ex"), lax.axis_index("feat")
-    near = lax.div(ex, half) == lax.axis_index("pb")
+    near = lax.axis_index("pb") == 0
     here = lax.rem(ex, half)
-    examples, lines, lanes = rows.shape
-    block_lines = lines // ex_count
+    examples, block_lines, lanes = rows.shape
     mine = ex_count * pb_count
-    place_rows(sizes, sources, pieces, rows)
-    block = rows[:, pl.ds(ex * block_lines, block_lines), :]
-    diag = jnp.sum(block * block, axis=0) / examples
-    weight = 1.0 / (math.sqrt(lines * lanes) * (diag + DAMPING))
-    own = rows[pl.ds(feat * mine, mine), pl.ds(ex * block_lines, block_lines), :]
+    place_rows(sizes, origins, pieces, rows)
+    diag = jnp.sum(rows[...] * rows[...], axis=0) / examples
+    weight = 1.0 / (math.sqrt(ex_count * block_lines * lanes) * (diag + DAMPING))
+    own = rows[pl.ds(feat * mine, mine)]
     scaled[...] = (own * weight[None]).reshape(mine * block_lines, lanes)
     parts = [scaled[pl.ds(j, mine, stride=block_lines), :] for j in range(block_lines)]
     wide = jnp.concatenate(parts, axis=1)
     high = wide.astype(jnp.bfloat16)
     low = (wide - high.astype(jnp.float32)).astype(jnp.bfloat16)
     both = jnp.concatenate([high, low], axis=0)
-    products = lax.dot_general(both, query_ref[...], NT, preferred_element_type=jnp.float32)
-    result = products[:mine] + products[mine:]
+    for side, queries in enumerate((query_ref, other_query_ref)):
+
+        @pl.when(lax.div(ex, half) == side)
+        def _():
+            products[...] = lax.dot_general(
+                both, queries[...], NT, preferred_element_type=jnp.float32
+            )
+
+    result = products[:mine, :] + products[mine:, :]
     width = chunks.shape[2]
     for t in range(half):
         chunks[t] = result[:, t * width : (t + 1) * width]
@@ -133,10 +170,10 @@
     )
 
 
-def partial_scores(sizes, queries, query_ids, example_ids, pieces):
+def partial_scores(sizes, queries, other_queries, query_ids, example_ids, pieces):
     ex_count, feat_count, pb_count = sizes
     examples = ex_count * feat_count * pb_count
-    lines, lanes = pieces[0][0].shape[1:]
+    lines, lanes = pieces[0][0].shape[2:]
     half = ex_count // pb_count
     chunk = (pb_count * ex_count, queries.shape[0] // half)
     vmem = pl.BlockSpec(memory_space=pltpu.VMEM)
@@ -144,32 +181,28 @@
         functools.partial(score_kernel, sizes, [piece[1:] for piece in pieces]),
         out_shape=[jax.ShapeDtypeStruct(chunk, jnp.float32)] * (half + 1)
         + [jax.ShapeDtypeStruct((ex_count, chunk[1]), jnp.float32)],
-        in_specs=[vmem] * (3 + len(pieces)),
+        in_specs=[vmem] * (4 + len(pieces)),
         out_specs=[vmem] * (half + 2),
         scratch_shapes=[
             pltpu.VMEM((examples, lines, lanes), jnp.float32),
-            pltpu.VMEM((pb_count * lines, lanes), jnp.float32),
+            pltpu.VMEM((pb_count * ex_count * lines, lanes), jnp.float32),
             pltpu.VMEM((half, *chunk), jnp.float32),
+            pltpu.VMEM((2 * chunk[0], queries.shape[0]), jnp.float32),
         ],
         compiler_params=pltpu.CompilerParams(vmem_limit_bytes=24 * 2**20),
         name="scores",
-    )(queries, query_ids, example_ids, *[piece[0] for piece in pieces])
-
-
-def gram_kernel(sizes, sources, kept_ref, *refs):
-    ex_count, fp_count = sizes[0], sizes[1] * sizes[2]
-    pieces = refs[: len(sources)]
-    out_hbm, kept_out_ref, rows, left, right, result, sems = refs[len(sources) :]
-    ex = lax.axis_index("ex")
-    fp = lax.axis_index("feat") * sizes[2] + lax.axis_index("pb")
-    examples, lines, lanes = rows.shape
-    left_lines, right_lines = lines // ex_count, lines // fp_count
+    )(queries, other_queries, query_ids, example_ids, *[piece[0] for piece in pieces])
+
+
+def gram_kernel(sizes, origins, kept_ref, *refs):
+    pieces, refs = refs[: len(origins)], refs[len(origins) :]
+    out_hbm, kept_out_ref, left_rows, right_rows, left, right, result, sems = refs
     kept_out_ref[...] = kept_ref[...]
-    place_rows(sizes, sources, pieces, rows)
-    block = rows[:, pl.ds(ex * left_lines, left_lines), :]
-    left[...] = block.reshape(examples * left_lines, lanes)
-    block = rows[:, pl.ds(fp * right_lines, right_lines), :]
-    right[...] = block.reshape(examples * right_lines, lanes)
+    examples, left_lines, lanes = left_rows.shape
+    right_lines = right_rows.shape[1]
+    place_rows(sizes, origins, pieces, left_rows, right_rows)
+    left[...] = left_rows[...].reshape(examples * left_lines, lanes)
+    right[...] = right_rows[...].reshape(examples * right_lines, lanes)
     across = jnp.concatenate(
         [right[pl.ds(j, examples, stride=right_lines), :] for j in range(right_lines)], axis=1
     ).astype(jnp.bfloat16)
@@ -188,11 +221,10 @@
 
 
 def make_gram(sizes, pieces, kept):
-    ex_count, fp_count = sizes[0], sizes[1] * sizes[2]
-    examples = ex_count * fp_count
-    lines, lanes = pieces[0][0].shape[1:]
-    left_lines, right_lines = lines // ex_count, lines // fp_count
-    shape = (left_lines * lanes, right_lines * lanes)
+    examples = sizes[0] * sizes[1] * sizes[2]
+    left_lines = pieces[0][0].shape[2]
+    right_lines = left_lines * sizes[0] // (sizes[1] * sizes[2])
+    shape = (left_lines * LANES, right_lines * LANES)
     return pl.pallas_call(
         functools.partial(gram_kernel, sizes, [piece[1:] for piece in pieces]),
         out_shape=[
@@ -202,9 +234,10 @@
         in_specs=[pl.BlockSpec(memory_space=pltpu.VMEM)] * (1 + len(pieces)),
         out_specs=[pl.BlockSpec(memory_space=pl.ANY), pl.BlockSpec(memory_space=pltpu.VMEM)],
         scratch_shapes=[
-            pltpu.VMEM((examples, lines, lanes), jnp.float32),
-            pltpu.VMEM((examples * left_lines, lanes), jnp.float32),
-            pltpu.VMEM((examples * right_lines, lanes), jnp.float32),
+            pltpu.VMEM((examples, left_lines, LANES), jnp.float32),
+            pltpu.VMEM((examples, right_lines, LANES), jnp.float32),
+            pltpu.VMEM((examples * left_lines, LANES), jnp.float32),
+            pltpu.VMEM((examples * right_lines, LANES), jnp.float32),
             pltpu.VMEM(shape, jnp.float32),
             pltpu.SemaphoreType.DMA((left_lines,)),
         ],
@@ -224,9 +257,8 @@
     for i, chunk in enumerate(chunks):
         pairs = []
         for e in range(ex_count):
-            near, far = e // half, 1 - e // half
-            pairs.append((e * 2 + near, (e ^ (i + 1 if i < half - 1 else 1)) * 2 + near))
-            pairs.append((e * 2 + far, (e ^ (half + i)) * 2 + near))
+            pairs.append((e * 2, (e ^ (i + 1 if i < half - 1 else 1)) * 2))
+            pairs.append((e * 2 + 1, (e ^ (half + i)) * 2 + 1))
         arrived.append(lax.ppermute(chunk, ("ex", "pb"), pairs))
     return sum(arrived)
 
@@ -239,10 +271,12 @@
     sketch = make_sketch(
         activations[0, 0], out_grads[0, 0], act_proj, grad_proj, tok_counts[0, 0]
     )
-    pieces = gather_rows(sketch)
+    pieces, others = gather_rows(sizes, sketch, query_sketch)
     width = query_ids.shape[0] // ex_count
     ids = query_ids.reshape(-1, min(width, 128))
-    *chunks, own, is_open = partial_scores(sizes, query_sketch, ids, example_ids.T, pieces)
+    *chunks, own, is_open = partial_scores(
+        sizes, query_sketch, others, ids, example_ids.T, pieces
+    )
     part = to_owners(chunks, ex_count)
     gram, own = make_gram(sizes, pieces, own)
     part = (part + own).reshape(pb_count, ex_count, -1)

time: 25.9 us -> 25.7 us (level)
  starting transfers between devices: 10.2 us -> 9.93 us
    ppermute x5 -> x6, starting transfers between devices: 4.78 us -> 4.44 us  [exchange(): lax.ppermute(block, axis, [(i, i ^ step) for i in range(lax.axis_size(axi...]
    ppermute x5 -> x6, waiting for transfers between devices: 3.81 us -> 3.97 us  [exchange(): lax.ppermute(block, axis, [(i, i ^ step) for i in range(lax.axis_size(axi...]
    unnamed x10 -> x7, local copies, waits for them, and re-layouts: 0.63 us -> 0.61 us
  transfers between devices with their start and end apart: 9 -> 10, of which waited for: 5 -> 5; matrix products, arithmetic and copies ran while one was open for 0% -> 0% of each run, Pallas kernels for 9% -> 9%
where the time goes in v6:
time: 25.7 us; the launch traced here: 25.5 us
  starting transfers between devices  9.93 us (39%)
  waiting for transfers between devices  7.04 us (27%)
  Pallas kernels  6.16 us (24%)
  between operations  1.48 us (6%)
  local copies, waits for them, and re-layouts  0.74 us (3%)
    ppermute x6, starting transfers between devices, exchange(): lax.ppermute(block, axis, [(i, i ^ step) for i in range(lax.axis_size(axi...  4.44 us
    ppermute x6, waiting for transfers between devices, exchange(): lax.ppermute(block, axis, [(i, i ^ step) for i in range(lax.axis_size(axi...  3.97 us
    ppermute x2, starting transfers between devices, spread(): return lax.ppermute(block, ('ex', 'pb'), pairs)  3.45 us
    pallas_call x1, Pallas kernels, make_sketch(): pl.pallas_call(project_kernel, out_shape=[jax.ShapeDtypeStruct((seq_len,...  3.25 us
    ppermute x2, waiting for transfers between devices, spread(): return lax.ppermute(block, ('ex', 'pb'), pairs)  3.06 us
    pallas_call x1, Pallas kernels, make_gram(): pl.pallas_call(functools.partial(gram_kernel, sizes, [piece[1:] for piece...  2.37 us
    ppermute x2, starting transfers between devices, to_owners(): arrived.append(lax.ppermute(chunk, ('ex', 'pb'), pairs))  2.05 us
    unnamed x7, local copies, waits for them, and re-layouts  0.61 us
  transfers between devices with their start and end apart: 10, of which 5 were waited for; matrix products, arithmetic and copies ran while one was open for 0% of the time, Pallas kernels for 9%

profile of v6, /device:TPU:0, one launch (start us, length us, event | category | flops | bytes accessed | tf_op | source)
XLA Modules:
  0.0 25.5 jit_solution(6571324976460938781)
XLA Ops:
  0.6 0.0 copy-start
  0.6 0.0 copy-start.1
  0.7 0.0 copy-start.2
  1.4 3.2 %project.1 = (bf16[128,64]{1,0:T(8,128)(2,1)S(1)}, bf16[64,128]{1,0:T(8,128)(2,1)S(1)}) custom-call(bf16[128,4096]{1,0:T(8,128)(2,1)} %bitcast.33, bf16[128,7168]{1,0:T(8,128)(2,1)} %bitcast.32, bf16[64,4096]{1,0:T(8,128)(2,1)} %bitcast.35, bf16[64,7168]{1,0:T(8,128)(2,1)} %bitcast.34), custom_call_target="tpu_custom_call" | custom-call | tf_op jit(solution)/shard_map/project/pallas_call | solution.py:42
  4.7 0.1 fusion
  4.8 0.1 reshape.30
  4.9 0.0 copy-done
  4.9 0.5 %collective-permute-start = (bf16[512,1024]{1,0:T(8,128)(2,1)S(1)}, bf16[512,1024]{1,0:T(8,128)(2,1)S(1)}, u32[]{:S(2)}, u32[]{:S(2)}) collective-permute-start(bf16[512,1024]{1,0:T(8,128)(2,1)S(1)} %copy-done), channel_id=1, source_target_pairs={{0,1},{1,0},{2,3},{3,2},{4,5},{5,4},{6,7},{7,6},{8,9},{9,8},{10,11... | collective-permute-start | bytes 3145736 | tf_op jit(solution)/shard_map/ppermute | solution.py:17
  5.4 0.1 collective-permute-start.1
  5.5 2.9 %collective-permute-start.2 = (bf16[1,4,8,128]{3,2,1,0:T(8,128)(2,1)S(1)}, bf16[1,4,8,128]{3,2,1,0:T(8,128)(2,1)S(1)}, u32[]{:S(2)}, u32[]{:S(2)}) collective-permute-start(bf16[1,4,8,128]{3,2,1,0:T(8,128)(2,1)S(1)} %bitcast.37), channel_id=1, source_target_pairs={{0,2},{1,3},{2,0},{3,1},{4,6},{5,7},{6,4},{7,5},{8,10},{9,11},{10,... | collective-permute-start | bytes 24584 | tf_op jit(solution)/shard_map/ppermute | solution.py:17
  8.4 0.0 collective-permute-start.3
  8.4 0.0 collective-permute-done.1
  8.4 1.6 %collective-permute-done.2 = bf16[1,4,8,128]{3,2,1,0:T(8,128)(2,1)S(1)} collective-permute-done((bf16[1,4,8,128]{3,2,1,0:T(8,128)(2,1)S(1)}, bf16[1,4,8,128]{3,2,1,0:T(8,128)(2,1)S(1)}, u32[]{:S(2)}, u32[]{:S(2)}) %collective-permute-start.2) | collective-permute-done | bytes 8224 | tf_op jit(solution)/shard_map/ppermute | solution.py:17
  10.0 1.5 %collective-permute-done.3 = bf16[1,4,8,128]{3,2,1,0:T(8,128)(2,1)S(1)} collective-permute-done((bf16[1,4,8,128]{3,2,1,0:T(8,128)(2,1)S(1)}, bf16[1,4,8,128]{3,2,1,0:T(8,128)(2,1)S(1)}, u32[]{:S(2)}, u32[]{:S(2)}) %collective-permute-start.3) | collective-permute-done | bytes 8224 | tf_op jit(solution)/shard_map/ppermute | solution.py:17
  11.6 1.6 %collective-permute-start.4 = (bf16[3,4,8,128]{3,2,1,0:T(8,128)(2,1)S(1)}, bf16[3,4,8,128]{3,2,1,0:T(8,128)(2,1)S(1)}, u32[]{:S(2)}, u32[]{:S(2)}) collective-permute-start(bf16[3,4,8,128]{3,2,1,0:T(8,128)(2,1)S(1)} %pad_maximum_fusion.1), channel_id=1, source_target_pairs={{0,4},{1,9},{4,0},{5,13},{8,12},{9,1},{12,8},{13,5},{2,6},{3,11},{... | collective-permute-start | bytes 73736 | tf_op jit(solution)/shard_map/ppermute | solution.py:68
  13.2 1.8 %collective-permute-start.6 = (bf16[2,4,8,128]{3,2,1,0:T(8,128)(2,1)S(1)}, bf16[2,4,8,128]{3,2,1,0:T(8,128)(2,1)S(1)}, u32[]{:S(2)}, u32[]{:S(2)}) collective-permute-start(bf16[2,4,8,128]{3,2,1,0:T(8,128)(2,1)S(1)} %pad_maximum_fusion.2), channel_id=1, source_target_pairs={{0,13},{1,12},{4,9},{5,8},{8,5},{9,4},{12,1},{13,0},{2,15},{3,14},... | collective-permute-start | bytes 49160 | tf_op jit(solution)/shard_map/ppermute | solution.py:68
  15.0 0.7 %collective-permute-done.4.refs_1_ = bf16[3,4,8,128]{3,2,1,0:T(8,128)(2,1)S(1)} collective-permute-done((bf16[3,4,8,128]{3,2,1,0:T(8,128)(2,1)S(1)}, bf16[3,4,8,128]{3,2,1,0:T(8,128)(2,1)S(1)}, u32[]{:S(2)}, u32[]{:S(2)}) %collective-permute-start.4) | collective-permute-done | bytes 24608 | tf_op jit(solution)/shard_map/ppermute | solution.py:68
  15.7 0.1 collective-permute-start.5
  15.8 2.4 %collective-permute-done.6.refs_3_ = bf16[2,4,8,128]{3,2,1,0:T(8,128)(2,1)S(1)} collective-permute-done((bf16[2,4,8,128]{3,2,1,0:T(8,128)(2,1)S(1)}, bf16[2,4,8,128]{3,2,1,0:T(8,128)(2,1)S(1)}, u32[]{:S(2)}, u32[]{:S(2)}) %collective-permute-start.6) | collective-permute-done | bytes 16416 | tf_op jit(solution)/shard_map/ppermute | solution.py:68
  18.2 0.0 collective-permute-done.5.refs_2_
  18.2 0.0 collective-permute-done.other_query_ref
  18.2 0.0 copy-done.1
  18.2 0.0 copy-done.2
  18.2 0.5 %scores.1 = (f32[8,256]{1,0:T(8,128)S(1)}, f32[8,256]{1,0:T(8,128)S(1)}, f32[8,256]{1,0:T(8,128)S(1)}, f32[4,256]{1,0:T(4,128)S(1)}) custom-call(bf16[512,1024]{1,0:T(8,128)(2,1)S(1)} %copy-done, bf16[512,1024]{1,0:T(8,128)(2,1)S(1)} %collective-permute-done.other_query_ref, s32[8,128]{1,0:T(8,128)S(1)} %bitcast.30, s32[1,4]{1,0:T(1,128)S(1)} %bitcast.31, ...), custom_call_target="tpu_custom_call" | custom-call | tf_op jit(solution)/shard_map/scores/pallas_call | solution.py:180
  18.7 0.2 collective-permute-start.7
  18.9 1.9 %collective-permute-start.8 = (f32[8,256]{1,0:T(8,128)S(1)}, f32[8,256]{1,0:T(8,128)S(1)}, u32[]{:S(2)}, u32[]{:S(2)}) collective-permute-start(f32[8,256]{1,0:T(8,128)S(1)} %get-tuple-element.20), channel_id=1, source_target_pairs={{0,4},{1,13},{4,0},{5,9},{8,12},{9,5},{12,8},{13,1},{2,6},{3,15},{... | collective-permute-start | bytes 24584 | tf_op jit(solution)/shard_map/ppermute | solution.py:262
  20.8 2.4 %gram.1 = (f32[1024,1024]{1,0:T(8,128)}, f32[8,256]{1,0:T(8,128)S(1)}) custom-call(f32[8,256]{1,0:T(8,128)S(1)} %get-tuple-element.16.kept_ref, bf16[4,4,8,128]{3,2,1,0:T(8,128)(2,1)S(1)} %pad_maximum_fusion.refs_0_, bf16[3,4,8,128]{3,2,1,0:T(8,128)(2,1)S(1)} %collective-permute-done.4.refs_1_, bf16[2,4,8,128]{3,2,1,0:T(8,128)(2,1)S(1)} %collective-permute-done.5.refs_2_, ...), custom_call_target="tpu_custom_call" | custom-call | flops 536870912 | bytes 4194304 | tf_op jit(solution)/shard_map/gram/pallas_call | solution.py:228
  23.2 0.0 collective-permute-done.7
  23.2 0.0 collective-permute-done.8
  23.2 0.9 %collective-permute-start.9 = (f32[4,256]{1,0:T(4,128)S(1)}, f32[4,256]{1,0:T(4,128)S(1)}, u32[]{:S(2)}, u32[]{:S(2)}) collective-permute-start(f32[4,256]{1,0:T(4,128)S(1)} %dynamic-slice_bitcast_fusion.4), channel_id=1, source_target_pairs={{0,1},{1,0},{2,3},{3,2},{4,5},{5,4},{6,7},{7,6},{8,9},{9,8},{10,11... | collective-permute-start | bytes 12296 | tf_op jit(solution)/shard_map/ppermute | solution.py:17
  24.1 0.8 %collective-permute-done.9 = f32[4,256]{1,0:T(4,128)S(1)} collective-permute-done((f32[4,256]{1,0:T(4,128)S(1)}, f32[4,256]{1,0:T(4,128)S(1)}, u32[]{:S(2)}, u32[]{:S(2)}) %collective-permute-start.9) | collective-permute-done | bytes 4128 | tf_op jit(solution)/shard_map/ppermute | solution.py:17
  24.9 0.6 %copy.10 = f32[256,4,1]{0,2,1:T(1,128)} copy(f32[256,4,1]{0,1,2:T(4,128)S(1)} %fusion.4) | data formatting | bytes 8192
  (10 shorter events, 0.1 us)
Async XLA Ops:
  0.6 4.3 %copy-start = (bf16[512,1024]{1,0:T(8,128)(2,1)S(1)}, bf16[512,1024]{1,0:T(8,128)(2,1)}, u32[]{:S(2)}) copy-start(bf16[512,1024]{1,0:T(8,128)(2,1)} %query_ref.1) | copy-start | bytes 3145732
  0.6 17.5 %copy-start.1 = (s32[1024]{0:T(1024)S(1)}, s32[1024]{0:T(1024)}, u32[]{:S(2)}) copy-start(s32[1024]{0:T(1024)} %param.15) | copy-start | bytes 12292
  0.7 17.5 %copy-start.2 = (s32[4,1]{0,1:T(1,128)S(1)}, s32[4,1]{0,1:T(1,128)}, u32[]{:S(2)}) copy-start(s32[4,1]{0,1:T(1,128)} %param.13) | copy-start | bytes 52
  4.9 13.3 %collective-permute-start = (bf16[512,1024]{1,0:T(8,128)(2,1)S(1)}, bf16[512,1024]{1,0:T(8,128)(2,1)S(1)}, u32[]{:S(2)}, u32[]{:S(2)}) collective-permute-start(bf16[512,1024]{1,0:T(8,128)(2,1)S(1)} %copy-done), channel_id=1, source_target_pairs={{0,1},{1,0},{2,3},{3,2},{4,5},{5,4},{6,7},{7,6},{8,9},{9,8},{10,11... | collective-permute-start | bytes 3145736 | tf_op jit(solution)/shard_map/ppermute | solution.py:17
  5.4 3.0 %collective-permute-start.1 = (bf16[1,4,8,128]{3,2,1,0:T(8,128)(2,1)S(1)}, bf16[1,4,8,128]{3,2,1,0:T(8,128)(2,1)S(1)}, u32[]{:S(2)}, u32[]{:S(2)}) collective-permute-start(bf16[1,4,8,128]{3,2,1,0:T(8,128)(2,1)S(1)} %bitcast.36), channel_id=1, source_target_pairs={{0,1},{1,0},{2,3},{3,2},{4,5},{5,4},{6,7},{7,6},{8,9},{9,8},{10,11... | collective-permute-start | bytes 24584 | tf_op jit(solution)/shard_map/ppermute | solution.py:17
  5.5 4.5 %collective-permute-start.2 = (bf16[1,4,8,128]{3,2,1,0:T(8,128)(2,1)S(1)}, bf16[1,4,8,128]{3,2,1,0:T(8,128)(2,1)S(1)}, u32[]{:S(2)}, u32[]{:S(2)}) collective-permute-start(bf16[1,4,8,128]{3,2,1,0:T(8,128)(2,1)S(1)} %bitcast.37), channel_id=1, source_target_pairs={{0,2},{1,3},{2,0},{3,1},{4,6},{5,7},{6,4},{7,5},{8,10},{9,11},{10,... | collective-permute-start | bytes 24584 | tf_op jit(solution)/shard_map/ppermute | solution.py:17
  8.4 3.1 %collective-permute-start.3 = (bf16[1,4,8,128]{3,2,1,0:T(8,128)(2,1)S(1)}, bf16[1,4,8,128]{3,2,1,0:T(8,128)(2,1)S(1)}, u32[]{:S(2)}, u32[]{:S(2)}) collective-permute-start(bf16[1,4,8,128]{3,2,1,0:T(8,128)(2,1)S(1)} %bitcast.38), channel_id=1, source_target_pairs={{0,3},{1,2},{2,1},{3,0},{4,7},{5,6},{6,5},{7,4},{8,11},{9,10},{10,... | collective-permute-start | bytes 24584 | tf_op jit(solution)/shard_map/ppermute | solution.py:17
  11.6 4.2 %collective-permute-start.4 = (bf16[3,4,8,128]{3,2,1,0:T(8,128)(2,1)S(1)}, bf16[3,4,8,128]{3,2,1,0:T(8,128)(2,1)S(1)}, u32[]{:S(2)}, u32[]{:S(2)}) collective-permute-start(bf16[3,4,8,128]{3,2,1,0:T(8,128)(2,1)S(1)} %pad_maximum_fusion.1), channel_id=1, source_target_pairs={{0,4},{1,9},{4,0},{5,13},{8,12},{9,1},{12,8},{13,5},{2,6},{3,11},{... | collective-permute-start | bytes 73736 | tf_op jit(solution)/shard_map/ppermute | solution.py:68
  13.2 5.0 %collective-permute-start.6 = (bf16[2,4,8,128]{3,2,1,0:T(8,128)(2,1)S(1)}, bf16[2,4,8,128]{3,2,1,0:T(8,128)(2,1)S(1)}, u32[]{:S(2)}, u32[]{:S(2)}) collective-permute-start(bf16[2,4,8,128]{3,2,1,0:T(8,128)(2,1)S(1)} %pad_maximum_fusion.2), channel_id=1, source_target_pairs={{0,13},{1,12},{4,9},{5,8},{8,5},{9,4},{12,1},{13,0},{2,15},{3,14},... | collective-permute-start | bytes 49160 | tf_op jit(solution)/shard_map/ppermute | solution.py:68
  15.7 2.5 %collective-permute-start.5 = (bf16[2,4,8,128]{3,2,1,0:T(8,128)(2,1)S(1)}, bf16[2,4,8,128]{3,2,1,0:T(8,128)(2,1)S(1)}, u32[]{:S(2)}, u32[]{:S(2)}) collective-permute-start(bf16[2,4,8,128]{3,2,1,0:T(8,128)(2,1)S(1)} %slice.4), channel_id=1, source_target_pairs={{0,1},{1,0},{2,3},{3,2},{4,5},{5,4},{6,7},{7,6},{8,9},{9,8},{10,11... | collective-permute-start | bytes 49160 | tf_op jit(solution)/shard_map/ppermute | solution.py:17
  18.7 4.4 %collective-permute-start.7 = (f32[8,256]{1,0:T(8,128)S(1)}, f32[8,256]{1,0:T(8,128)S(1)}, u32[]{:S(2)}, u32[]{:S(2)}) collective-permute-start(f32[8,256]{1,0:T(8,128)S(1)} %get-tuple-element.19), channel_id=1, source_target_pairs={{0,4},{1,9},{4,0},{5,13},{8,12},{9,1},{12,8},{13,5},{2,6},{3,11},{... | collective-permute-start | bytes 24584 | tf_op jit(solution)/shard_map/ppermute | solution.py:262
  18.9 4.3 %collective-permute-start.8 = (f32[8,256]{1,0:T(8,128)S(1)}, f32[8,256]{1,0:T(8,128)S(1)}, u32[]{:S(2)}, u32[]{:S(2)}) collective-permute-start(f32[8,256]{1,0:T(8,128)S(1)} %get-tuple-element.20), channel_id=1, source_target_pairs={{0,4},{1,13},{4,0},{5,9},{8,12},{9,5},{12,8},{13,1},{2,6},{3,15},{... | collective-permute-start | bytes 24584 | tf_op jit(solution)/shard_map/ppermute | solution.py:262
  23.2 1.7 %collective-permute-start.9 = (f32[4,256]{1,0:T(4,128)S(1)}, f32[4,256]{1,0:T(4,128)S(1)}, u32[]{:S(2)}, u32[]{:S(2)}) collective-permute-start(f32[4,256]{1,0:T(4,128)S(1)} %dynamic-slice_bitcast_fusion.4), channel_id=1, source_target_pairs={{0,1},{1,0},{2,3},{3,2},{4,5},{5,4},{6,7},{7,6},{8,9},{9,8},{10,11... | collective-permute-start | bytes 12296 | tf_op jit(solution)/shard_map/ppermute | solution.py:17

commit v7 on v6

--- a/solution.py
+++ b/solution.py
@@ -17,14 +17,17 @@
     return lax.ppermute(block, axis, [(i, i ^ step) for i in range(lax.axis_size(axis))])
 
 
-def project_kernel(acts_hbm, grads_hbm, act_proj_hbm, grad_proj_hbm, act_low_ref, grad_low_ref, acts, grads, act_proj, grad_proj, sems):
+def project_kernel(
+    acts_hbm, grads_hbm, act_proj_hbm, grad_proj_hbm, act_low_ref, grad_low_ref,
+    acts, grads, act_proj, grad_proj, sems,
+):
     sources = (act_proj_hbm, acts_hbm, grad_proj_hbm, grads_hbm)
     targets = (act_proj, acts, grad_proj, grads)
     copies = [
         pltpu.make_async_copy(s, t, sems.at[i]) for i, (s, t) in enumerate(zip(sources, targets))
     ]
-    for copy in copies:
-        copy.start()
+    for copy, priority in zip(copies, (0, 0, 1, 0)):
+        copy.start(priority=priority)
     for copy in copies[:2]:
         copy.wait()
     act_sum = lax.dot_general(acts[...], act_proj[...], NT, preferred_element_type=jnp.float32)
@@ -36,8 +39,7 @@
 
 
 def make_sketch(acts, grads, act_proj, grad_proj, tok_count):
-    seq_len, width = acts.shape
-    hidden, rank = grad_proj.shape
+    seq_len, rank = acts.shape[0], act_proj.shape[1]
     operands = (acts, grads, act_proj.T, grad_proj.T)
     act_low, grad_low = pl.pallas_call(
         project_kernel,
@@ -81,10 +83,14 @@
     ex, feat, pb = (lax.axis_index(axis) for axis in ("ex", "feat", "pb"))
     fp_count, fp = feat_count * pb_count, feat * pb_count + pb
     ratio = ex_count // fp_count
-    sketch, queries = lax.optimization_barrier((sketch, queries))
     own = sketch.reshape(1, ex_count, -1, LANES)
+    own = jnp.concatenate([own, exchange(own, "pb", 1)])
+    own, queries = lax.optimization_barrier((own, queries))
     others = exchange(queries, "pb", 1)
-    block = jnp.concatenate([own] + [exchange(own, ("feat", "pb"), s) for s in range(1, fp_count)])
+    line = [own]
+    for k in range(1, feat_count):
+        line.append(exchange(own, ("feat", "pb"), k * pb_count + 1)[::-1])
+    block = jnp.concatenate(line)
     by_fp = block.reshape(fp_count, fp_count, ratio, -1, LANES)
 
     def columns(index):
@@ -129,34 +135,36 @@
     pieces, refs = refs[: len(origins)], refs[len(origins) :]
     half = ex_count // pb_count
     outs = refs[:half]
-    own_ref, open_ref, rows, scaled, chunks, products = refs[-6:]
+    own_ref, open_ref, rows, scaled, chunks = refs[-5:]
     ex, feat = lax.axis_index("ex"), lax.axis_index("feat")
     near = lax.axis_index("pb") == 0
     here = lax.rem(ex, half)
     examples, block_lines, lanes = rows.shape
     mine = ex_count * pb_count
-    place_rows(sizes, origins, pieces, rows)
-    diag = jnp.sum(rows[...] * rows[...], axis=0) / examples
-    weight = 1.0 / (math.sqrt(ex_count * block_lines * lanes) * (diag + DAMPING))
-    own = rows[pl.ds(feat * mine, mine)]
-    scaled[...] = (own * weight[None]).reshape(mine * block_lines, lanes)
-    parts = [scaled[pl.ds(j, mine, stride=block_lines), :] for j in range(block_lines)]
-    wide = jnp.concatenate(parts, axis=1)
-    high = wide.astype(jnp.bfloat16)
-    low = (wide - high.astype(jnp.float32)).astype(jnp.bfloat16)
-    both = jnp.concatenate([high, low], axis=0)
+    width = chunks.shape[2]
     for side, queries in enumerate((query_ref, other_query_ref)):
 
         @pl.when(lax.div(ex, half) == side)
         def _():
-            products[...] = lax.dot_general(
+            place_rows(sizes, origins, pieces, rows)
+            diag = jnp.sum(rows[...] * rows[...], axis=0) / examples
+            weight = 1.0 / (math.sqrt(ex_count * block_lines * lanes) * (diag + DAMPING))
+            own = rows[pl.ds(feat * mine, mine)]
+            scaled[pl.ds(0, mine * block_lines), :] = (own * weight[None]).reshape(
+                mine * block_lines, lanes
+            )
+            parts = [scaled[pl.ds(j, mine, stride=block_lines), :] for j in range(block_lines)]
+            wide = jnp.concatenate(parts, axis=1)
+            high = wide.astype(jnp.bfloat16)
+            low = (wide - high.astype(jnp.float32)).astype(jnp.bfloat16)
+            both = jnp.concatenate([high, low], axis=0)
+            products = lax.dot_general(
                 both, queries[...], NT, preferred_element_type=jnp.float32
             )
-
-    result = products[:mine, :] + products[mine:, :]
-    width = chunks.shape[2]
-    for t in range(half):
-        chunks[t] = result[:, t * width : (t + 1) * width]
+            result = products[:mine] + products[mine:]
+            for t in range(half):
+                chunks[t] = result[:, t * width : (t + 1) * width]
+
     shift = near.astype(jnp.int32)
     for i in range(half - 1):
         outs[i][...] = chunks[here ^ (i + shift)]
@@ -165,9 +173,8 @@
     spans = chunks.shape[2] // query_ids_ref.shape[1]
     ids = [query_ids_ref[pl.ds(ex * spans + i, 1), :] for i in range(spans)]
     ids = jnp.concatenate(ids, axis=1)
-    open_ref[...] = jnp.concatenate(
-        [jnp.where(example_ids_ref[:, a : a + 1] == ids, 0.0, 1.0) for a in range(ex_count)]
-    )
+    for a in range(ex_count):
+        open_ref[a] = jnp.where(example_ids_ref[:, a : a + 1] == ids, 0.0, 1.0)
 
 
 def partial_scores(sizes, queries, other_queries, query_ids, example_ids, pieces):
@@ -180,14 +187,13 @@
     return pl.pallas_call(
         functools.partial(score_kernel, sizes, [piece[1:] for piece in pieces]),
         out_shape=[jax.ShapeDtypeStruct(chunk, jnp.float32)] * (half + 1)
-        + [jax.ShapeDtypeStruct((ex_count, chunk[1]), jnp.float32)],
+        + [jax.ShapeDtypeStruct((ex_count, 1, chunk[1]), jnp.float32)],
         in_specs=[vmem] * (4 + len(pieces)),
         out_specs=[vmem] * (half + 2),
         scratch_shapes=[
             pltpu.VMEM((examples, lines, lanes), jnp.float32),
-            pltpu.VMEM((pb_count * ex_count * lines, lanes), jnp.float32),
+            pltpu.VMEM(((pb_count * ex_count + 1) * lines, lanes), jnp.float32),
             pltpu.VMEM((half, *chunk), jnp.float32),
-            pltpu.VMEM((2 * chunk[0], queries.shape[0]), jnp.float32),
         ],
         compiler_params=pltpu.CompilerParams(vmem_limit_bytes=24 * 2**20),
         name="scores",
@@ -201,8 +207,9 @@
     examples, left_lines, lanes = left_rows.shape
     right_lines = right_rows.shape[1]
     place_rows(sizes, origins, pieces, left_rows, right_rows)
-    left[...] = left_rows[...].reshape(examples * left_lines, lanes)
-    right[...] = right_rows[...].reshape(examples * right_lines, lanes)
+    for rows, flat in ((left_rows, left), (right_rows, right)):
+        lines = examples * rows.shape[1]
+        flat[pl.ds(0, lines), :] = rows[...].reshape(lines, lanes)
     across = jnp.concatenate(
         [right[pl.ds(j, examples, stride=right_lines), :] for j in range(right_lines)], axis=1
     ).astype(jnp.bfloat16)
@@ -236,8 +243,8 @@
         scratch_shapes=[
             pltpu.VMEM((examples, left_lines, LANES), jnp.float32),
             pltpu.VMEM((examples, right_lines, LANES), jnp.float32),
-            pltpu.VMEM((examples * left_lines, LANES), jnp.float32),
-            pltpu.VMEM((examples * right_lines, LANES), jnp.float32),
+            pltpu.VMEM(((examples + 1) * left_lines, LANES), jnp.float32),
+            pltpu.VMEM(((examples + 1) * right_lines, LANES), jnp.float32),
             pltpu.VMEM(shape, jnp.float32),
             pltpu.SemaphoreType.DMA((left_lines,)),
         ],
@@ -279,12 +286,12 @@
     )
     part = to_owners(chunks, ex_count)
     gram, own = make_gram(sizes, pieces, own)
-    part = (part + own).reshape(pb_count, ex_count, -1)
+    part = (part + own).reshape(pb_count, ex_count, 1, -1)
     pb = lax.axis_index("pb")
     theirs = lax.dynamic_index_in_dim(part, 1 - pb, 0, keepdims=False)
     total = lax.dynamic_index_in_dim(part, pb, 0, keepdims=False) + exchange(theirs, "pb", 1)
     scores = jnp.where(is_open == 0.0, jnp.float32(0.0), total)
-    return gram, scores.T[:, :, None]
+    return gram, scores.transpose(2, 0, 1)
 
 
 def solution(mesh):

time: 25.7 us -> 25.1 us (0.977)
  waiting for transfers between devices: 7.04 us -> 5.48 us
  starting transfers between devices: 9.93 us -> 11.1 us
  other arithmetic: 0.03 us -> 0.64 us
  local copies, waits for them, and re-layouts: 0.74 us -> 0.13 us
    ppermute x6 -> x5, waiting for transfers between devices: 3.97 us -> 3.1 us  [exchange(): lax.ppermute(block, axis, [(i, i ^ step) for i in range(lax.axis_size(axi...]
    ppermute x2, waiting for transfers between devices: 3.06 us -> 2.37 us  [spread(): return lax.ppermute(block, ('ex', 'pb'), pairs)]
    transpose x0 -> x1, other arithmetic: none -> 0.6 us  [shards(): return (gram, scores.transpose(2, 0, 1))]
    unnamed x7 -> x6, local copies, waits for them, and re-layouts: 0.61 us -> 0.01 us
    ppermute x6 -> x5, starting transfers between devices: 4.44 us -> 5 us  [exchange(): lax.ppermute(block, axis, [(i, i ^ step) for i in range(lax.axis_size(axi...]
    ppermute x2, starting transfers between devices: 3.45 us -> 3.98 us  [spread(): return lax.ppermute(block, ('ex', 'pb'), pairs)]
  transfers between devices with their start and end apart: 10 -> 9, of which waited for: 5 -> 4; matrix products, arithmetic and copies ran while one was open for 0% -> 0% of each run, Pallas kernels for 9% -> 9%
where the time goes in v7:
time: 25.1 us; the launch traced here: 25 us
  starting transfers between devices  11.1 us (44%)
  Pallas kernels  6.05 us (24%)
  waiting for transfers between devices  5.48 us (22%)
  between operations  1.48 us (6%)
  other arithmetic  0.64 us (3%)
    ppermute x5, starting transfers between devices, exchange(): lax.ppermute(block, axis, [(i, i ^ step) for i in range(lax.axis_size(axi...  5 us
    ppermute x2, starting transfers between devices, spread(): return lax.ppermute(block, ('ex', 'pb'), pairs)  3.98 us
    pallas_call x1, Pallas kernels, make_sketch(): pl.pallas_call(project_kernel, out_shape=[jax.ShapeDtypeStruct((seq_len,...  3.19 us
    ppermute x5, waiting for transfers between devices, exchange(): lax.ppermute(block, axis, [(i, i ^ step) for i in range(lax.axis_size(axi...  3.1 us
    pallas_call x1, Pallas kernels, make_gram(): pl.pallas_call(functools.partial(gram_kernel, sizes, [piece[1:] for piece...  2.37 us
    ppermute x2, waiting for transfers between devices, spread(): return lax.ppermute(block, ('ex', 'pb'), pairs)  2.37 us
    ppermute x2, starting transfers between devices, to_owners(): arrived.append(lax.ppermute(chunk, ('ex', 'pb'), pairs))  2.08 us
    transpose x1, other arithmetic, shards(): return (gram, scores.transpose(2, 0, 1))  0.6 us
  transfers between devices with their start and end apart: 9, of which 4 were waited for; matrix products, arithmetic and copies ran while one was open for 0% of the time, Pallas kernels for 9%

profile of v7, /device:TPU:0, one launch (start us, length us, event | category | flops | bytes accessed | tf_op | source)
XLA Modules:
  0.0 25.0 jit_solution(9286411150307046977)
XLA Ops:
  0.6 0.0 copy-start
  0.6 0.0 copy-start.1
  0.7 0.0 copy-start.2
  1.4 3.2 %project.1 = (bf16[128,64]{1,0:T(8,128)(2,1)S(1)}, bf16[64,128]{1,0:T(8,128)(2,1)S(1)}) custom-call(bf16[128,4096]{1,0:T(8,128)(2,1)} %bitcast.25, bf16[128,7168]{1,0:T(8,128)(2,1)} %bitcast.24, bf16[64,4096]{1,0:T(8,128)(2,1)} %bitcast.27, bf16[64,7168]{1,0:T(8,128)(2,1)} %bitcast.26), custom_call_target="tpu_custom_call" | custom-call | tf_op jit(solution)/shard_map/project/pallas_call | solution.py:44
  4.6 0.1 fusion
  4.7 0.1 reshape_reshape.3
  4.8 0.5 %collective-permute-start = (bf16[1,4,8,128]{3,2,1,0:T(8,128)(2,1)S(1)}, bf16[1,4,8,128]{3,2,1,0:T(8,128)(2,1)S(1)}, u32[]{:S(2)}, u32[]{:S(2)}) collective-permute-start(bf16[1,4,8,128]{3,2,1,0:T(8,128)(2,1)S(1)} %reshape_reshape.3), channel_id=1, source_target_pairs={{0,1},{1,0},{2,3},{3,2},{4,5},{5,4},{6,7},{7,6},{8,9},{9,8},{10,11... | collective-permute-start | bytes 24584 | tf_op jit(solution)/shard_map/ppermute | solution.py:17
  5.3 0.8 %collective-permute-done = bf16[1,4,8,128]{3,2,1,0:T(8,128)(2,1)S(1)} collective-permute-done((bf16[1,4,8,128]{3,2,1,0:T(8,128)(2,1)S(1)}, bf16[1,4,8,128]{3,2,1,0:T(8,128)(2,1)S(1)}, u32[]{:S(2)}, u32[]{:S(2)}) %collective-permute-start) | collective-permute-done | bytes 8224 | tf_op jit(solution)/shard_map/ppermute | solution.py:17
  6.1 0.0 copy-done
  6.1 0.3 %collective-permute-start.1 = (bf16[512,1024]{1,0:T(8,128)(2,1)S(1)}, bf16[512,1024]{1,0:T(8,128)(2,1)S(1)}, u32[]{:S(2)}, u32[]{:S(2)}) collective-permute-start(bf16[512,1024]{1,0:T(8,128)(2,1)S(1)} %copy-done), channel_id=1, source_target_pairs={{0,1},{1,0},{2,3},{3,2},{4,5},{5,4},{6,7},{7,6},{8,9},{9,8},{10,11... | collective-permute-start | bytes 3145736 | tf_op jit(solution)/shard_map/ppermute | solution.py:17
  6.5 2.6 %collective-permute-start.2 = (bf16[2,4,8,128]{3,2,1,0:T(8,128)(2,1)S(1)}, bf16[2,4,8,128]{3,2,1,0:T(8,128)(2,1)S(1)}, u32[]{:S(2)}, u32[]{:S(2)}) collective-permute-start(bf16[2,4,8,128]{3,2,1,0:T(8,128)(2,1)S(1)} %pad_maximum_fusion.2), channel_id=1, source_target_pairs={{0,3},{1,2},{2,1},{3,0},{4,7},{5,6},{6,5},{7,4},{8,11},{9,10},{10,... | collective-permute-start | bytes 49160 | tf_op jit(solution)/shard_map/ppermute | solution.py:17
  9.1 1.4 %collective-permute-done.2 = bf16[2,4,8,128]{3,2,1,0:T(8,128)(2,1)S(1)} collective-permute-done((bf16[2,4,8,128]{3,2,1,0:T(8,128)(2,1)S(1)}, bf16[2,4,8,128]{3,2,1,0:T(8,128)(2,1)S(1)}, u32[]{:S(2)}, u32[]{:S(2)}) %collective-permute-start.2) | collective-permute-done | bytes 16416 | tf_op jit(solution)/shard_map/ppermute | solution.py:17
  10.5 1.9 %collective-permute-start.3 = (bf16[3,4,8,128]{3,2,1,0:T(8,128)(2,1)S(1)}, bf16[3,4,8,128]{3,2,1,0:T(8,128)(2,1)S(1)}, u32[]{:S(2)}, u32[]{:S(2)}) collective-permute-start(bf16[3,4,8,128]{3,2,1,0:T(8,128)(2,1)S(1)} %pad_maximum_fusion.1), channel_id=1, source_target_pairs={{0,4},{1,9},{4,0},{5,13},{8,12},{9,1},{12,8},{13,5},{2,6},{3,11},{... | collective-permute-start | bytes 73736 | tf_op jit(solution)/shard_map/ppermute | solution.py:70
  12.5 2.1 %collective-permute-start.5 = (bf16[2,4,8,128]{3,2,1,0:T(8,128)(2,1)S(1)}, bf16[2,4,8,128]{3,2,1,0:T(8,128)(2,1)S(1)}, u32[]{:S(2)}, u32[]{:S(2)}) collective-permute-start(bf16[2,4,8,128]{3,2,1,0:T(8,128)(2,1)S(1)} %pad_maximum_fusion.3), channel_id=1, source_target_pairs={{0,13},{1,12},{4,9},{5,8},{8,5},{9,4},{12,1},{13,0},{2,15},{3,14},... | collective-permute-start | bytes 49160 | tf_op jit(solution)/shard_map/ppermute | solution.py:70
  14.5 0.0 collective-permute-done.3.refs_1_
  14.5 0.5 %collective-permute-start.4 = (bf16[2,4,8,128]{3,2,1,0:T(8,128)(2,1)S(1)}, bf16[2,4,8,128]{3,2,1,0:T(8,128)(2,1)S(1)}, u32[]{:S(2)}, u32[]{:S(2)}) collective-permute-start(bf16[2,4,8,128]{3,2,1,0:T(8,128)(2,1)S(1)} %slice.4), channel_id=1, source_target_pairs={{0,1},{1,0},{2,3},{3,2},{4,5},{5,4},{6,7},{7,6},{8,9},{9,8},{10,11... | collective-permute-start | bytes 49160 | tf_op jit(solution)/shard_map/ppermute | solution.py:17
  15.1 2.4 %collective-permute-done.5.refs_3_ = bf16[2,4,8,128]{3,2,1,0:T(8,128)(2,1)S(1)} collective-permute-done((bf16[2,4,8,128]{3,2,1,0:T(8,128)(2,1)S(1)}, bf16[2,4,8,128]{3,2,1,0:T(8,128)(2,1)S(1)}, u32[]{:S(2)}, u32[]{:S(2)}) %collective-permute-start.5) | collective-permute-done | bytes 16416 | tf_op jit(solution)/shard_map/ppermute | solution.py:70
  17.4 0.0 collective-permute-done.4.refs_2_
  17.4 0.0 collective-permute-done.1.other_query_ref
  17.4 0.0 copy-done.1
  17.4 0.0 copy-done.2
  17.4 0.5 %scores.1 = (f32[8,256]{1,0:T(8,128)S(1)}, f32[8,256]{1,0:T(8,128)S(1)}, f32[8,256]{1,0:T(8,128)S(1)}, f32[4,1,256]{2,1,0:T(1,128)S(1)}) custom-call(bf16[512,1024]{1,0:T(8,128)(2,1)S(1)} %copy-done, bf16[512,1024]{1,0:T(8,128)(2,1)S(1)} %collective-permute-done.1.other_query_ref, s32[8,128]{1,0:T(8,128)S(1)} %bitcast.22, s32[1,4]{1,0:T(1,128)S(1)} %bitcast.23, ...), custom_call_target="tpu_custom_call" | custom-call | tf_op jit(solution)/shard_map/scores/pallas_call | solution.py:187
  17.9 0.1 collective-permute-start.6
  18.0 2.0 %collective-permute-start.7 = (f32[8,256]{1,0:T(8,128)S(1)}, f32[8,256]{1,0:T(8,128)S(1)}, u32[]{:S(2)}, u32[]{:S(2)}) collective-permute-start(f32[8,256]{1,0:T(8,128)S(1)} %get-tuple-element.20), channel_id=1, source_target_pairs={{0,4},{1,13},{4,0},{5,9},{8,12},{9,5},{12,8},{13,1},{2,6},{3,15},{... | collective-permute-start | bytes 24584 | tf_op jit(solution)/shard_map/ppermute | solution.py:269
  20.0 2.4 %gram.1 = (f32[1024,1024]{1,0:T(8,128)}, f32[8,256]{1,0:T(8,128)S(1)}) custom-call(f32[8,256]{1,0:T(8,128)S(1)} %get-tuple-element.16.kept_ref, bf16[4,4,8,128]{3,2,1,0:T(8,128)(2,1)S(1)} %pad_maximum_fusion.refs_0_, bf16[3,4,8,128]{3,2,1,0:T(8,128)(2,1)S(1)} %collective-permute-done.3.refs_1_, bf16[2,4,8,128]{3,2,1,0:T(8,128)(2,1)S(1)} %collective-permute-done.4.refs_2_, ...), custom_call_target="tpu_custom_call" | custom-call | flops 536870912 | bytes 4194304 | tf_op jit(solution)/shard_map/gram/pallas_call | solution.py:235
  22.4 0.0 collective-permute-done.6
  22.4 0.0 collective-permute-done.7
  22.5 1.1 %collective-permute-start.8 = (f32[4,1,256]{2,1,0:T(1,128)S(1)}, f32[4,1,256]{2,1,0:T(1,128)S(1)}, u32[]{:S(2)}, u32[]{:S(2)}) collective-permute-start(f32[4,1,256]{2,1,0:T(1,128)S(1)} %squeeze.27), channel_id=1, source_target_pairs={{0,1},{1,0},{2,3},{3,2},{4,5},{5,4},{6,7},{7,6},{8,9},{9,8},{10,11... | collective-permute-start | bytes 12296 | tf_op jit(solution)/shard_map/ppermute | solution.py:17
  23.5 0.8 %collective-permute-done.8 = f32[4,1,256]{2,1,0:T(1,128)S(1)} collective-permute-done((f32[4,1,256]{2,1,0:T(1,128)S(1)}, f32[4,1,256]{2,1,0:T(1,128)S(1)}, u32[]{:S(2)}, u32[]{:S(2)}) %collective-permute-start.8) | collective-permute-done | bytes 4128 | tf_op jit(solution)/shard_map/ppermute | solution.py:17
  24.4 0.6 %fusion.11 = f32[256,4,1]{0,2,1:T(1,128)} fusion(f32[4,1,256]{2,1,0:T(1,128)S(1)} %get-tuple-element.18, f32[4,1,256]{2,1,0:T(1,128)S(1)} %collective-permute-done.8, f32[1,4,1,256]{3,1,0,2:T(4,128)S(1)} %get-tuple-element.26), kind=kLoop, calls=%fused_computation.26 | loop fusion | flops 3072 | bytes 16384 | tf_op jit(solution)/shard_map/transpose | solution.py:294
  (12 shorter events, 0.1 us)
Async XLA Ops:
  0.6 5.5 %copy-start = (bf16[512,1024]{1,0:T(8,128)(2,1)S(1)}, bf16[512,1024]{1,0:T(8,128)(2,1)}, u32[]{:S(2)}) copy-start(bf16[512,1024]{1,0:T(8,128)(2,1)} %query_ref.1) | copy-start | bytes 3145732
  0.6 16.8 %copy-start.1 = (s32[1024]{0:T(1024)S(1)}, s32[1024]{0:T(1024)}, u32[]{:S(2)}) copy-start(s32[1024]{0:T(1024)} %param.15) | copy-start | bytes 12292
  0.7 16.8 %copy-start.2 = (s32[4,1]{0,1:T(1,128)S(1)}, s32[4,1]{0,1:T(1,128)}, u32[]{:S(2)}) copy-start(s32[4,1]{0,1:T(1,128)} %param.13) | copy-start | bytes 52
  4.8 1.3 %collective-permute-start = (bf16[1,4,8,128]{3,2,1,0:T(8,128)(2,1)S(1)}, bf16[1,4,8,128]{3,2,1,0:T(8,128)(2,1)S(1)}, u32[]{:S(2)}, u32[]{:S(2)}) collective-permute-start(bf16[1,4,8,128]{3,2,1,0:T(8,128)(2,1)S(1)} %reshape_reshape.3), channel_id=1, source_target_pairs={{0,1},{1,0},{2,3},{3,2},{4,5},{5,4},{6,7},{7,6},{8,9},{9,8},{10,11... | collective-permute-start | bytes 24584 | tf_op jit(solution)/shard_map/ppermute | solution.py:17
  6.1 11.3 %collective-permute-start.1 = (bf16[512,1024]{1,0:T(8,128)(2,1)S(1)}, bf16[512,1024]{1,0:T(8,128)(2,1)S(1)}, u32[]{:S(2)}, u32[]{:S(2)}) collective-permute-start(bf16[512,1024]{1,0:T(8,128)(2,1)S(1)} %copy-done), channel_id=1, source_target_pairs={{0,1},{1,0},{2,3},{3,2},{4,5},{5,4},{6,7},{7,6},{8,9},{9,8},{10,11... | collective-permute-start | bytes 3145736 | tf_op jit(solution)/shard_map/ppermute | solution.py:17
  6.5 4.0 %collective-permute-start.2 = (bf16[2,4,8,128]{3,2,1,0:T(8,128)(2,1)S(1)}, bf16[2,4,8,128]{3,2,1,0:T(8,128)(2,1)S(1)}, u32[]{:S(2)}, u32[]{:S(2)}) collective-permute-start(bf16[2,4,8,128]{3,2,1,0:T(8,128)(2,1)S(1)} %pad_maximum_fusion.2), channel_id=1, source_target_pairs={{0,3},{1,2},{2,1},{3,0},{4,7},{5,6},{6,5},{7,4},{8,11},{9,10},{10,... | collective-permute-start | bytes 49160 | tf_op jit(solution)/shard_map/ppermute | solution.py:17
  10.5 4.0 %collective-permute-start.3 = (bf16[3,4,8,128]{3,2,1,0:T(8,128)(2,1)S(1)}, bf16[3,4,8,128]{3,2,1,0:T(8,128)(2,1)S(1)}, u32[]{:S(2)}, u32[]{:S(2)}) collective-permute-start(bf16[3,4,8,128]{3,2,1,0:T(8,128)(2,1)S(1)} %pad_maximum_fusion.1), channel_id=1, source_target_pairs={{0,4},{1,9},{4,0},{5,13},{8,12},{9,1},{12,8},{13,5},{2,6},{3,11},{... | collective-permute-start | bytes 73736 | tf_op jit(solution)/shard_map/ppermute | solution.py:70
  12.5 5.0 %collective-permute-start.5 = (bf16[2,4,8,128]{3,2,1,0:T(8,128)(2,1)S(1)}, bf16[2,4,8,128]{3,2,1,0:T(8,128)(2,1)S(1)}, u32[]{:S(2)}, u32[]{:S(2)}) collective-permute-start(bf16[2,4,8,128]{3,2,1,0:T(8,128)(2,1)S(1)} %pad_maximum_fusion.3), channel_id=1, source_target_pairs={{0,13},{1,12},{4,9},{5,8},{8,5},{9,4},{12,1},{13,0},{2,15},{3,14},... | collective-permute-start | bytes 49160 | tf_op jit(solution)/shard_map/ppermute | solution.py:70
  14.5 2.9 %collective-permute-start.4 = (bf16[2,4,8,128]{3,2,1,0:T(8,128)(2,1)S(1)}, bf16[2,4,8,128]{3,2,1,0:T(8,128)(2,1)S(1)}, u32[]{:S(2)}, u32[]{:S(2)}) collective-permute-start(bf16[2,4,8,128]{3,2,1,0:T(8,128)(2,1)S(1)} %slice.4), channel_id=1, source_target_pairs={{0,1},{1,0},{2,3},{3,2},{4,5},{5,4},{6,7},{7,6},{8,9},{9,8},{10,11... | collective-permute-start | bytes 49160 | tf_op jit(solution)/shard_map/ppermute | solution.py:17
  17.9 4.5 %collective-permute-start.6 = (f32[8,256]{1,0:T(8,128)S(1)}, f32[8,256]{1,0:T(8,128)S(1)}, u32[]{:S(2)}, u32[]{:S(2)}) collective-permute-start(f32[8,256]{1,0:T(8,128)S(1)} %get-tuple-element.19), channel_id=1, source_target_pairs={{0,4},{1,9},{4,0},{5,13},{8,12},{9,1},{12,8},{13,5},{2,6},{3,11},{... | collective-permute-start | bytes 24584 | tf_op jit(solution)/shard_map/ppermute | solution.py:269
  18.0 4.4 %collective-permute-start.7 = (f32[8,256]{1,0:T(8,128)S(1)}, f32[8,256]{1,0:T(8,128)S(1)}, u32[]{:S(2)}, u32[]{:S(2)}) collective-permute-start(f32[8,256]{1,0:T(8,128)S(1)} %get-tuple-element.20), channel_id=1, source_target_pairs={{0,4},{1,13},{4,0},{5,9},{8,12},{9,5},{12,8},{13,1},{2,6},{3,15},{... | collective-permute-start | bytes 24584 | tf_op jit(solution)/shard_map/ppermute | solution.py:269
  22.5 1.9 %collective-permute-start.8 = (f32[4,1,256]{2,1,0:T(1,128)S(1)}, f32[4,1,256]{2,1,0:T(1,128)S(1)}, u32[]{:S(2)}, u32[]{:S(2)}) collective-permute-start(f32[4,1,256]{2,1,0:T(1,128)S(1)} %squeeze.27), channel_id=1, source_target_pairs={{0,1},{1,0},{2,3},{3,2},{4,5},{5,4},{6,7},{7,6},{8,9},{9,8},{10,11... | collective-permute-start | bytes 12296 | tf_op jit(solution)/shard_map/ppermute | solution.py:17

commit v8 on v7

--- a/solution.py
+++ b/solution.py
@@ -61,9 +61,8 @@
 
 
 def spread(block, distances):
-    crossed = int(distances[0] == distances[1])
     pairs = [
-        (e * len(distances) + p, (e ^ k) * len(distances) + (p ^ crossed))
+        (e * len(distances) + p, (e ^ k) * len(distances) + p)
         for e in range(lax.axis_size("ex"))
         for p, k in enumerate(distances)
     ]
@@ -96,16 +95,17 @@
     def columns(index):
         return jnp.moveaxis(take(by_fp, index), 1, 0)
 
-    pieces = [(block, (0, 0), 0)]
+    pieces = [(block, (0, 0), 0, None)]
     for near, far in pairs_of_distances(ex_count):
         theirs = take(block, ex ^ (near + (far - near) * pb))[None]
-        for_other = jnp.concatenate([theirs, columns(fp ^ 1)])
         if near == far:
-            pieces.append((spread(for_other, (near, far)), (near, far), 1))
+            rows = spread(jnp.concatenate([theirs, columns(fp)]), (near, far))
+            pieces.append((rows, (near, far), 0, 0))
         else:
-            both = spread(jnp.concatenate([columns(fp), for_other]), (near, far))
-            pieces.append((both, (near, far), 0))
-            pieces.append((exchange(both[ratio:], "pb", 1), (far, near), 1))
+            rows = jnp.concatenate([columns(fp), theirs, columns(fp ^ 1)])
+            rows = spread(rows, (near, far))
+            pieces.append((rows, (near, far), 0, ratio))
+            pieces.append((exchange(rows[ratio:], "pb", 1), (far, near), 1, 0))
     return pieces, others
 
 
@@ -115,16 +115,18 @@
     fp_count = feat_count * pb_count
     ratio = ex_count // fp_count
     fp = lax.axis_index("feat") * pb_count + pb
-    for piece, (distances, other) in zip(pieces, origins):
+    for piece, (distances, other, left) in zip(pieces, origins):
         where = ex ^ (distances[0] + (distances[1] - distances[0]) * pb)
-        whole = distances == (0, 0)
-        left, right = (0, 1) if other else (ratio, 0)
         for s in range(fp_count):
             slot = (fp ^ other ^ s) * ex_count + where
-            block = piece[s, ex] if whole else piece[left, s]
+            block = piece[s, ex] if left is None else piece[left, s]
             left_rows[slot] = block.astype(jnp.float32)
             if right_rows is not None:
-                block = piece[s, pl.ds(fp * ratio, ratio)] if whole else piece[right : right + ratio, s]
+                if left is None:
+                    block = piece[s, pl.ds(fp * ratio, ratio)]
+                else:
+                    right = 0 if left else 1
+                    block = piece[right : right + ratio, s]
                 right_rows[slot] = block.astype(jnp.float32).reshape(right_rows.shape[1:])
 
 
@@ -258,15 +260,22 @@
     )(kept, *[piece[0] for piece in pieces])
 
 
-def to_owners(chunks, ex_count):
-    half = ex_count // 2
+def to_owners(chunks, sizes):
+    ex_count, feat_count, pb_count = sizes
+    half = ex_count // pb_count
+
+    def device(e, f, p):
+        return (e * feat_count + f) * pb_count + p
+
     arrived = []
     for i, chunk in enumerate(chunks):
         pairs = []
         for e in range(ex_count):
-            pairs.append((e * 2, (e ^ (i + 1 if i < half - 1 else 1)) * 2))
-            pairs.append((e * 2 + 1, (e ^ (half + i)) * 2 + 1))
-        arrived.append(lax.ppermute(chunk, ("ex", "pb"), pairs))
+            for f in range(feat_count):
+                near = device(e ^ (i + 1), f, 0) if i < half - 1 else device(e, f ^ 1, 0)
+                pairs.append((device(e, f, 0), near))
+                pairs.append((device(e, f, 1), device(e ^ (half + i), f, 1)))
+        arrived.append(lax.ppermute(chunk, ("ex", "feat", "pb"), pairs))
     return sum(arrived)
 
 
@@ -284,7 +293,7 @@
     *chunks, own, is_open = partial_scores(
         sizes, query_sketch, others, ids, example_ids.T, pieces
     )
-    part = to_owners(chunks, ex_count)
+    part = to_owners(chunks, sizes)
     gram, own = make_gram(sizes, pieces, own)
     part = (part + own).reshape(pb_count, ex_count, 1, -1)
     pb = lax.axis_index("pb")

time: 25.1 us -> 24.9 us (level)
  starting transfers between devices: 11.1 us -> 10.1 us
  waiting for transfers between devices: 5.48 us -> 6.22 us
    ppermute x5, starting transfers between devices: 5 us -> 4.07 us  [exchange(): lax.ppermute(block, axis, [(i, i ^ step) for i in range(lax.axis_size(axi...]
    ppermute x2, waiting for transfers between devices: 2.37 us -> 3.12 us  [spread(): return lax.ppermute(block, ('ex', 'pb'), pairs)]
    ppermute x2, starting transfers between devices: 2.08 us -> 1.61 us  [to_owners(): arrived.append(lax.ppermute(chunk, ('ex', 'feat', 'pb'), pairs))]
    ppermute x2, starting transfers between devices: 3.98 us -> 4.39 us  [spread(): return lax.ppermute(block, ('ex', 'pb'), pairs)]
  transfers between devices with their start and end apart: 9 -> 9, of which waited for: 4 -> 4; matrix products, arithmetic and copies ran while one was open for 0% -> 0% of each run, Pallas kernels for 9% -> 10%
where the time goes in v8:
time: 24.9 us; the launch traced here: 24.7 us
  starting transfers between devices  10.1 us (41%)
  waiting for transfers between devices  6.22 us (25%)
  Pallas kernels  6.05 us (24%)
  between operations  1.5 us (6%)
  other arithmetic  0.64 us (3%)
    ppermute x2, starting transfers between devices, spread(): return lax.ppermute(block, ('ex', 'pb'), pairs)  4.39 us
    ppermute x5, starting transfers between devices, exchange(): lax.ppermute(block, axis, [(i, i ^ step) for i in range(lax.axis_size(axi...  4.07 us
    pallas_call x1, Pallas kernels, make_sketch(): pl.pallas_call(project_kernel, out_shape=[jax.ShapeDtypeStruct((seq_len,...  3.19 us
    ppermute x2, waiting for transfers between devices, spread(): return lax.ppermute(block, ('ex', 'pb'), pairs)  3.12 us
    ppermute x5, waiting for transfers between devices, exchange(): lax.ppermute(block, axis, [(i, i ^ step) for i in range(lax.axis_size(axi...  3.1 us
    pallas_call x1, Pallas kernels, make_gram(): pl.pallas_call(functools.partial(gram_kernel, sizes, [piece[1:] for piece...  2.37 us
    ppermute x2, starting transfers between devices, to_owners(): arrived.append(lax.ppermute(chunk, ('ex', 'feat', 'pb'), pairs))  1.61 us
    transpose x1, other arithmetic, shards(): return (gram, scores.transpose(2, 0, 1))  0.6 us
  transfers between devices with their start and end apart: 9, of which 4 were waited for; matrix products, arithmetic and copies ran while one was open for 0% of the time, Pallas kernels for 10%

profile of v8, /device:TPU:0, one launch (start us, length us, event | category | flops | bytes accessed | tf_op | source)
XLA Modules:
  0.0 24.7 jit_solution(10852392851196433990)
XLA Ops:
  0.6 0.0 copy-start
  0.6 0.0 copy-start.1
  0.7 0.0 copy-start.2
  1.4 3.2 %project.1 = (bf16[128,64]{1,0:T(8,128)(2,1)S(1)}, bf16[64,128]{1,0:T(8,128)(2,1)S(1)}) custom-call(bf16[128,4096]{1,0:T(8,128)(2,1)} %bitcast.25, bf16[128,7168]{1,0:T(8,128)(2,1)} %bitcast.24, bf16[64,4096]{1,0:T(8,128)(2,1)} %bitcast.27, bf16[64,7168]{1,0:T(8,128)(2,1)} %bitcast.26), custom_call_target="tpu_custom_call" | custom-call | tf_op jit(solution)/shard_map/project/pallas_call | solution.py:44
  4.6 0.1 fusion
  4.7 0.1 reshape_reshape.3
  4.8 0.5 %collective-permute-start = (bf16[1,4,8,128]{3,2,1,0:T(8,128)(2,1)S(1)}, bf16[1,4,8,128]{3,2,1,0:T(8,128)(2,1)S(1)}, u32[]{:S(2)}, u32[]{:S(2)}) collective-permute-start(bf16[1,4,8,128]{3,2,1,0:T(8,128)(2,1)S(1)} %reshape_reshape.3), channel_id=1, source_target_pairs={{0,1},{1,0},{2,3},{3,2},{4,5},{5,4},{6,7},{7,6},{8,9},{9,8},{10,11... | collective-permute-start | bytes 24584 | tf_op jit(solution)/shard_map/ppermute | solution.py:17
  5.3 0.8 %collective-permute-done = bf16[1,4,8,128]{3,2,1,0:T(8,128)(2,1)S(1)} collective-permute-done((bf16[1,4,8,128]{3,2,1,0:T(8,128)(2,1)S(1)}, bf16[1,4,8,128]{3,2,1,0:T(8,128)(2,1)S(1)}, u32[]{:S(2)}, u32[]{:S(2)}) %collective-permute-start) | collective-permute-done | bytes 8224 | tf_op jit(solution)/shard_map/ppermute | solution.py:17
  6.1 0.0 copy-done
  6.1 0.3 %collective-permute-start.1 = (bf16[512,1024]{1,0:T(8,128)(2,1)S(1)}, bf16[512,1024]{1,0:T(8,128)(2,1)S(1)}, u32[]{:S(2)}, u32[]{:S(2)}) collective-permute-start(bf16[512,1024]{1,0:T(8,128)(2,1)S(1)} %copy-done), channel_id=1, source_target_pairs={{0,1},{1,0},{2,3},{3,2},{4,5},{5,4},{6,7},{7,6},{8,9},{9,8},{10,11... | collective-permute-start | bytes 3145736 | tf_op jit(solution)/shard_map/ppermute | solution.py:17
  6.5 2.6 %collective-permute-start.2 = (bf16[2,4,8,128]{3,2,1,0:T(8,128)(2,1)S(1)}, bf16[2,4,8,128]{3,2,1,0:T(8,128)(2,1)S(1)}, u32[]{:S(2)}, u32[]{:S(2)}) collective-permute-start(bf16[2,4,8,128]{3,2,1,0:T(8,128)(2,1)S(1)} %pad_maximum_fusion.2), channel_id=1, source_target_pairs={{0,3},{1,2},{2,1},{3,0},{4,7},{5,6},{6,5},{7,4},{8,11},{9,10},{10,... | collective-permute-start | bytes 49160 | tf_op jit(solution)/shard_map/ppermute | solution.py:17
  9.1 1.4 %collective-permute-done.2 = bf16[2,4,8,128]{3,2,1,0:T(8,128)(2,1)S(1)} collective-permute-done((bf16[2,4,8,128]{3,2,1,0:T(8,128)(2,1)S(1)}, bf16[2,4,8,128]{3,2,1,0:T(8,128)(2,1)S(1)}, u32[]{:S(2)}, u32[]{:S(2)}) %collective-permute-start.2) | collective-permute-done | bytes 16416 | tf_op jit(solution)/shard_map/ppermute | solution.py:17
  10.5 1.9 %collective-permute-start.3 = (bf16[3,4,8,128]{3,2,1,0:T(8,128)(2,1)S(1)}, bf16[3,4,8,128]{3,2,1,0:T(8,128)(2,1)S(1)}, u32[]{:S(2)}, u32[]{:S(2)}) collective-permute-start(bf16[3,4,8,128]{3,2,1,0:T(8,128)(2,1)S(1)} %pad_maximum_fusion.1), channel_id=1, source_target_pairs={{0,4},{1,9},{4,0},{5,13},{8,12},{9,1},{12,8},{13,5},{2,6},{3,11},{... | collective-permute-start | bytes 73736 | tf_op jit(solution)/shard_map/ppermute | solution.py:69
  12.5 2.5 %collective-permute-start.5 = (bf16[2,4,8,128]{3,2,1,0:T(8,128)(2,1)S(1)}, bf16[2,4,8,128]{3,2,1,0:T(8,128)(2,1)S(1)}, u32[]{:S(2)}, u32[]{:S(2)}) collective-permute-start(bf16[2,4,8,128]{3,2,1,0:T(8,128)(2,1)S(1)} %pad_maximum_fusion.3), channel_id=1, source_target_pairs={{0,12},{1,13},{4,8},{5,9},{8,4},{9,5},{12,0},{13,1},{2,14},{3,15},... | collective-permute-start | bytes 49160 | tf_op jit(solution)/shard_map/ppermute | solution.py:69
  14.9 0.0 collective-permute-done.3.refs_1_
  14.9 0.0 collective-permute-start.4
  15.0 3.1 %collective-permute-done.5.refs_3_ = bf16[2,4,8,128]{3,2,1,0:T(8,128)(2,1)S(1)} collective-permute-done((bf16[2,4,8,128]{3,2,1,0:T(8,128)(2,1)S(1)}, bf16[2,4,8,128]{3,2,1,0:T(8,128)(2,1)S(1)}, u32[]{:S(2)}, u32[]{:S(2)}) %collective-permute-start.5) | collective-permute-done | bytes 16416 | tf_op jit(solution)/shard_map/ppermute | solution.py:69
  18.1 0.0 collective-permute-done.4.refs_2_
  18.1 0.0 collective-permute-done.1.other_query_ref
  18.1 0.0 copy-done.1
  18.1 0.0 copy-done.2
  18.1 0.5 %scores.1 = (f32[8,256]{1,0:T(8,128)S(1)}, f32[8,256]{1,0:T(8,128)S(1)}, f32[8,256]{1,0:T(8,128)S(1)}, f32[4,1,256]{2,1,0:T(1,128)S(1)}) custom-call(bf16[512,1024]{1,0:T(8,128)(2,1)S(1)} %copy-done, bf16[512,1024]{1,0:T(8,128)(2,1)S(1)} %collective-permute-done.1.other_query_ref, s32[8,128]{1,0:T(8,128)S(1)} %bitcast.22, s32[1,4]{1,0:T(1,128)S(1)} %bitcast.23, ...), custom_call_target="tpu_custom_call" | custom-call | tf_op jit(solution)/shard_map/scores/pallas_call | solution.py:189
  18.6 0.1 collective-permute-start.6
  18.6 1.5 %collective-permute-start.7 = (f32[8,256]{1,0:T(8,128)S(1)}, f32[8,256]{1,0:T(8,128)S(1)}, u32[]{:S(2)}, u32[]{:S(2)}) collective-permute-start(f32[8,256]{1,0:T(8,128)S(1)} %get-tuple-element.20), channel_id=1, source_target_pairs={{0,2},{1,13},{2,0},{3,15},{4,6},{5,9},{6,4},{7,11},{8,10},{9,5},{1... | collective-permute-start | bytes 24584 | tf_op jit(solution)/shard_map/ppermute | solution.py:278
  20.2 2.4 %gram.1 = (f32[1024,1024]{1,0:T(8,128)}, f32[8,256]{1,0:T(8,128)S(1)}) custom-call(f32[8,256]{1,0:T(8,128)S(1)} %get-tuple-element.16.kept_ref, bf16[4,4,8,128]{3,2,1,0:T(8,128)(2,1)S(1)} %pad_maximum_fusion.refs_0_, bf16[3,4,8,128]{3,2,1,0:T(8,128)(2,1)S(1)} %collective-permute-done.3.refs_1_, bf16[2,4,8,128]{3,2,1,0:T(8,128)(2,1)S(1)} %collective-permute-done.4.refs_2_, ...), custom_call_target="tpu_custom_call" | custom-call | flops 536870912 | bytes 4194304 | tf_op jit(solution)/shard_map/gram/pallas_call | solution.py:237
  22.6 0.0 collective-permute-done.6
  22.6 0.0 collective-permute-done.7
  22.7 0.7 %collective-permute-start.8 = (f32[4,1,256]{2,1,0:T(1,128)S(1)}, f32[4,1,256]{2,1,0:T(1,128)S(1)}, u32[]{:S(2)}, u32[]{:S(2)}) collective-permute-start(f32[4,1,256]{2,1,0:T(1,128)S(1)} %squeeze.27), channel_id=1, source_target_pairs={{0,1},{1,0},{2,3},{3,2},{4,5},{5,4},{6,7},{7,6},{8,9},{9,8},{10,11... | collective-permute-start | bytes 12296 | tf_op jit(solution)/shard_map/ppermute | solution.py:17
  23.3 0.8 %collective-permute-done.8 = f32[4,1,256]{2,1,0:T(1,128)S(1)} collective-permute-done((f32[4,1,256]{2,1,0:T(1,128)S(1)}, f32[4,1,256]{2,1,0:T(1,128)S(1)}, u32[]{:S(2)}, u32[]{:S(2)}) %collective-permute-start.8) | collective-permute-done | bytes 4128 | tf_op jit(solution)/shard_map/ppermute | solution.py:17
  24.1 0.6 %fusion.11 = f32[256,4,1]{0,2,1:T(1,128)} fusion(f32[4,1,256]{2,1,0:T(1,128)S(1)} %get-tuple-element.18, f32[4,1,256]{2,1,0:T(1,128)S(1)} %collective-permute-done.8, f32[1,4,1,256]{3,1,0,2:T(4,128)S(1)} %get-tuple-element.26), kind=kLoop, calls=%fused_computation.26 | loop fusion | flops 3072 | bytes 16384 | tf_op jit(solution)/shard_map/transpose | solution.py:303
  (12 shorter events, 0.1 us)
Async XLA Ops:
  0.6 5.5 %copy-start = (bf16[512,1024]{1,0:T(8,128)(2,1)S(1)}, bf16[512,1024]{1,0:T(8,128)(2,1)}, u32[]{:S(2)}) copy-start(bf16[512,1024]{1,0:T(8,128)(2,1)} %query_ref.1) | copy-start | bytes 3145732
  0.6 17.4 %copy-start.1 = (s32[1024]{0:T(1024)S(1)}, s32[1024]{0:T(1024)}, u32[]{:S(2)}) copy-start(s32[1024]{0:T(1024)} %param.15) | copy-start | bytes 12292
  0.7 17.4 %copy-start.2 = (s32[4,1]{0,1:T(1,128)S(1)}, s32[4,1]{0,1:T(1,128)}, u32[]{:S(2)}) copy-start(s32[4,1]{0,1:T(1,128)} %param.13) | copy-start | bytes 52
  4.8 1.3 %collective-permute-start = (bf16[1,4,8,128]{3,2,1,0:T(8,128)(2,1)S(1)}, bf16[1,4,8,128]{3,2,1,0:T(8,128)(2,1)S(1)}, u32[]{:S(2)}, u32[]{:S(2)}) collective-permute-start(bf16[1,4,8,128]{3,2,1,0:T(8,128)(2,1)S(1)} %reshape_reshape.3), channel_id=1, source_target_pairs={{0,1},{1,0},{2,3},{3,2},{4,5},{5,4},{6,7},{7,6},{8,9},{9,8},{10,11... | collective-permute-start | bytes 24584 | tf_op jit(solution)/shard_map/ppermute | solution.py:17
  6.1 12.0 %collective-permute-start.1 = (bf16[512,1024]{1,0:T(8,128)(2,1)S(1)}, bf16[512,1024]{1,0:T(8,128)(2,1)S(1)}, u32[]{:S(2)}, u32[]{:S(2)}) collective-permute-start(bf16[512,1024]{1,0:T(8,128)(2,1)S(1)} %copy-done), channel_id=1, source_target_pairs={{0,1},{1,0},{2,3},{3,2},{4,5},{5,4},{6,7},{7,6},{8,9},{9,8},{10,11... | collective-permute-start | bytes 3145736 | tf_op jit(solution)/shard_map/ppermute | solution.py:17
  6.5 4.0 %collective-permute-start.2 = (bf16[2,4,8,128]{3,2,1,0:T(8,128)(2,1)S(1)}, bf16[2,4,8,128]{3,2,1,0:T(8,128)(2,1)S(1)}, u32[]{:S(2)}, u32[]{:S(2)}) collective-permute-start(bf16[2,4,8,128]{3,2,1,0:T(8,128)(2,1)S(1)} %pad_maximum_fusion.2), channel_id=1, source_target_pairs={{0,3},{1,2},{2,1},{3,0},{4,7},{5,6},{6,5},{7,4},{8,11},{9,10},{10,... | collective-permute-start | bytes 49160 | tf_op jit(solution)/shard_map/ppermute | solution.py:17
  10.5 4.4 %collective-permute-start.3 = (bf16[3,4,8,128]{3,2,1,0:T(8,128)(2,1)S(1)}, bf16[3,4,8,128]{3,2,1,0:T(8,128)(2,1)S(1)}, u32[]{:S(2)}, u32[]{:S(2)}) collective-permute-start(bf16[3,4,8,128]{3,2,1,0:T(8,128)(2,1)S(1)} %pad_maximum_fusion.1), channel_id=1, source_target_pairs={{0,4},{1,9},{4,0},{5,13},{8,12},{9,1},{12,8},{13,5},{2,6},{3,11},{... | collective-permute-start | bytes 73736 | tf_op jit(solution)/shard_map/ppermute | solution.py:69
  12.5 5.6 %collective-permute-start.5 = (bf16[2,4,8,128]{3,2,1,0:T(8,128)(2,1)S(1)}, bf16[2,4,8,128]{3,2,1,0:T(8,128)(2,1)S(1)}, u32[]{:S(2)}, u32[]{:S(2)}) collective-permute-start(bf16[2,4,8,128]{3,2,1,0:T(8,128)(2,1)S(1)} %pad_maximum_fusion.3), channel_id=1, source_target_pairs={{0,12},{1,13},{4,8},{5,9},{8,4},{9,5},{12,0},{13,1},{2,14},{3,15},... | collective-permute-start | bytes 49160 | tf_op jit(solution)/shard_map/ppermute | solution.py:69
  14.9 3.1 %collective-permute-start.4 = (bf16[2,4,8,128]{3,2,1,0:T(8,128)(2,1)S(1)}, bf16[2,4,8,128]{3,2,1,0:T(8,128)(2,1)S(1)}, u32[]{:S(2)}, u32[]{:S(2)}) collective-permute-start(bf16[2,4,8,128]{3,2,1,0:T(8,128)(2,1)S(1)} %slice.4), channel_id=1, source_target_pairs={{0,1},{1,0},{2,3},{3,2},{4,5},{5,4},{6,7},{7,6},{8,9},{9,8},{10,11... | collective-permute-start | bytes 49160 | tf_op jit(solution)/shard_map/ppermute | solution.py:17
  18.6 4.0 %collective-permute-start.6 = (f32[8,256]{1,0:T(8,128)S(1)}, f32[8,256]{1,0:T(8,128)S(1)}, u32[]{:S(2)}, u32[]{:S(2)}) collective-permute-start(f32[8,256]{1,0:T(8,128)S(1)} %get-tuple-element.19), channel_id=1, source_target_pairs={{0,4},{1,9},{2,6},{3,11},{4,0},{5,13},{6,2},{7,15},{8,12},{9,1},{1... | collective-permute-start | bytes 24584 | tf_op jit(solution)/shard_map/ppermute | solution.py:278
  18.6 3.9 %collective-permute-start.7 = (f32[8,256]{1,0:T(8,128)S(1)}, f32[8,256]{1,0:T(8,128)S(1)}, u32[]{:S(2)}, u32[]{:S(2)}) collective-permute-start(f32[8,256]{1,0:T(8,128)S(1)} %get-tuple-element.20), channel_id=1, source_target_pairs={{0,2},{1,13},{2,0},{3,15},{4,6},{5,9},{6,4},{7,11},{8,10},{9,5},{1... | collective-permute-start | bytes 24584 | tf_op jit(solution)/shard_map/ppermute | solution.py:278
  22.7 1.5 %collective-permute-start.8 = (f32[4,1,256]{2,1,0:T(1,128)S(1)}, f32[4,1,256]{2,1,0:T(1,128)S(1)}, u32[]{:S(2)}, u32[]{:S(2)}) collective-permute-start(f32[4,1,256]{2,1,0:T(1,128)S(1)} %squeeze.27), channel_id=1, source_target_pairs={{0,1},{1,0},{2,3},{3,2},{4,5},{5,4},{6,7},{7,6},{8,9},{9,8},{10,11... | collective-permute-start | bytes 12296 | tf_op jit(solution)/shard_map/ppermute | solution.py:17

commit v9 on v8

--- a/solution.py
+++ b/solution.py
@@ -17,9 +17,9 @@
     return lax.ppermute(block, axis, [(i, i ^ step) for i in range(lax.axis_size(axis))])
 
 
-def project_kernel(
-    acts_hbm, grads_hbm, act_proj_hbm, grad_proj_hbm, act_low_ref, grad_low_ref,
-    acts, grads, act_proj, grad_proj, sems,
+def sketch_kernel(
+    acts_hbm, grads_hbm, act_proj_hbm, grad_proj_hbm, keep_ref, out_ref,
+    acts, grads, act_proj, grad_proj, turned, sems,
 ):
     sources = (act_proj_hbm, acts_hbm, grad_proj_hbm, grads_hbm)
     targets = (act_proj, acts, grad_proj, grads)
@@ -31,33 +31,39 @@
     for copy in copies[:2]:
         copy.wait()
     act_sum = lax.dot_general(acts[...], act_proj[...], NT, preferred_element_type=jnp.float32)
+    act_low = act_sum.astype(jnp.bfloat16)
     for copy in copies[2:]:
         copy.wait()
     grad_sum = lax.dot_general(grad_proj[...], grads[...], NT, preferred_element_type=jnp.float32)
-    act_low_ref[...] = act_sum.astype(jnp.bfloat16)
-    grad_low_ref[...] = grad_sum.astype(jnp.bfloat16)
+    rank, seq_len = grad_sum.shape
+    turned[pl.ds(0, rank), :] = grad_sum * keep_ref[...]
+    halves = [
+        jnp.dot(
+            turned[pl.ds(side, rank // 2, stride=2), :].astype(jnp.bfloat16),
+            act_low,
+            preferred_element_type=jnp.float32,
+        )
+        for side in range(2)
+    ]
+    outer = jnp.concatenate(halves, axis=1) * (1.0 / math.sqrt(seq_len))
+    out_ref[...] = outer.astype(jnp.bfloat16)
 
 
 def make_sketch(acts, grads, act_proj, grad_proj, tok_count):
     seq_len, rank = acts.shape[0], act_proj.shape[1]
     operands = (acts, grads, act_proj.T, grad_proj.T)
-    act_low, grad_low = pl.pallas_call(
-        project_kernel,
-        out_shape=[
-            jax.ShapeDtypeStruct((seq_len, rank), jnp.bfloat16),
-            jax.ShapeDtypeStruct((rank, seq_len), jnp.bfloat16),
-        ],
-        in_specs=[pl.BlockSpec(memory_space=pl.ANY)] * 4,
-        out_specs=[pl.BlockSpec(memory_space=pltpu.VMEM)] * 2,
+    keep = (jnp.arange(seq_len, dtype=jnp.int32) < tok_count).astype(jnp.float32)
+    vmem = pl.BlockSpec(memory_space=pltpu.VMEM)
+    return pl.pallas_call(
+        sketch_kernel,
+        out_shape=jax.ShapeDtypeStruct((rank // 2, 2 * rank), jnp.bfloat16),
+        in_specs=[pl.BlockSpec(memory_space=pl.ANY)] * 4 + [vmem],
+        out_specs=vmem,
         scratch_shapes=[pltpu.VMEM(x.shape, x.dtype) for x in operands]
-        + [pltpu.SemaphoreType.DMA((4,))],
+        + [pltpu.VMEM((rank + 8, seq_len), jnp.float32), pltpu.SemaphoreType.DMA((4,))],
         compiler_params=pltpu.CompilerParams(vmem_limit_bytes=16 * 2**20),
-        name="project",
-    )(*[pltpu.with_memory_space_constraint(x, pltpu.HBM) for x in operands])
-    mask = (jnp.arange(seq_len, dtype=jnp.int32) < tok_count).astype(jnp.bfloat16)
-    outer = jnp.dot(grad_low * mask[None, :], act_low, preferred_element_type=jnp.float32)
-    outer = outer * (1.0 / math.sqrt(seq_len))
-    return outer.astype(jnp.bfloat16).reshape(rank * rank // LANES, LANES)
+        name="sketch",
+    )(*[pltpu.with_memory_space_constraint(x, pltpu.HBM) for x in operands], keep[None])
 
 
 def spread(block, distances):
@@ -82,10 +88,9 @@
     ex, feat, pb = (lax.axis_index(axis) for axis in ("ex", "feat", "pb"))
     fp_count, fp = feat_count * pb_count, feat * pb_count + pb
     ratio = ex_count // fp_count
+    others = exchange(queries, "pb", 1)
     own = sketch.reshape(1, ex_count, -1, LANES)
     own = jnp.concatenate([own, exchange(own, "pb", 1)])
-    own, queries = lax.optimization_barrier((own, queries))
-    others = exchange(queries, "pb", 1)
     line = [own]
     for k in range(1, feat_count):
         line.append(exchange(own, ("feat", "pb"), k * pb_count + 1)[::-1])
@@ -130,14 +135,12 @@
                 right_rows[slot] = block.astype(jnp.float32).reshape(right_rows.shape[1:])
 
 
-def score_kernel(
-    sizes, origins, query_ref, other_query_ref, query_ids_ref, example_ids_ref, *refs
-):
+def score_kernel(sizes, origins, query_ref, other_query_ref, *refs):
     ex_count, feat_count, pb_count = sizes
     pieces, refs = refs[: len(origins)], refs[len(origins) :]
     half = ex_count // pb_count
     outs = refs[:half]
-    own_ref, open_ref, rows, scaled, chunks = refs[-5:]
+    own_ref, rows, scaled, chunks = refs[-4:]
     ex, feat = lax.axis_index("ex"), lax.axis_index("feat")
     near = lax.axis_index("pb") == 0
     here = lax.rem(ex, half)
@@ -172,14 +175,9 @@
         outs[i][...] = chunks[here ^ (i + shift)]
     outs[half - 1][...] = jnp.where(near, 0.0, chunks[here ^ (half - 1)])
     own_ref[...] = jnp.where(near, chunks[here], 0.0)
-    spans = chunks.shape[2] // query_ids_ref.shape[1]
-    ids = [query_ids_ref[pl.ds(ex * spans + i, 1), :] for i in range(spans)]
-    ids = jnp.concatenate(ids, axis=1)
-    for a in range(ex_count):
-        open_ref[a] = jnp.where(example_ids_ref[:, a : a + 1] == ids, 0.0, 1.0)
-
-
-def partial_scores(sizes, queries, other_queries, query_ids, example_ids, pieces):
+
+
+def partial_scores(sizes, queries, other_queries, pieces):
     ex_count, feat_count, pb_count = sizes
     examples = ex_count * feat_count * pb_count
     lines, lanes = pieces[0][0].shape[2:]
@@ -188,10 +186,9 @@
     vmem = pl.BlockSpec(memory_space=pltpu.VMEM)
     return pl.pallas_call(
         functools.partial(score_kernel, sizes, [piece[1:] for piece in pieces]),
-        out_shape=[jax.ShapeDtypeStruct(chunk, jnp.float32)] * (half + 1)
-        + [jax.ShapeDtypeStruct((ex_count, 1, chunk[1]), jnp.float32)],
-        in_specs=[vmem] * (4 + len(pieces)),
-        out_specs=[vmem] * (half + 2),
+        out_shape=[jax.ShapeDtypeStruct(chunk, jnp.float32)] * (half + 1),
+        in_specs=[vmem] * (2 + len(pieces)),
+        out_specs=[vmem] * (half + 1),
         scratch_shapes=[
             pltpu.VMEM((examples, lines, lanes), jnp.float32),
             pltpu.VMEM(((pb_count * ex_count + 1) * lines, lanes), jnp.float32),
@@ -199,13 +196,19 @@
         ],
         compiler_params=pltpu.CompilerParams(vmem_limit_bytes=24 * 2**20),
         name="scores",
-    )(queries, other_queries, query_ids, example_ids, *[piece[0] for piece in pieces])
-
-
-def gram_kernel(sizes, origins, kept_ref, *refs):
+    )(queries, other_queries, *[piece[0] for piece in pieces])
+
+
+def gram_kernel(sizes, origins, kept_ref, query_ids_ref, example_ids_ref, *refs):
     pieces, refs = refs[: len(origins)], refs[len(origins) :]
-    out_hbm, kept_out_ref, left_rows, right_rows, left, right, result, sems = refs
+    out_hbm, kept_out_ref, open_ref, left_rows, right_rows, left, right, result, sems = refs
     kept_out_ref[...] = kept_ref[...]
+    ex = lax.axis_index("ex")
+    spans = open_ref.shape[2] // query_ids_ref.shape[1]
+    ids = [query_ids_ref[pl.ds(ex * spans + i, 1), :] for i in range(spans)]
+    ids = jnp.concatenate(ids, axis=1)
+    for a in range(open_ref.shape[0]):
+        open_ref[a] = jnp.where(example_ids_ref[:, a : a + 1] == ids, 0.0, 1.0)
     examples, left_lines, lanes = left_rows.shape
     right_lines = right_rows.shape[1]
     place_rows(sizes, origins, pieces, left_rows, right_rows)
@@ -229,19 +232,21 @@
         copy.wait()
 
 
-def make_gram(sizes, pieces, kept):
+def make_gram(sizes, pieces, kept, query_ids, example_ids):
     examples = sizes[0] * sizes[1] * sizes[2]
     left_lines = pieces[0][0].shape[2]
     right_lines = left_lines * sizes[0] // (sizes[1] * sizes[2])
     shape = (left_lines * LANES, right_lines * LANES)
+    vmem = pl.BlockSpec(memory_space=pltpu.VMEM)
     return pl.pallas_call(
         functools.partial(gram_kernel, sizes, [piece[1:] for piece in pieces]),
         out_shape=[
             jax.ShapeDtypeStruct(shape, jnp.float32),
             jax.ShapeDtypeStruct(kept.shape, kept.dtype),
+            jax.ShapeDtypeStruct((sizes[0], 1, kept.shape[1]), jnp.float32),
         ],
-        in_specs=[pl.BlockSpec(memory_space=pltpu.VMEM)] * (1 + len(pieces)),
-        out_specs=[pl.BlockSpec(memory_space=pl.ANY), pl.BlockSpec(memory_space=pltpu.VMEM)],
+        in_specs=[vmem] * (3 + len(pieces)),
+        out_specs=[pl.BlockSpec(memory_space=pl.ANY), vmem, vmem],
         scratch_shapes=[
             pltpu.VMEM((examples, left_lines, LANES), jnp.float32),
             pltpu.VMEM((examples, right_lines, LANES), jnp.float32),
@@ -257,7 +262,7 @@
             transcendentals=0,
         ),
         name="gram",
-    )(kept, *[piece[0] for piece in pieces])
+    )(kept, query_ids, example_ids, *[piece[0] for piece in pieces])
 
 
 def to_owners(chunks, sizes):
@@ -290,11 +295,9 @@
     pieces, others = gather_rows(sizes, sketch, query_sketch)
     width = query_ids.shape[0] // ex_count
     ids = query_ids.reshape(-1, min(width, 128))
-    *chunks, own, is_open = partial_scores(
-        sizes, query_sketch, others, ids, example_ids.T, pieces
-    )
+    *chunks, own = partial_scores(sizes, query_sketch, others, pieces)
     part = to_owners(chunks, sizes)
-    gram, own = make_gram(sizes, pieces, own)
+    gram, own, is_open = make_gram(sizes, pieces, own, ids, example_ids.T)
     part = (part + own).reshape(pb_count, ex_count, 1, -1)
     pb = lax.axis_index("pb")
     theirs = lax.dynamic_index_in_dim(part, 1 - pb, 0, keepdims=False)

time: 24.9 us -> 24.8 us (level)
  transfers between devices with their start and end apart: 9 -> 9, of which waited for: 4 -> 4; matrix products, arithmetic and copies ran while one was open for 0% -> 0% of each run, Pallas kernels for 10% -> 23%
where the time goes in v9:
time: 24.8 us; the launch traced here: 24.6 us
  starting transfers between devices  9.95 us (40%)
  waiting for transfers between devices  6.44 us (26%)
  Pallas kernels  6.13 us (25%)
  between operations  1.41 us (6%)
  other arithmetic  0.63 us (3%)
    ppermute x2, starting transfers between devices, spread(): return lax.ppermute(block, ('ex', 'pb'), pairs)  4.4 us
    ppermute x5, starting transfers between devices, exchange(): lax.ppermute(block, axis, [(i, i ^ step) for i in range(lax.axis_size(axi...  3.98 us
    pallas_call x1, Pallas kernels, make_sketch(): pl.pallas_call(sketch_kernel, out_shape=jax.ShapeDtypeStruct((rank // 2,...  3.35 us
    ppermute x5, waiting for transfers between devices, exchange(): lax.ppermute(block, axis, [(i, i ^ step) for i in range(lax.axis_size(axi...  3.31 us
    ppermute x2, waiting for transfers between devices, spread(): return lax.ppermute(block, ('ex', 'pb'), pairs)  3.12 us
    pallas_call x1, Pallas kernels, make_gram(): pl.pallas_call(functools.partial(gram_kernel, sizes, [piece[1:] for piece...  2.38 us
    ppermute x2, starting transfers between devices, to_owners(): arrived.append(lax.ppermute(chunk, ('ex', 'feat', 'pb'), pairs))  1.57 us
    transpose x1, other arithmetic, shards(): return (gram, scores.transpose(2, 0, 1))  0.6 us
  transfers between devices with their start and end apart: 9, of which 4 were waited for; matrix products, arithmetic and copies ran while one was open for 0% of the time, Pallas kernels for 23%

profile of v9, /device:TPU:0, one launch (start us, length us, event | category | flops | bytes accessed | tf_op | source)
XLA Modules:
  0.0 24.6 jit_solution(12734556115075146970)
XLA Ops:
  0.6 0.0 copy-start
  0.6 0.0 copy-start.1
  0.7 0.0 copy-start.2
  0.7 0.5 %collective-permute-start = (bf16[512,1024]{1,0:T(8,128)(2,1)}, bf16[512,1024]{1,0:T(8,128)(2,1)S(1)}, u32[]{:S(2)}, u32[]{:S(2)}) collective-permute-start(bf16[512,1024]{1,0:T(8,128)(2,1)} %query_ref.1), channel_id=1, source_target_pairs={{0,1},{1,0},{2,3},{3,2},{4,5},{5,4},{6,7},{7,6},{8,9},{9,8},{10,11... | collective-permute-start | bytes 3145736 | tf_op jit(solution)/shard_map/ppermute | solution.py:17
  1.8 3.4 %sketch.1 = bf16[32,128]{1,0:T(8,128)(2,1)S(1)} custom-call(bf16[128,4096]{1,0:T(8,128)(2,1)} %bitcast.31, bf16[128,7168]{1,0:T(8,128)(2,1)} %bitcast.30, bf16[64,4096]{1,0:T(8,128)(2,1)} %bitcast.33, bf16[64,7168]{1,0:T(8,128)(2,1)} %bitcast.32, f32[1,128]{1,0:T(1,128)S(1)} %compare_convert_fusion.keep_ref), custom_call_target="tpu_custom_call" | custom-call | tf_op jit(solution)/shard_map/sketch/pallas_call | solution.py:57
  5.2 0.2 collective-permute-start.1
  5.4 1.0 %collective-permute-done.1 = bf16[1,4,8,128]{3,2,1,0:T(8,128)(2,1)S(1)} collective-permute-done((bf16[1,4,8,128]{3,2,1,0:T(8,128)(2,1)S(1)}, bf16[1,4,8,128]{3,2,1,0:T(8,128)(2,1)S(1)}, u32[]{:S(2)}, u32[]{:S(2)}) %collective-permute-start.1) | collective-permute-done | bytes 8224 | tf_op jit(solution)/shard_map/ppermute | solution.py:17
  6.4 2.6 %collective-permute-start.2 = (bf16[2,4,8,128]{3,2,1,0:T(8,128)(2,1)S(1)}, bf16[2,4,8,128]{3,2,1,0:T(8,128)(2,1)S(1)}, u32[]{:S(2)}, u32[]{:S(2)}) collective-permute-start(bf16[2,4,8,128]{3,2,1,0:T(8,128)(2,1)S(1)} %pad_maximum_fusion.2), channel_id=1, source_target_pairs={{0,3},{1,2},{2,1},{3,0},{4,7},{5,6},{6,5},{7,4},{8,11},{9,10},{10,... | collective-permute-start | bytes 49160 | tf_op jit(solution)/shard_map/ppermute | solution.py:17
  9.0 1.4 %collective-permute-done.2 = bf16[2,4,8,128]{3,2,1,0:T(8,128)(2,1)S(1)} collective-permute-done((bf16[2,4,8,128]{3,2,1,0:T(8,128)(2,1)S(1)}, bf16[2,4,8,128]{3,2,1,0:T(8,128)(2,1)S(1)}, u32[]{:S(2)}, u32[]{:S(2)}) %collective-permute-start.2) | collective-permute-done | bytes 16416 | tf_op jit(solution)/shard_map/ppermute | solution.py:17
  10.5 1.9 %collective-permute-start.3 = (bf16[3,4,8,128]{3,2,1,0:T(8,128)(2,1)S(1)}, bf16[3,4,8,128]{3,2,1,0:T(8,128)(2,1)S(1)}, u32[]{:S(2)}, u32[]{:S(2)}) collective-permute-start(bf16[3,4,8,128]{3,2,1,0:T(8,128)(2,1)S(1)} %pad_maximum_fusion.1), channel_id=1, source_target_pairs={{0,4},{1,9},{4,0},{5,13},{8,12},{9,1},{12,8},{13,5},{2,6},{3,11},{... | collective-permute-start | bytes 73736 | tf_op jit(solution)/shard_map/ppermute | solution.py:75
  12.5 2.5 %collective-permute-start.5 = (bf16[2,4,8,128]{3,2,1,0:T(8,128)(2,1)S(1)}, bf16[2,4,8,128]{3,2,1,0:T(8,128)(2,1)S(1)}, u32[]{:S(2)}, u32[]{:S(2)}) collective-permute-start(bf16[2,4,8,128]{3,2,1,0:T(8,128)(2,1)S(1)} %pad_maximum_fusion.3), channel_id=1, source_target_pairs={{0,12},{1,13},{4,8},{5,9},{8,4},{9,5},{12,0},{13,1},{2,14},{3,15},... | collective-permute-start | bytes 49160 | tf_op jit(solution)/shard_map/ppermute | solution.py:75
  14.9 0.0 collective-permute-done.3.refs_1_
  14.9 0.0 collective-permute-start.4
  15.0 3.1 %collective-permute-done.5.refs_3_ = bf16[2,4,8,128]{3,2,1,0:T(8,128)(2,1)S(1)} collective-permute-done((bf16[2,4,8,128]{3,2,1,0:T(8,128)(2,1)S(1)}, bf16[2,4,8,128]{3,2,1,0:T(8,128)(2,1)S(1)}, u32[]{:S(2)}, u32[]{:S(2)}) %collective-permute-start.5) | collective-permute-done | bytes 16416 | tf_op jit(solution)/shard_map/ppermute | solution.py:75
  18.1 0.0 collective-permute-done.4.refs_2_
  18.1 0.0 collective-permute-done.other_query_ref
  18.1 0.0 copy-done
  18.1 0.4 %scores.1 = (f32[8,256]{1,0:T(8,128)S(1)}, f32[8,256]{1,0:T(8,128)S(1)}, f32[8,256]{1,0:T(8,128)S(1)}) custom-call(bf16[512,1024]{1,0:T(8,128)(2,1)S(1)} %copy-done, bf16[512,1024]{1,0:T(8,128)(2,1)S(1)} %collective-permute-done.other_query_ref, bf16[4,4,8,128]{3,2,1,0:T(8,128)(2,1)S(1)} %pad_maximum_fusion.refs_0_, ...), custom_call_target="tpu_custom_call" | custom-call | tf_op jit(solution)/shard_map/scores/pallas_call | solution.py:187
  18.5 0.0 collective-permute-start.6
  18.5 1.6 %collective-permute-start.7 = (f32[8,256]{1,0:T(8,128)S(1)}, f32[8,256]{1,0:T(8,128)S(1)}, u32[]{:S(2)}, u32[]{:S(2)}) collective-permute-start(f32[8,256]{1,0:T(8,128)S(1)} %get-tuple-element.12), channel_id=1, source_target_pairs={{0,2},{1,13},{2,0},{3,15},{4,6},{5,9},{6,4},{7,11},{8,10},{9,5},{1... | collective-permute-start | bytes 24584 | tf_op jit(solution)/shard_map/ppermute | solution.py:283
  20.1 0.0 copy-done.1
  20.1 0.0 copy-done.2
  20.1 2.4 %gram.1 = (f32[1024,1024]{1,0:T(8,128)}, f32[8,256]{1,0:T(8,128)S(1)}, f32[4,1,256]{2,1,0:T(1,128)S(1)}) custom-call(f32[8,256]{1,0:T(8,128)S(1)} %get-tuple-element.8.kept_ref, s32[8,128]{1,0:T(8,128)S(1)} %bitcast.28, s32[1,4]{1,0:T(1,128)S(1)} %bitcast.29, bf16[4,4,8,128]{3,2,1,0:T(8,128)(2,1)S(1)} %pad_maximum_fusion.refs_0_, ...), custom_call_target="tpu_custom_call" | custom-call | flops 536870912 | bytes 4194304 | tf_op jit(solution)/shard_map/gram/pallas_call | solution.py:241
  22.5 0.0 collective-permute-done.6
  22.5 0.0 collective-permute-done.7
  22.5 0.7 %collective-permute-start.8 = (f32[4,1,256]{2,1,0:T(1,128)S(1)}, f32[4,1,256]{2,1,0:T(1,128)S(1)}, u32[]{:S(2)}, u32[]{:S(2)}) collective-permute-start(f32[4,1,256]{2,1,0:T(1,128)S(1)} %dynamic-slice_bitcast_fusion.4), channel_id=1, source_target_pairs={{0,1},{1,0},{2,3},{3,2},{4,5},{5,4},{6,7},{7,6},{8,9},{9,8},{10,11... | collective-permute-start | bytes 12296 | tf_op jit(solution)/shard_map/ppermute | solution.py:17
  23.2 0.8 %collective-permute-done.8 = f32[4,1,256]{2,1,0:T(1,128)S(1)} collective-permute-done((f32[4,1,256]{2,1,0:T(1,128)S(1)}, f32[4,1,256]{2,1,0:T(1,128)S(1)}, u32[]{:S(2)}, u32[]{:S(2)}) %collective-permute-start.8) | collective-permute-done | bytes 4128 | tf_op jit(solution)/shard_map/ppermute | solution.py:17
  24.0 0.6 %fusion = f32[256,4,1]{0,2,1:T(1,128)} fusion(f32[4,1,256]{2,1,0:T(1,128)S(1)} %get-tuple-element.10, f32[4,1,256]{2,1,0:T(1,128)S(1)} %collective-permute-done.8, f32[2,4,1,256]{3,2,1,0:T(1,128)S(1)} %reshape.35, s32[]{:T(128)S(6)} %select_n.30), kind=kLoop, calls=%fused_computation.10 | loop fusion | flops 3072 | bytes 16388 | tf_op jit(solution)/shard_map/transpose | solution.py:306
  (11 shorter events, 0.1 us)
Async XLA Ops:
  0.6 17.4 %copy-start = (bf16[512,1024]{1,0:T(8,128)(2,1)S(1)}, bf16[512,1024]{1,0:T(8,128)(2,1)}, u32[]{:S(2)}) copy-start(bf16[512,1024]{1,0:T(8,128)(2,1)} %query_ref.1) | copy-start | bytes 3145732
  0.6 19.4 %copy-start.1 = (s32[1024]{0:T(1024)S(1)}, s32[1024]{0:T(1024)}, u32[]{:S(2)}) copy-start(s32[1024]{0:T(1024)} %param.15) | copy-start | bytes 12292
  0.7 19.4 %copy-start.2 = (s32[4,1]{0,1:T(1,128)S(1)}, s32[4,1]{0,1:T(1,128)}, u32[]{:S(2)}) copy-start(s32[4,1]{0,1:T(1,128)} %param.13) | copy-start | bytes 52
  0.7 17.4 %collective-permute-start = (bf16[512,1024]{1,0:T(8,128)(2,1)}, bf16[512,1024]{1,0:T(8,128)(2,1)S(1)}, u32[]{:S(2)}, u32[]{:S(2)}) collective-permute-start(bf16[512,1024]{1,0:T(8,128)(2,1)} %query_ref.1), channel_id=1, source_target_pairs={{0,1},{1,0},{2,3},{3,2},{4,5},{5,4},{6,7},{7,6},{8,9},{9,8},{10,11... | collective-permute-start | bytes 3145736 | tf_op jit(solution)/shard_map/ppermute | solution.py:17
  5.2 1.2 %collective-permute-start.1 = (bf16[1,4,8,128]{3,2,1,0:T(8,128)(2,1)S(1)}, bf16[1,4,8,128]{3,2,1,0:T(8,128)(2,1)S(1)}, u32[]{:S(2)}, u32[]{:S(2)}) collective-permute-start(bf16[1,4,8,128]{3,2,1,0:T(8,128)(2,1)S(1)} %bitcast.25), channel_id=1, source_target_pairs={{0,1},{1,0},{2,3},{3,2},{4,5},{5,4},{6,7},{7,6},{8,9},{9,8},{10,11... | collective-permute-start | bytes 24584 | tf_op jit(solution)/shard_map/ppermute | solution.py:17
  6.4 4.0 %collective-permute-start.2 = (bf16[2,4,8,128]{3,2,1,0:T(8,128)(2,1)S(1)}, bf16[2,4,8,128]{3,2,1,0:T(8,128)(2,1)S(1)}, u32[]{:S(2)}, u32[]{:S(2)}) collective-permute-start(bf16[2,4,8,128]{3,2,1,0:T(8,128)(2,1)S(1)} %pad_maximum_fusion.2), channel_id=1, source_target_pairs={{0,3},{1,2},{2,1},{3,0},{4,7},{5,6},{6,5},{7,4},{8,11},{9,10},{10,... | collective-permute-start | bytes 49160 | tf_op jit(solution)/shard_map/ppermute | solution.py:17
  10.5 4.4 %collective-permute-start.3 = (bf16[3,4,8,128]{3,2,1,0:T(8,128)(2,1)S(1)}, bf16[3,4,8,128]{3,2,1,0:T(8,128)(2,1)S(1)}, u32[]{:S(2)}, u32[]{:S(2)}) collective-permute-start(bf16[3,4,8,128]{3,2,1,0:T(8,128)(2,1)S(1)} %pad_maximum_fusion.1), channel_id=1, source_target_pairs={{0,4},{1,9},{4,0},{5,13},{8,12},{9,1},{12,8},{13,5},{2,6},{3,11},{... | collective-permute-start | bytes 73736 | tf_op jit(solution)/shard_map/ppermute | solution.py:75
  12.5 5.6 %collective-permute-start.5 = (bf16[2,4,8,128]{3,2,1,0:T(8,128)(2,1)S(1)}, bf16[2,4,8,128]{3,2,1,0:T(8,128)(2,1)S(1)}, u32[]{:S(2)}, u32[]{:S(2)}) collective-permute-start(bf16[2,4,8,128]{3,2,1,0:T(8,128)(2,1)S(1)} %pad_maximum_fusion.3), channel_id=1, source_target_pairs={{0,12},{1,13},{4,8},{5,9},{8,4},{9,5},{12,0},{13,1},{2,14},{3,15},... | collective-permute-start | bytes 49160 | tf_op jit(solution)/shard_map/ppermute | solution.py:75
  14.9 3.1 %collective-permute-start.4 = (bf16[2,4,8,128]{3,2,1,0:T(8,128)(2,1)S(1)}, bf16[2,4,8,128]{3,2,1,0:T(8,128)(2,1)S(1)}, u32[]{:S(2)}, u32[]{:S(2)}) collective-permute-start(bf16[2,4,8,128]{3,2,1,0:T(8,128)(2,1)S(1)} %slice.4), channel_id=1, source_target_pairs={{0,1},{1,0},{2,3},{3,2},{4,5},{5,4},{6,7},{7,6},{8,9},{9,8},{10,11... | collective-permute-start | bytes 49160 | tf_op jit(solution)/shard_map/ppermute | solution.py:17
  18.5 4.0 %collective-permute-start.6 = (f32[8,256]{1,0:T(8,128)S(1)}, f32[8,256]{1,0:T(8,128)S(1)}, u32[]{:S(2)}, u32[]{:S(2)}) collective-permute-start(f32[8,256]{1,0:T(8,128)S(1)} %get-tuple-element.11), channel_id=1, source_target_pairs={{0,4},{1,9},{2,6},{3,11},{4,0},{5,13},{6,2},{7,15},{8,12},{9,1},{1... | collective-permute-start | bytes 24584 | tf_op jit(solution)/shard_map/ppermute | solution.py:283
  18.5 4.0 %collective-permute-start.7 = (f32[8,256]{1,0:T(8,128)S(1)}, f32[8,256]{1,0:T(8,128)S(1)}, u32[]{:S(2)}, u32[]{:S(2)}) collective-permute-start(f32[8,256]{1,0:T(8,128)S(1)} %get-tuple-element.12), channel_id=1, source_target_pairs={{0,2},{1,13},{2,0},{3,15},{4,6},{5,9},{6,4},{7,11},{8,10},{9,5},{1... | collective-permute-start | bytes 24584 | tf_op jit(solution)/shard_map/ppermute | solution.py:283
  22.5 1.5 %collective-permute-start.8 = (f32[4,1,256]{2,1,0:T(1,128)S(1)}, f32[4,1,256]{2,1,0:T(1,128)S(1)}, u32[]{:S(2)}, u32[]{:S(2)}) collective-permute-start(f32[4,1,256]{2,1,0:T(1,128)S(1)} %dynamic-slice_bitcast_fusion.4), channel_id=1, source_target_pairs={{0,1},{1,0},{2,3},{3,2},{4,5},{5,4},{6,7},{7,6},{8,9},{9,8},{10,11... | collective-permute-start | bytes 12296 | tf_op jit(solution)/shard_map/ppermute | solution.py:17

commit v10 on v9

--- a/solution.py
+++ b/solution.py
@@ -88,9 +88,10 @@
     ex, feat, pb = (lax.axis_index(axis) for axis in ("ex", "feat", "pb"))
     fp_count, fp = feat_count * pb_count, feat * pb_count + pb
     ratio = ex_count // fp_count
-    others = exchange(queries, "pb", 1)
     own = sketch.reshape(1, ex_count, -1, LANES)
     own = jnp.concatenate([own, exchange(own, "pb", 1)])
+    own, queries = lax.optimization_barrier((own, queries))
+    others = exchange(queries, "pb", 1)
     line = [own]
     for k in range(1, feat_count):
         line.append(exchange(own, ("feat", "pb"), k * pb_count + 1)[::-1])

time: 24.8 us -> 24.7 us (level)
  transfers between devices with their start and end apart: 9 -> 9, of which waited for: 4 -> 4; matrix products, arithmetic and copies ran while one was open for 0% -> 0% of each run, Pallas kernels for 23% -> 10%
where the time goes in v10:
time: 24.7 us; the launch traced here: 24.6 us
  starting transfers between devices  10.1 us (41%)
  waiting for transfers between devices  6.21 us (25%)
  Pallas kernels  6.12 us (25%)
  between operations  1.48 us (6%)
  other arithmetic  0.64 us (3%)
    ppermute x2, starting transfers between devices, spread(): return lax.ppermute(block, ('ex', 'pb'), pairs)  4.39 us
    ppermute x5, starting transfers between devices, exchange(): lax.ppermute(block, axis, [(i, i ^ step) for i in range(lax.axis_size(axi...  4.14 us
    pallas_call x1, Pallas kernels, make_sketch(): pl.pallas_call(sketch_kernel, out_shape=jax.ShapeDtypeStruct((rank // 2,...  3.35 us
    ppermute x2, waiting for transfers between devices, spread(): return lax.ppermute(block, ('ex', 'pb'), pairs)  3.1 us
    ppermute x5, waiting for transfers between devices, exchange(): lax.ppermute(block, axis, [(i, i ^ step) for i in range(lax.axis_size(axi...  3.1 us
    pallas_call x1, Pallas kernels, make_gram(): pl.pallas_call(functools.partial(gram_kernel, sizes, [piece[1:] for piece...  2.38 us
    ppermute x2, starting transfers between devices, to_owners(): arrived.append(lax.ppermute(chunk, ('ex', 'feat', 'pb'), pairs))  1.58 us
    transpose x1, other arithmetic, shards(): return (gram, scores.transpose(2, 0, 1))  0.6 us
  transfers between devices with their start and end apart: 9, of which 4 were waited for; matrix products, arithmetic and copies ran while one was open for 0% of the time, Pallas kernels for 10%

profile of v10, /device:TPU:0, one launch (start us, length us, event | category | flops | bytes accessed | tf_op | source)
XLA Modules:
  0.0 24.6 jit_solution(6894158170670342301)
XLA Ops:
  0.6 0.0 copy-start
  0.6 0.0 copy-start.1
  0.7 0.0 copy-start.2
  1.4 3.4 %sketch.1 = bf16[32,128]{1,0:T(8,128)(2,1)S(1)} custom-call(bf16[128,4096]{1,0:T(8,128)(2,1)} %bitcast.30, bf16[128,7168]{1,0:T(8,128)(2,1)} %bitcast.29, bf16[64,4096]{1,0:T(8,128)(2,1)} %bitcast.32, bf16[64,7168]{1,0:T(8,128)(2,1)} %bitcast.31, f32[1,128]{1,0:T(1,128)S(1)} %compare_convert_fusion.keep_ref), custom_call_target="tpu_custom_call" | custom-call | tf_op jit(solution)/shard_map/sketch/pallas_call | solution.py:57
  4.8 0.5 %collective-permute-start = (bf16[1,4,8,128]{3,2,1,0:T(8,128)(2,1)S(1)}, bf16[1,4,8,128]{3,2,1,0:T(8,128)(2,1)S(1)}, u32[]{:S(2)}, u32[]{:S(2)}) collective-permute-start(bf16[1,4,8,128]{3,2,1,0:T(8,128)(2,1)S(1)} %bitcast.25), channel_id=1, source_target_pairs={{0,1},{1,0},{2,3},{3,2},{4,5},{5,4},{6,7},{7,6},{8,9},{9,8},{10,11... | collective-permute-start | bytes 24584 | tf_op jit(solution)/shard_map/ppermute | solution.py:17
  5.3 0.8 %collective-permute-done = bf16[1,4,8,128]{3,2,1,0:T(8,128)(2,1)S(1)} collective-permute-done((bf16[1,4,8,128]{3,2,1,0:T(8,128)(2,1)S(1)}, bf16[1,4,8,128]{3,2,1,0:T(8,128)(2,1)S(1)}, u32[]{:S(2)}, u32[]{:S(2)}) %collective-permute-start) | collective-permute-done | bytes 8224 | tf_op jit(solution)/shard_map/ppermute | solution.py:17
  6.1 0.0 copy-done
  6.1 0.3 %collective-permute-start.1 = (bf16[512,1024]{1,0:T(8,128)(2,1)S(1)}, bf16[512,1024]{1,0:T(8,128)(2,1)S(1)}, u32[]{:S(2)}, u32[]{:S(2)}) collective-permute-start(bf16[512,1024]{1,0:T(8,128)(2,1)S(1)} %copy-done), channel_id=1, source_target_pairs={{0,1},{1,0},{2,3},{3,2},{4,5},{5,4},{6,7},{7,6},{8,9},{9,8},{10,11... | collective-permute-start | bytes 3145736 | tf_op jit(solution)/shard_map/ppermute | solution.py:17
  6.5 2.6 %collective-permute-start.2 = (bf16[2,4,8,128]{3,2,1,0:T(8,128)(2,1)S(1)}, bf16[2,4,8,128]{3,2,1,0:T(8,128)(2,1)S(1)}, u32[]{:S(2)}, u32[]{:S(2)}) collective-permute-start(bf16[2,4,8,128]{3,2,1,0:T(8,128)(2,1)S(1)} %pad_maximum_fusion.2), channel_id=1, source_target_pairs={{0,3},{1,2},{2,1},{3,0},{4,7},{5,6},{6,5},{7,4},{8,11},{9,10},{10,... | collective-permute-start | bytes 49160 | tf_op jit(solution)/shard_map/ppermute | solution.py:17
  9.1 1.4 %collective-permute-done.2 = bf16[2,4,8,128]{3,2,1,0:T(8,128)(2,1)S(1)} collective-permute-done((bf16[2,4,8,128]{3,2,1,0:T(8,128)(2,1)S(1)}, bf16[2,4,8,128]{3,2,1,0:T(8,128)(2,1)S(1)}, u32[]{:S(2)}, u32[]{:S(2)}) %collective-permute-start.2) | collective-permute-done | bytes 16416 | tf_op jit(solution)/shard_map/ppermute | solution.py:17
  10.5 1.9 %collective-permute-start.3 = (bf16[3,4,8,128]{3,2,1,0:T(8,128)(2,1)S(1)}, bf16[3,4,8,128]{3,2,1,0:T(8,128)(2,1)S(1)}, u32[]{:S(2)}, u32[]{:S(2)}) collective-permute-start(bf16[3,4,8,128]{3,2,1,0:T(8,128)(2,1)S(1)} %pad_maximum_fusion.1), channel_id=1, source_target_pairs={{0,4},{1,9},{4,0},{5,13},{8,12},{9,1},{12,8},{13,5},{2,6},{3,11},{... | collective-permute-start | bytes 73736 | tf_op jit(solution)/shard_map/ppermute | solution.py:75
  12.5 2.5 %collective-permute-start.5 = (bf16[2,4,8,128]{3,2,1,0:T(8,128)(2,1)S(1)}, bf16[2,4,8,128]{3,2,1,0:T(8,128)(2,1)S(1)}, u32[]{:S(2)}, u32[]{:S(2)}) collective-permute-start(bf16[2,4,8,128]{3,2,1,0:T(8,128)(2,1)S(1)} %pad_maximum_fusion.3), channel_id=1, source_target_pairs={{0,12},{1,13},{4,8},{5,9},{8,4},{9,5},{12,0},{13,1},{2,14},{3,15},... | collective-permute-start | bytes 49160 | tf_op jit(solution)/shard_map/ppermute | solution.py:75
  14.9 0.0 collective-permute-done.3.refs_1_
  14.9 0.0 collective-permute-start.4
  15.0 3.1 %collective-permute-done.5.refs_3_ = bf16[2,4,8,128]{3,2,1,0:T(8,128)(2,1)S(1)} collective-permute-done((bf16[2,4,8,128]{3,2,1,0:T(8,128)(2,1)S(1)}, bf16[2,4,8,128]{3,2,1,0:T(8,128)(2,1)S(1)}, u32[]{:S(2)}, u32[]{:S(2)}) %collective-permute-start.5) | collective-permute-done | bytes 16416 | tf_op jit(solution)/shard_map/ppermute | solution.py:75
  18.1 0.0 collective-permute-done.4.refs_2_
  18.1 0.0 collective-permute-done.1.other_query_ref
  18.1 0.4 %scores.1 = (f32[8,256]{1,0:T(8,128)S(1)}, f32[8,256]{1,0:T(8,128)S(1)}, f32[8,256]{1,0:T(8,128)S(1)}) custom-call(bf16[512,1024]{1,0:T(8,128)(2,1)S(1)} %copy-done, bf16[512,1024]{1,0:T(8,128)(2,1)S(1)} %collective-permute-done.1.other_query_ref, bf16[4,4,8,128]{3,2,1,0:T(8,128)(2,1)S(1)} %pad_maximum_fusion.refs_0_, ...), custom_call_target="tpu_custom_call" | custom-call | tf_op jit(solution)/shard_map/scores/pallas_call | solution.py:188
  18.4 0.0 collective-permute-start.6
  18.5 1.6 %collective-permute-start.7 = (f32[8,256]{1,0:T(8,128)S(1)}, f32[8,256]{1,0:T(8,128)S(1)}, u32[]{:S(2)}, u32[]{:S(2)}) collective-permute-start(f32[8,256]{1,0:T(8,128)S(1)} %get-tuple-element.16), channel_id=1, source_target_pairs={{0,2},{1,13},{2,0},{3,15},{4,6},{5,9},{6,4},{7,11},{8,10},{9,5},{1... | collective-permute-start | bytes 24584 | tf_op jit(solution)/shard_map/ppermute | solution.py:284
  20.0 0.0 copy-done.1
  20.0 0.0 copy-done.2
  20.0 2.4 %gram.1 = (f32[1024,1024]{1,0:T(8,128)}, f32[8,256]{1,0:T(8,128)S(1)}, f32[4,1,256]{2,1,0:T(1,128)S(1)}) custom-call(f32[8,256]{1,0:T(8,128)S(1)} %get-tuple-element.12.kept_ref, s32[8,128]{1,0:T(8,128)S(1)} %bitcast.27, s32[1,4]{1,0:T(1,128)S(1)} %bitcast.28, bf16[4,4,8,128]{3,2,1,0:T(8,128)(2,1)S(1)} %pad_maximum_fusion.refs_0_, ...), custom_call_target="tpu_custom_call" | custom-call | flops 536870912 | bytes 4194304 | tf_op jit(solution)/shard_map/gram/pallas_call | solution.py:242
  22.4 0.0 collective-permute-done.6
  22.4 0.0 collective-permute-done.7
  22.5 0.7 %collective-permute-start.8 = (f32[4,1,256]{2,1,0:T(1,128)S(1)}, f32[4,1,256]{2,1,0:T(1,128)S(1)}, u32[]{:S(2)}, u32[]{:S(2)}) collective-permute-start(f32[4,1,256]{2,1,0:T(1,128)S(1)} %dynamic-slice_bitcast_fusion), channel_id=1, source_target_pairs={{0,1},{1,0},{2,3},{3,2},{4,5},{5,4},{6,7},{7,6},{8,9},{9,8},{10,11... | collective-permute-start | bytes 12296 | tf_op jit(solution)/shard_map/ppermute | solution.py:17
  23.2 0.8 %collective-permute-done.8 = f32[4,1,256]{2,1,0:T(1,128)S(1)} collective-permute-done((f32[4,1,256]{2,1,0:T(1,128)S(1)}, f32[4,1,256]{2,1,0:T(1,128)S(1)}, u32[]{:S(2)}, u32[]{:S(2)}) %collective-permute-start.8) | collective-permute-done | bytes 4128 | tf_op jit(solution)/shard_map/ppermute | solution.py:17
  24.0 0.6 %fusion.8 = f32[256,4,1]{0,2,1:T(1,128)} fusion(f32[4,1,256]{2,1,0:T(1,128)S(1)} %get-tuple-element.14, f32[4,1,256]{2,1,0:T(1,128)S(1)} %collective-permute-done.8, f32[2,4,1,256]{3,2,1,0:T(1,128)S(1)} %reshape.35, s32[]{:T(128)S(6)} %select_n.30), kind=kLoop, calls=%fused_computation.22 | loop fusion | flops 3072 | bytes 16388 | tf_op jit(solution)/shard_map/transpose | solution.py:307
  (11 shorter events, 0.1 us)
Async XLA Ops:
  0.6 5.5 %copy-start = (bf16[512,1024]{1,0:T(8,128)(2,1)S(1)}, bf16[512,1024]{1,0:T(8,128)(2,1)}, u32[]{:S(2)}) copy-start(bf16[512,1024]{1,0:T(8,128)(2,1)} %query_ref.1) | copy-start | bytes 3145732
  0.6 19.4 %copy-start.1 = (s32[1024]{0:T(1024)S(1)}, s32[1024]{0:T(1024)}, u32[]{:S(2)}) copy-start(s32[1024]{0:T(1024)} %param.15) | copy-start | bytes 12292
  0.7 19.4 %copy-start.2 = (s32[4,1]{0,1:T(1,128)S(1)}, s32[4,1]{0,1:T(1,128)}, u32[]{:S(2)}) copy-start(s32[4,1]{0,1:T(1,128)} %param.13) | copy-start | bytes 52
  4.8 1.3 %collective-permute-start = (bf16[1,4,8,128]{3,2,1,0:T(8,128)(2,1)S(1)}, bf16[1,4,8,128]{3,2,1,0:T(8,128)(2,1)S(1)}, u32[]{:S(2)}, u32[]{:S(2)}) collective-permute-start(bf16[1,4,8,128]{3,2,1,0:T(8,128)(2,1)S(1)} %bitcast.25), channel_id=1, source_target_pairs={{0,1},{1,0},{2,3},{3,2},{4,5},{5,4},{6,7},{7,6},{8,9},{9,8},{10,11... | collective-permute-start | bytes 24584 | tf_op jit(solution)/shard_map/ppermute | solution.py:17
  6.1 11.9 %collective-permute-start.1 = (bf16[512,1024]{1,0:T(8,128)(2,1)S(1)}, bf16[512,1024]{1,0:T(8,128)(2,1)S(1)}, u32[]{:S(2)}, u32[]{:S(2)}) collective-permute-start(bf16[512,1024]{1,0:T(8,128)(2,1)S(1)} %copy-done), channel_id=1, source_target_pairs={{0,1},{1,0},{2,3},{3,2},{4,5},{5,4},{6,7},{7,6},{8,9},{9,8},{10,11... | collective-permute-start | bytes 3145736 | tf_op jit(solution)/shard_map/ppermute | solution.py:17
  6.5 4.0 %collective-permute-start.2 = (bf16[2,4,8,128]{3,2,1,0:T(8,128)(2,1)S(1)}, bf16[2,4,8,128]{3,2,1,0:T(8,128)(2,1)S(1)}, u32[]{:S(2)}, u32[]{:S(2)}) collective-permute-start(bf16[2,4,8,128]{3,2,1,0:T(8,128)(2,1)S(1)} %pad_maximum_fusion.2), channel_id=1, source_target_pairs={{0,3},{1,2},{2,1},{3,0},{4,7},{5,6},{6,5},{7,4},{8,11},{9,10},{10,... | collective-permute-start | bytes 49160 | tf_op jit(solution)/shard_map/ppermute | solution.py:17
  10.5 4.4 %collective-permute-start.3 = (bf16[3,4,8,128]{3,2,1,0:T(8,128)(2,1)S(1)}, bf16[3,4,8,128]{3,2,1,0:T(8,128)(2,1)S(1)}, u32[]{:S(2)}, u32[]{:S(2)}) collective-permute-start(bf16[3,4,8,128]{3,2,1,0:T(8,128)(2,1)S(1)} %pad_maximum_fusion.1), channel_id=1, source_target_pairs={{0,4},{1,9},{4,0},{5,13},{8,12},{9,1},{12,8},{13,5},{2,6},{3,11},{... | collective-permute-start | bytes 73736 | tf_op jit(solution)/shard_map/ppermute | solution.py:75
  12.5 5.6 %collective-permute-start.5 = (bf16[2,4,8,128]{3,2,1,0:T(8,128)(2,1)S(1)}, bf16[2,4,8,128]{3,2,1,0:T(8,128)(2,1)S(1)}, u32[]{:S(2)}, u32[]{:S(2)}) collective-permute-start(bf16[2,4,8,128]{3,2,1,0:T(8,128)(2,1)S(1)} %pad_maximum_fusion.3), channel_id=1, source_target_pairs={{0,12},{1,13},{4,8},{5,9},{8,4},{9,5},{12,0},{13,1},{2,14},{3,15},... | collective-permute-start | bytes 49160 | tf_op jit(solution)/shard_map/ppermute | solution.py:75
  14.9 3.1 %collective-permute-start.4 = (bf16[2,4,8,128]{3,2,1,0:T(8,128)(2,1)S(1)}, bf16[2,4,8,128]{3,2,1,0:T(8,128)(2,1)S(1)}, u32[]{:S(2)}, u32[]{:S(2)}) collective-permute-start(bf16[2,4,8,128]{3,2,1,0:T(8,128)(2,1)S(1)} %slice.4), channel_id=1, source_target_pairs={{0,1},{1,0},{2,3},{3,2},{4,5},{5,4},{6,7},{7,6},{8,9},{9,8},{10,11... | collective-permute-start | bytes 49160 | tf_op jit(solution)/shard_map/ppermute | solution.py:17
  18.4 4.0 %collective-permute-start.6 = (f32[8,256]{1,0:T(8,128)S(1)}, f32[8,256]{1,0:T(8,128)S(1)}, u32[]{:S(2)}, u32[]{:S(2)}) collective-permute-start(f32[8,256]{1,0:T(8,128)S(1)} %get-tuple-element.15), channel_id=1, source_target_pairs={{0,4},{1,9},{2,6},{3,11},{4,0},{5,13},{6,2},{7,15},{8,12},{9,1},{1... | collective-permute-start | bytes 24584 | tf_op jit(solution)/shard_map/ppermute | solution.py:284
  18.5 4.0 %collective-permute-start.7 = (f32[8,256]{1,0:T(8,128)S(1)}, f32[8,256]{1,0:T(8,128)S(1)}, u32[]{:S(2)}, u32[]{:S(2)}) collective-permute-start(f32[8,256]{1,0:T(8,128)S(1)} %get-tuple-element.16), channel_id=1, source_target_pairs={{0,2},{1,13},{2,0},{3,15},{4,6},{5,9},{6,4},{7,11},{8,10},{9,5},{1... | collective-permute-start | bytes 24584 | tf_op jit(solution)/shard_map/ppermute | solution.py:284
  22.5 1.5 %collective-permute-start.8 = (f32[4,1,256]{2,1,0:T(1,128)S(1)}, f32[4,1,256]{2,1,0:T(1,128)S(1)}, u32[]{:S(2)}, u32[]{:S(2)}) collective-permute-start(f32[4,1,256]{2,1,0:T(1,128)S(1)} %dynamic-slice_bitcast_fusion), channel_id=1, source_target_pairs={{0,1},{1,0},{2,3},{3,2},{4,5},{5,4},{6,7},{7,6},{8,9},{9,8},{10,11... | collective-permute-start | bytes 12296 | tf_op jit(solution)/shard_map/ppermute | solution.py:17

commit v11 on v10

--- a/solution.py
+++ b/solution.py
@@ -164,12 +164,14 @@
             high = wide.astype(jnp.bfloat16)
             low = (wide - high.astype(jnp.float32)).astype(jnp.bfloat16)
             both = jnp.concatenate([high, low], axis=0)
-            products = lax.dot_general(
-                both, queries[...], NT, preferred_element_type=jnp.float32
-            )
-            result = products[:mine] + products[mine:]
             for t in range(half):
-                chunks[t] = result[:, t * width : (t + 1) * width]
+                products = lax.dot_general(
+                    both,
+                    queries[t * width : (t + 1) * width, :],
+                    NT,
+                    preferred_element_type=jnp.float32,
+                )
+                chunks[t] = products[:mine] + products[mine:]
 
     shift = near.astype(jnp.int32)
     for i in range(half - 1):

time: 24.7 us -> 24.7 us (level)
  no operation moved by 1% of the time
where the time goes in v11:
time: 24.7 us; the launch traced here: 24.6 us
  starting transfers between devices  10.1 us (41%)
  waiting for transfers between devices  6.21 us (25%)
  Pallas kernels  6.12 us (25%)
  between operations  1.48 us (6%)
  other arithmetic  0.64 us (3%)
    ppermute x2, starting transfers between devices, spread(): return lax.ppermute(block, ('ex', 'pb'), pairs)  4.39 us
    ppermute x5, starting transfers between devices, exchange(): lax.ppermute(block, axis, [(i, i ^ step) for i in range(lax.axis_size(axi...  4.14 us
    pallas_call x1, Pallas kernels, make_sketch(): pl.pallas_call(sketch_kernel, out_shape=jax.ShapeDtypeStruct((rank // 2,...  3.35 us
    ppermute x2, waiting for transfers between devices, spread(): return lax.ppermute(block, ('ex', 'pb'), pairs)  3.1 us
    ppermute x5, waiting for transfers between devices, exchange(): lax.ppermute(block, axis, [(i, i ^ step) for i in range(lax.axis_size(axi...  3.1 us
    pallas_call x1, Pallas kernels, make_gram(): pl.pallas_call(functools.partial(gram_kernel, sizes, [piece[1:] for piece...  2.38 us
    ppermute x2, starting transfers between devices, to_owners(): arrived.append(lax.ppermute(chunk, ('ex', 'feat', 'pb'), pairs))  1.58 us
    transpose x1, other arithmetic, shards(): return (gram, scores.transpose(2, 0, 1))  0.6 us
  transfers between devices with their start and end apart: 9, of which 4 were waited for; matrix products, arithmetic and copies ran while one was open for 0% of the time, Pallas kernels for 10%

profile of v11, /device:TPU:0, one launch (start us, length us, event | category | flops | bytes accessed | tf_op | source)
XLA Modules:
  0.0 24.6 jit_solution(6894158170670342301)
XLA Ops:
  0.6 0.0 copy-start
  0.6 0.0 copy-start.1
  0.7 0.0 copy-start.2
  1.4 3.4 %sketch.1 = bf16[32,128]{1,0:T(8,128)(2,1)S(1)} custom-call(bf16[128,4096]{1,0:T(8,128)(2,1)} %bitcast.30, bf16[128,7168]{1,0:T(8,128)(2,1)} %bitcast.29, bf16[64,4096]{1,0:T(8,128)(2,1)} %bitcast.32, bf16[64,7168]{1,0:T(8,128)(2,1)} %bitcast.31, f32[1,128]{1,0:T(1,128)S(1)} %compare_convert_fusion.keep_ref), custom_call_target="tpu_custom_call" | custom-call | tf_op jit(solution)/shard_map/sketch/pallas_call | solution.py:57
  4.8 0.5 %collective-permute-start = (bf16[1,4,8,128]{3,2,1,0:T(8,128)(2,1)S(1)}, bf16[1,4,8,128]{3,2,1,0:T(8,128)(2,1)S(1)}, u32[]{:S(2)}, u32[]{:S(2)}) collective-permute-start(bf16[1,4,8,128]{3,2,1,0:T(8,128)(2,1)S(1)} %bitcast.25), channel_id=1, source_target_pairs={{0,1},{1,0},{2,3},{3,2},{4,5},{5,4},{6,7},{7,6},{8,9},{9,8},{10,11... | collective-permute-start | bytes 24584 | tf_op jit(solution)/shard_map/ppermute | solution.py:17
  5.3 0.8 %collective-permute-done = bf16[1,4,8,128]{3,2,1,0:T(8,128)(2,1)S(1)} collective-permute-done((bf16[1,4,8,128]{3,2,1,0:T(8,128)(2,1)S(1)}, bf16[1,4,8,128]{3,2,1,0:T(8,128)(2,1)S(1)}, u32[]{:S(2)}, u32[]{:S(2)}) %collective-permute-start) | collective-permute-done | bytes 8224 | tf_op jit(solution)/shard_map/ppermute | solution.py:17
  6.1 0.0 copy-done
  6.1 0.3 %collective-permute-start.1 = (bf16[512,1024]{1,0:T(8,128)(2,1)S(1)}, bf16[512,1024]{1,0:T(8,128)(2,1)S(1)}, u32[]{:S(2)}, u32[]{:S(2)}) collective-permute-start(bf16[512,1024]{1,0:T(8,128)(2,1)S(1)} %copy-done), channel_id=1, source_target_pairs={{0,1},{1,0},{2,3},{3,2},{4,5},{5,4},{6,7},{7,6},{8,9},{9,8},{10,11... | collective-permute-start | bytes 3145736 | tf_op jit(solution)/shard_map/ppermute | solution.py:17
  6.5 2.6 %collective-permute-start.2 = (bf16[2,4,8,128]{3,2,1,0:T(8,128)(2,1)S(1)}, bf16[2,4,8,128]{3,2,1,0:T(8,128)(2,1)S(1)}, u32[]{:S(2)}, u32[]{:S(2)}) collective-permute-start(bf16[2,4,8,128]{3,2,1,0:T(8,128)(2,1)S(1)} %pad_maximum_fusion.2), channel_id=1, source_target_pairs={{0,3},{1,2},{2,1},{3,0},{4,7},{5,6},{6,5},{7,4},{8,11},{9,10},{10,... | collective-permute-start | bytes 49160 | tf_op jit(solution)/shard_map/ppermute | solution.py:17
  9.1 1.4 %collective-permute-done.2 = bf16[2,4,8,128]{3,2,1,0:T(8,128)(2,1)S(1)} collective-permute-done((bf16[2,4,8,128]{3,2,1,0:T(8,128)(2,1)S(1)}, bf16[2,4,8,128]{3,2,1,0:T(8,128)(2,1)S(1)}, u32[]{:S(2)}, u32[]{:S(2)}) %collective-permute-start.2) | collective-permute-done | bytes 16416 | tf_op jit(solution)/shard_map/ppermute | solution.py:17
  10.5 1.9 %collective-permute-start.3 = (bf16[3,4,8,128]{3,2,1,0:T(8,128)(2,1)S(1)}, bf16[3,4,8,128]{3,2,1,0:T(8,128)(2,1)S(1)}, u32[]{:S(2)}, u32[]{:S(2)}) collective-permute-start(bf16[3,4,8,128]{3,2,1,0:T(8,128)(2,1)S(1)} %pad_maximum_fusion.1), channel_id=1, source_target_pairs={{0,4},{1,9},{4,0},{5,13},{8,12},{9,1},{12,8},{13,5},{2,6},{3,11},{... | collective-permute-start | bytes 73736 | tf_op jit(solution)/shard_map/ppermute | solution.py:75
  12.5 2.5 %collective-permute-start.5 = (bf16[2,4,8,128]{3,2,1,0:T(8,128)(2,1)S(1)}, bf16[2,4,8,128]{3,2,1,0:T(8,128)(2,1)S(1)}, u32[]{:S(2)}, u32[]{:S(2)}) collective-permute-start(bf16[2,4,8,128]{3,2,1,0:T(8,128)(2,1)S(1)} %pad_maximum_fusion.3), channel_id=1, source_target_pairs={{0,12},{1,13},{4,8},{5,9},{8,4},{9,5},{12,0},{13,1},{2,14},{3,15},... | collective-permute-start | bytes 49160 | tf_op jit(solution)/shard_map/ppermute | solution.py:75
  14.9 0.0 collective-permute-done.3.refs_1_
  14.9 0.0 collective-permute-start.4
  15.0 3.1 %collective-permute-done.5.refs_3_ = bf16[2,4,8,128]{3,2,1,0:T(8,128)(2,1)S(1)} collective-permute-done((bf16[2,4,8,128]{3,2,1,0:T(8,128)(2,1)S(1)}, bf16[2,4,8,128]{3,2,1,0:T(8,128)(2,1)S(1)}, u32[]{:S(2)}, u32[]{:S(2)}) %collective-permute-start.5) | collective-permute-done | bytes 16416 | tf_op jit(solution)/shard_map/ppermute | solution.py:75
  18.1 0.0 collective-permute-done.4.refs_2_
  18.1 0.0 collective-permute-done.1.other_query_ref
  18.1 0.4 %scores.1 = (f32[8,256]{1,0:T(8,128)S(1)}, f32[8,256]{1,0:T(8,128)S(1)}, f32[8,256]{1,0:T(8,128)S(1)}) custom-call(bf16[512,1024]{1,0:T(8,128)(2,1)S(1)} %copy-done, bf16[512,1024]{1,0:T(8,128)(2,1)S(1)} %collective-permute-done.1.other_query_ref, bf16[4,4,8,128]{3,2,1,0:T(8,128)(2,1)S(1)} %pad_maximum_fusion.refs_0_, ...), custom_call_target="tpu_custom_call" | custom-call | tf_op jit(solution)/shard_map/scores/pallas_call | solution.py:190
  18.4 0.0 collective-permute-start.6
  18.5 1.6 %collective-permute-start.7 = (f32[8,256]{1,0:T(8,128)S(1)}, f32[8,256]{1,0:T(8,128)S(1)}, u32[]{:S(2)}, u32[]{:S(2)}) collective-permute-start(f32[8,256]{1,0:T(8,128)S(1)} %get-tuple-element.16), channel_id=1, source_target_pairs={{0,2},{1,13},{2,0},{3,15},{4,6},{5,9},{6,4},{7,11},{8,10},{9,5},{1... | collective-permute-start | bytes 24584 | tf_op jit(solution)/shard_map/ppermute | solution.py:286
  20.0 0.0 copy-done.1
  20.0 0.0 copy-done.2
  20.0 2.4 %gram.1 = (f32[1024,1024]{1,0:T(8,128)}, f32[8,256]{1,0:T(8,128)S(1)}, f32[4,1,256]{2,1,0:T(1,128)S(1)}) custom-call(f32[8,256]{1,0:T(8,128)S(1)} %get-tuple-element.12.kept_ref, s32[8,128]{1,0:T(8,128)S(1)} %bitcast.27, s32[1,4]{1,0:T(1,128)S(1)} %bitcast.28, bf16[4,4,8,128]{3,2,1,0:T(8,128)(2,1)S(1)} %pad_maximum_fusion.refs_0_, ...), custom_call_target="tpu_custom_call" | custom-call | flops 536870912 | bytes 4194304 | tf_op jit(solution)/shard_map/gram/pallas_call | solution.py:244
  22.4 0.0 collective-permute-done.6
  22.4 0.0 collective-permute-done.7
  22.5 0.7 %collective-permute-start.8 = (f32[4,1,256]{2,1,0:T(1,128)S(1)}, f32[4,1,256]{2,1,0:T(1,128)S(1)}, u32[]{:S(2)}, u32[]{:S(2)}) collective-permute-start(f32[4,1,256]{2,1,0:T(1,128)S(1)} %dynamic-slice_bitcast_fusion), channel_id=1, source_target_pairs={{0,1},{1,0},{2,3},{3,2},{4,5},{5,4},{6,7},{7,6},{8,9},{9,8},{10,11... | collective-permute-start | bytes 12296 | tf_op jit(solution)/shard_map/ppermute | solution.py:17
  23.2 0.8 %collective-permute-done.8 = f32[4,1,256]{2,1,0:T(1,128)S(1)} collective-permute-done((f32[4,1,256]{2,1,0:T(1,128)S(1)}, f32[4,1,256]{2,1,0:T(1,128)S(1)}, u32[]{:S(2)}, u32[]{:S(2)}) %collective-permute-start.8) | collective-permute-done | bytes 4128 | tf_op jit(solution)/shard_map/ppermute | solution.py:17
  24.0 0.6 %fusion.8 = f32[256,4,1]{0,2,1:T(1,128)} fusion(f32[4,1,256]{2,1,0:T(1,128)S(1)} %get-tuple-element.14, f32[4,1,256]{2,1,0:T(1,128)S(1)} %collective-permute-done.8, f32[2,4,1,256]{3,2,1,0:T(1,128)S(1)} %reshape.35, s32[]{:T(128)S(6)} %select_n.30), kind=kLoop, calls=%fused_computation.22 | loop fusion | flops 3072 | bytes 16388 | tf_op jit(solution)/shard_map/transpose | solution.py:309
  (11 shorter events, 0.1 us)
Async XLA Ops:
  0.6 5.5 %copy-start = (bf16[512,1024]{1,0:T(8,128)(2,1)S(1)}, bf16[512,1024]{1,0:T(8,128)(2,1)}, u32[]{:S(2)}) copy-start(bf16[512,1024]{1,0:T(8,128)(2,1)} %query_ref.1) | copy-start | bytes 3145732
  0.6 19.4 %copy-start.1 = (s32[1024]{0:T(1024)S(1)}, s32[1024]{0:T(1024)}, u32[]{:S(2)}) copy-start(s32[1024]{0:T(1024)} %param.15) | copy-start | bytes 12292
  0.7 19.4 %copy-start.2 = (s32[4,1]{0,1:T(1,128)S(1)}, s32[4,1]{0,1:T(1,128)}, u32[]{:S(2)}) copy-start(s32[4,1]{0,1:T(1,128)} %param.13) | copy-start | bytes 52
  4.8 1.3 %collective-permute-start = (bf16[1,4,8,128]{3,2,1,0:T(8,128)(2,1)S(1)}, bf16[1,4,8,128]{3,2,1,0:T(8,128)(2,1)S(1)}, u32[]{:S(2)}, u32[]{:S(2)}) collective-permute-start(bf16[1,4,8,128]{3,2,1,0:T(8,128)(2,1)S(1)} %bitcast.25), channel_id=1, source_target_pairs={{0,1},{1,0},{2,3},{3,2},{4,5},{5,4},{6,7},{7,6},{8,9},{9,8},{10,11... | collective-permute-start | bytes 24584 | tf_op jit(solution)/shard_map/ppermute | solution.py:17
  6.1 11.9 %collective-permute-start.1 = (bf16[512,1024]{1,0:T(8,128)(2,1)S(1)}, bf16[512,1024]{1,0:T(8,128)(2,1)S(1)}, u32[]{:S(2)}, u32[]{:S(2)}) collective-permute-start(bf16[512,1024]{1,0:T(8,128)(2,1)S(1)} %copy-done), channel_id=1, source_target_pairs={{0,1},{1,0},{2,3},{3,2},{4,5},{5,4},{6,7},{7,6},{8,9},{9,8},{10,11... | collective-permute-start | bytes 3145736 | tf_op jit(solution)/shard_map/ppermute | solution.py:17
  6.5 4.0 %collective-permute-start.2 = (bf16[2,4,8,128]{3,2,1,0:T(8,128)(2,1)S(1)}, bf16[2,4,8,128]{3,2,1,0:T(8,128)(2,1)S(1)}, u32[]{:S(2)}, u32[]{:S(2)}) collective-permute-start(bf16[2,4,8,128]{3,2,1,0:T(8,128)(2,1)S(1)} %pad_maximum_fusion.2), channel_id=1, source_target_pairs={{0,3},{1,2},{2,1},{3,0},{4,7},{5,6},{6,5},{7,4},{8,11},{9,10},{10,... | collective-permute-start | bytes 49160 | tf_op jit(solution)/shard_map/ppermute | solution.py:17
  10.5 4.4 %collective-permute-start.3 = (bf16[3,4,8,128]{3,2,1,0:T(8,128)(2,1)S(1)}, bf16[3,4,8,128]{3,2,1,0:T(8,128)(2,1)S(1)}, u32[]{:S(2)}, u32[]{:S(2)}) collective-permute-start(bf16[3,4,8,128]{3,2,1,0:T(8,128)(2,1)S(1)} %pad_maximum_fusion.1), channel_id=1, source_target_pairs={{0,4},{1,9},{4,0},{5,13},{8,12},{9,1},{12,8},{13,5},{2,6},{3,11},{... | collective-permute-start | bytes 73736 | tf_op jit(solution)/shard_map/ppermute | solution.py:75
  12.5 5.6 %collective-permute-start.5 = (bf16[2,4,8,128]{3,2,1,0:T(8,128)(2,1)S(1)}, bf16[2,4,8,128]{3,2,1,0:T(8,128)(2,1)S(1)}, u32[]{:S(2)}, u32[]{:S(2)}) collective-permute-start(bf16[2,4,8,128]{3,2,1,0:T(8,128)(2,1)S(1)} %pad_maximum_fusion.3), channel_id=1, source_target_pairs={{0,12},{1,13},{4,8},{5,9},{8,4},{9,5},{12,0},{13,1},{2,14},{3,15},... | collective-permute-start | bytes 49160 | tf_op jit(solution)/shard_map/ppermute | solution.py:75
  14.9 3.1 %collective-permute-start.4 = (bf16[2,4,8,128]{3,2,1,0:T(8,128)(2,1)S(1)}, bf16[2,4,8,128]{3,2,1,0:T(8,128)(2,1)S(1)}, u32[]{:S(2)}, u32[]{:S(2)}) collective-permute-start(bf16[2,4,8,128]{3,2,1,0:T(8,128)(2,1)S(1)} %slice.4), channel_id=1, source_target_pairs={{0,1},{1,0},{2,3},{3,2},{4,5},{5,4},{6,7},{7,6},{8,9},{9,8},{10,11... | collective-permute-start | bytes 49160 | tf_op jit(solution)/shard_map/ppermute | solution.py:17
  18.4 4.0 %collective-permute-start.6 = (f32[8,256]{1,0:T(8,128)S(1)}, f32[8,256]{1,0:T(8,128)S(1)}, u32[]{:S(2)}, u32[]{:S(2)}) collective-permute-start(f32[8,256]{1,0:T(8,128)S(1)} %get-tuple-element.15), channel_id=1, source_target_pairs={{0,4},{1,9},{2,6},{3,11},{4,0},{5,13},{6,2},{7,15},{8,12},{9,1},{1... | collective-permute-start | bytes 24584 | tf_op jit(solution)/shard_map/ppermute | solution.py:286
  18.5 4.0 %collective-permute-start.7 = (f32[8,256]{1,0:T(8,128)S(1)}, f32[8,256]{1,0:T(8,128)S(1)}, u32[]{:S(2)}, u32[]{:S(2)}) collective-permute-start(f32[8,256]{1,0:T(8,128)S(1)} %get-tuple-element.16), channel_id=1, source_target_pairs={{0,2},{1,13},{2,0},{3,15},{4,6},{5,9},{6,4},{7,11},{8,10},{9,5},{1... | collective-permute-start | bytes 24584 | tf_op jit(solution)/shard_map/ppermute | solution.py:286
  22.5 1.5 %collective-permute-start.8 = (f32[4,1,256]{2,1,0:T(1,128)S(1)}, f32[4,1,256]{2,1,0:T(1,128)S(1)}, u32[]{:S(2)}, u32[]{:S(2)}) collective-permute-start(f32[4,1,256]{2,1,0:T(1,128)S(1)} %dynamic-slice_bitcast_fusion), channel_id=1, source_target_pairs={{0,1},{1,0},{2,3},{3,2},{4,5},{5,4},{6,7},{7,6},{8,9},{9,8},{10,11... | collective-permute-start | bytes 12296 | tf_op jit(solution)/shard_map/ppermute | solution.py:17

commit v12 on v10

--- a/solution.py
+++ b/solution.py
@@ -21,22 +21,27 @@
     acts_hbm, grads_hbm, act_proj_hbm, grad_proj_hbm, keep_ref, out_ref,
     acts, grads, act_proj, grad_proj, turned, sems,
 ):
-    sources = (act_proj_hbm, acts_hbm, grad_proj_hbm, grads_hbm)
-    targets = (act_proj, acts, grad_proj, grads)
+    rows = grads.shape[0] // 2
+    parts = [pl.ds(c * rows, rows) for c in range(2)]
+    sources = (act_proj_hbm, acts_hbm, grad_proj_hbm, *(grads_hbm.at[part, :] for part in parts))
+    targets = (act_proj, acts, grad_proj, *(grads.at[part, :] for part in parts))
     copies = [
         pltpu.make_async_copy(s, t, sems.at[i]) for i, (s, t) in enumerate(zip(sources, targets))
     ]
-    for copy, priority in zip(copies, (0, 0, 1, 0)):
+    for copy, priority in zip(copies, (0, 0, 0, 0, 0)):
         copy.start(priority=priority)
     for copy in copies[:2]:
         copy.wait()
     act_sum = lax.dot_general(acts[...], act_proj[...], NT, preferred_element_type=jnp.float32)
     act_low = act_sum.astype(jnp.bfloat16)
-    for copy in copies[2:]:
+    copies[2].wait()
+    rank, seq_len = act_proj.shape[0], grads.shape[0]
+    for part, copy in zip(parts, copies[3:]):
         copy.wait()
-    grad_sum = lax.dot_general(grad_proj[...], grads[...], NT, preferred_element_type=jnp.float32)
-    rank, seq_len = grad_sum.shape
-    turned[pl.ds(0, rank), :] = grad_sum * keep_ref[...]
+        grad_sum = lax.dot_general(
+            grad_proj[...], grads[part, :], NT, preferred_element_type=jnp.float32
+        )
+        turned[pl.ds(0, rank), part] = grad_sum * keep_ref[:, part]
     halves = [
         jnp.dot(
             turned[pl.ds(side, rank // 2, stride=2), :].astype(jnp.bfloat16),
@@ -60,7 +65,7 @@
         in_specs=[pl.BlockSpec(memory_space=pl.ANY)] * 4 + [vmem],
         out_specs=vmem,
         scratch_shapes=[pltpu.VMEM(x.shape, x.dtype) for x in operands]
-        + [pltpu.VMEM((rank + 8, seq_len), jnp.float32), pltpu.SemaphoreType.DMA((4,))],
+        + [pltpu.VMEM((rank + 8, seq_len), jnp.float32), pltpu.SemaphoreType.DMA((5,))],
         compiler_params=pltpu.CompilerParams(vmem_limit_bytes=16 * 2**20),
         name="sketch",
     )(*[pltpu.with_memory_space_constraint(x, pltpu.HBM) for x in operands], keep[None])

time: 24.7 us -> 24.8 us (level)
  no operation moved by 1% of the time
where the time goes in v12:
time: 24.8 us; the launch traced here: 24.7 us
  starting transfers between devices  10.1 us (41%)
  waiting for transfers between devices  6.21 us (25%)
  Pallas kernels  6.2 us (25%)
  between operations  1.48 us (6%)
  other arithmetic  0.64 us (3%)
    ppermute x2, starting transfers between devices, spread(): return lax.ppermute(block, ('ex', 'pb'), pairs)  4.4 us
    ppermute x5, starting transfers between devices, exchange(): lax.ppermute(block, axis, [(i, i ^ step) for i in range(lax.axis_size(axi...  4.15 us
    pallas_call x1, Pallas kernels, make_sketch(): pl.pallas_call(sketch_kernel, out_shape=jax.ShapeDtypeStruct((rank // 2,...  3.43 us
    ppermute x2, waiting for transfers between devices, spread(): return lax.ppermute(block, ('ex', 'pb'), pairs)  3.1 us
    ppermute x5, waiting for transfers between devices, exchange(): lax.ppermute(block, axis, [(i, i ^ step) for i in range(lax.axis_size(axi...  3.1 us
    pallas_call x1, Pallas kernels, make_gram(): pl.pallas_call(functools.partial(gram_kernel, sizes, [piece[1:] for piece...  2.38 us
    ppermute x2, starting transfers between devices, to_owners(): arrived.append(lax.ppermute(chunk, ('ex', 'feat', 'pb'), pairs))  1.57 us
    transpose x1, other arithmetic, shards(): return (gram, scores.transpose(2, 0, 1))  0.6 us
  transfers between devices with their start and end apart: 9, of which 4 were waited for; matrix products, arithmetic and copies ran while one was open for 0% of the time, Pallas kernels for 10%

profile of v12, /device:TPU:0, one launch (start us, length us, event | category | flops | bytes accessed | tf_op | source)
XLA Modules:
  0.0 24.7 jit_solution(9382091796808522031)
XLA Ops:
  0.6 0.0 copy-start
  0.6 0.0 copy-start.1
  0.7 0.0 copy-start.2
  1.4 3.4 %sketch.1 = bf16[32,128]{1,0:T(8,128)(2,1)S(1)} custom-call(bf16[128,4096]{1,0:T(8,128)(2,1)} %bitcast.30, bf16[128,7168]{1,0:T(8,128)(2,1)} %bitcast.29, bf16[64,4096]{1,0:T(8,128)(2,1)} %bitcast.32, bf16[64,7168]{1,0:T(8,128)(2,1)} %bitcast.31, f32[1,128]{1,0:T(1,128)S(1)} %compare_convert_fusion.keep_ref), custom_call_target="tpu_custom_call" | custom-call | tf_op jit(solution)/shard_map/sketch/pallas_call | solution.py:62
  4.8 0.5 %collective-permute-start = (bf16[1,4,8,128]{3,2,1,0:T(8,128)(2,1)S(1)}, bf16[1,4,8,128]{3,2,1,0:T(8,128)(2,1)S(1)}, u32[]{:S(2)}, u32[]{:S(2)}) collective-permute-start(bf16[1,4,8,128]{3,2,1,0:T(8,128)(2,1)S(1)} %bitcast.25), channel_id=1, source_target_pairs={{0,1},{1,0},{2,3},{3,2},{4,5},{5,4},{6,7},{7,6},{8,9},{9,8},{10,11... | collective-permute-start | bytes 24584 | tf_op jit(solution)/shard_map/ppermute | solution.py:17
  5.4 0.8 %collective-permute-done = bf16[1,4,8,128]{3,2,1,0:T(8,128)(2,1)S(1)} collective-permute-done((bf16[1,4,8,128]{3,2,1,0:T(8,128)(2,1)S(1)}, bf16[1,4,8,128]{3,2,1,0:T(8,128)(2,1)S(1)}, u32[]{:S(2)}, u32[]{:S(2)}) %collective-permute-start) | collective-permute-done | bytes 8224 | tf_op jit(solution)/shard_map/ppermute | solution.py:17
  6.2 0.0 copy-done
  6.2 0.3 %collective-permute-start.1 = (bf16[512,1024]{1,0:T(8,128)(2,1)S(1)}, bf16[512,1024]{1,0:T(8,128)(2,1)S(1)}, u32[]{:S(2)}, u32[]{:S(2)}) collective-permute-start(bf16[512,1024]{1,0:T(8,128)(2,1)S(1)} %copy-done), channel_id=1, source_target_pairs={{0,1},{1,0},{2,3},{3,2},{4,5},{5,4},{6,7},{7,6},{8,9},{9,8},{10,11... | collective-permute-start | bytes 3145736 | tf_op jit(solution)/shard_map/ppermute | solution.py:17
  6.5 2.6 %collective-permute-start.2 = (bf16[2,4,8,128]{3,2,1,0:T(8,128)(2,1)S(1)}, bf16[2,4,8,128]{3,2,1,0:T(8,128)(2,1)S(1)}, u32[]{:S(2)}, u32[]{:S(2)}) collective-permute-start(bf16[2,4,8,128]{3,2,1,0:T(8,128)(2,1)S(1)} %pad_maximum_fusion.2), channel_id=1, source_target_pairs={{0,3},{1,2},{2,1},{3,0},{4,7},{5,6},{6,5},{7,4},{8,11},{9,10},{10,... | collective-permute-start | bytes 49160 | tf_op jit(solution)/shard_map/ppermute | solution.py:17
  9.1 1.4 %collective-permute-done.2 = bf16[2,4,8,128]{3,2,1,0:T(8,128)(2,1)S(1)} collective-permute-done((bf16[2,4,8,128]{3,2,1,0:T(8,128)(2,1)S(1)}, bf16[2,4,8,128]{3,2,1,0:T(8,128)(2,1)S(1)}, u32[]{:S(2)}, u32[]{:S(2)}) %collective-permute-start.2) | collective-permute-done | bytes 16416 | tf_op jit(solution)/shard_map/ppermute | solution.py:17
  10.6 1.9 %collective-permute-start.3 = (bf16[3,4,8,128]{3,2,1,0:T(8,128)(2,1)S(1)}, bf16[3,4,8,128]{3,2,1,0:T(8,128)(2,1)S(1)}, u32[]{:S(2)}, u32[]{:S(2)}) collective-permute-start(bf16[3,4,8,128]{3,2,1,0:T(8,128)(2,1)S(1)} %pad_maximum_fusion.1), channel_id=1, source_target_pairs={{0,4},{1,9},{4,0},{5,13},{8,12},{9,1},{12,8},{13,5},{2,6},{3,11},{... | collective-permute-start | bytes 73736 | tf_op jit(solution)/shard_map/ppermute | solution.py:80
  12.5 2.5 %collective-permute-start.5 = (bf16[2,4,8,128]{3,2,1,0:T(8,128)(2,1)S(1)}, bf16[2,4,8,128]{3,2,1,0:T(8,128)(2,1)S(1)}, u32[]{:S(2)}, u32[]{:S(2)}) collective-permute-start(bf16[2,4,8,128]{3,2,1,0:T(8,128)(2,1)S(1)} %pad_maximum_fusion.3), channel_id=1, source_target_pairs={{0,12},{1,13},{4,8},{5,9},{8,4},{9,5},{12,0},{13,1},{2,14},{3,15},... | collective-permute-start | bytes 49160 | tf_op jit(solution)/shard_map/ppermute | solution.py:80
  15.0 0.0 collective-permute-done.3.refs_1_
  15.0 0.0 collective-permute-start.4
  15.0 3.1 %collective-permute-done.5.refs_3_ = bf16[2,4,8,128]{3,2,1,0:T(8,128)(2,1)S(1)} collective-permute-done((bf16[2,4,8,128]{3,2,1,0:T(8,128)(2,1)S(1)}, bf16[2,4,8,128]{3,2,1,0:T(8,128)(2,1)S(1)}, u32[]{:S(2)}, u32[]{:S(2)}) %collective-permute-start.5) | collective-permute-done | bytes 16416 | tf_op jit(solution)/shard_map/ppermute | solution.py:80
  18.1 0.0 collective-permute-done.4.refs_2_
  18.2 0.0 collective-permute-done.1.other_query_ref
  18.2 0.4 %scores.1 = (f32[8,256]{1,0:T(8,128)S(1)}, f32[8,256]{1,0:T(8,128)S(1)}, f32[8,256]{1,0:T(8,128)S(1)}) custom-call(bf16[512,1024]{1,0:T(8,128)(2,1)S(1)} %copy-done, bf16[512,1024]{1,0:T(8,128)(2,1)S(1)} %collective-permute-done.1.other_query_ref, bf16[4,4,8,128]{3,2,1,0:T(8,128)(2,1)S(1)} %pad_maximum_fusion.refs_0_, ...), custom_call_target="tpu_custom_call" | custom-call | tf_op jit(solution)/shard_map/scores/pallas_call | solution.py:193
  18.5 0.0 collective-permute-start.6
  18.6 1.6 %collective-permute-start.7 = (f32[8,256]{1,0:T(8,128)S(1)}, f32[8,256]{1,0:T(8,128)S(1)}, u32[]{:S(2)}, u32[]{:S(2)}) collective-permute-start(f32[8,256]{1,0:T(8,128)S(1)} %get-tuple-element.16), channel_id=1, source_target_pairs={{0,2},{1,13},{2,0},{3,15},{4,6},{5,9},{6,4},{7,11},{8,10},{9,5},{1... | collective-permute-start | bytes 24584 | tf_op jit(solution)/shard_map/ppermute | solution.py:289
  20.1 0.0 copy-done.1
  20.1 0.0 copy-done.2
  20.1 2.4 %gram.1 = (f32[1024,1024]{1,0:T(8,128)}, f32[8,256]{1,0:T(8,128)S(1)}, f32[4,1,256]{2,1,0:T(1,128)S(1)}) custom-call(f32[8,256]{1,0:T(8,128)S(1)} %get-tuple-element.12.kept_ref, s32[8,128]{1,0:T(8,128)S(1)} %bitcast.27, s32[1,4]{1,0:T(1,128)S(1)} %bitcast.28, bf16[4,4,8,128]{3,2,1,0:T(8,128)(2,1)S(1)} %pad_maximum_fusion.refs_0_, ...), custom_call_target="tpu_custom_call" | custom-call | flops 536870912 | bytes 4194304 | tf_op jit(solution)/shard_map/gram/pallas_call | solution.py:247
  22.5 0.0 collective-permute-done.6
  22.5 0.0 collective-permute-done.7
  22.6 0.7 %collective-permute-start.8 = (f32[4,1,256]{2,1,0:T(1,128)S(1)}, f32[4,1,256]{2,1,0:T(1,128)S(1)}, u32[]{:S(2)}, u32[]{:S(2)}) collective-permute-start(f32[4,1,256]{2,1,0:T(1,128)S(1)} %dynamic-slice_bitcast_fusion), channel_id=1, source_target_pairs={{0,1},{1,0},{2,3},{3,2},{4,5},{5,4},{6,7},{7,6},{8,9},{9,8},{10,11... | collective-permute-start | bytes 12296 | tf_op jit(solution)/shard_map/ppermute | solution.py:17
  23.3 0.8 %collective-permute-done.8 = f32[4,1,256]{2,1,0:T(1,128)S(1)} collective-permute-done((f32[4,1,256]{2,1,0:T(1,128)S(1)}, f32[4,1,256]{2,1,0:T(1,128)S(1)}, u32[]{:S(2)}, u32[]{:S(2)}) %collective-permute-start.8) | collective-permute-done | bytes 4128 | tf_op jit(solution)/shard_map/ppermute | solution.py:17
  24.1 0.6 %fusion.8 = f32[256,4,1]{0,2,1:T(1,128)} fusion(f32[4,1,256]{2,1,0:T(1,128)S(1)} %get-tuple-element.14, f32[4,1,256]{2,1,0:T(1,128)S(1)} %collective-permute-done.8, f32[2,4,1,256]{3,2,1,0:T(1,128)S(1)} %reshape.35, s32[]{:T(128)S(6)} %select_n.30), kind=kLoop, calls=%fused_computation.22 | loop fusion | flops 3072 | bytes 16388 | tf_op jit(solution)/shard_map/transpose | solution.py:312
  (11 shorter events, 0.1 us)
Async XLA Ops:
  0.6 5.6 %copy-start = (bf16[512,1024]{1,0:T(8,128)(2,1)S(1)}, bf16[512,1024]{1,0:T(8,128)(2,1)}, u32[]{:S(2)}) copy-start(bf16[512,1024]{1,0:T(8,128)(2,1)} %query_ref.1) | copy-start | bytes 3145732
  0.6 19.5 %copy-start.1 = (s32[1024]{0:T(1024)S(1)}, s32[1024]{0:T(1024)}, u32[]{:S(2)}) copy-start(s32[1024]{0:T(1024)} %param.15) | copy-start | bytes 12292
  0.7 19.5 %copy-start.2 = (s32[4,1]{0,1:T(1,128)S(1)}, s32[4,1]{0,1:T(1,128)}, u32[]{:S(2)}) copy-start(s32[4,1]{0,1:T(1,128)} %param.13) | copy-start | bytes 52
  4.8 1.4 %collective-permute-start = (bf16[1,4,8,128]{3,2,1,0:T(8,128)(2,1)S(1)}, bf16[1,4,8,128]{3,2,1,0:T(8,128)(2,1)S(1)}, u32[]{:S(2)}, u32[]{:S(2)}) collective-permute-start(bf16[1,4,8,128]{3,2,1,0:T(8,128)(2,1)S(1)} %bitcast.25), channel_id=1, source_target_pairs={{0,1},{1,0},{2,3},{3,2},{4,5},{5,4},{6,7},{7,6},{8,9},{9,8},{10,11... | collective-permute-start | bytes 24584 | tf_op jit(solution)/shard_map/ppermute | solution.py:17
  6.2 11.9 %collective-permute-start.1 = (bf16[512,1024]{1,0:T(8,128)(2,1)S(1)}, bf16[512,1024]{1,0:T(8,128)(2,1)S(1)}, u32[]{:S(2)}, u32[]{:S(2)}) collective-permute-start(bf16[512,1024]{1,0:T(8,128)(2,1)S(1)} %copy-done), channel_id=1, source_target_pairs={{0,1},{1,0},{2,3},{3,2},{4,5},{5,4},{6,7},{7,6},{8,9},{9,8},{10,11... | collective-permute-start | bytes 3145736 | tf_op jit(solution)/shard_map/ppermute | solution.py:17
  6.5 4.0 %collective-permute-start.2 = (bf16[2,4,8,128]{3,2,1,0:T(8,128)(2,1)S(1)}, bf16[2,4,8,128]{3,2,1,0:T(8,128)(2,1)S(1)}, u32[]{:S(2)}, u32[]{:S(2)}) collective-permute-start(bf16[2,4,8,128]{3,2,1,0:T(8,128)(2,1)S(1)} %pad_maximum_fusion.2), channel_id=1, source_target_pairs={{0,3},{1,2},{2,1},{3,0},{4,7},{5,6},{6,5},{7,4},{8,11},{9,10},{10,... | collective-permute-start | bytes 49160 | tf_op jit(solution)/shard_map/ppermute | solution.py:17
  10.6 4.4 %collective-permute-start.3 = (bf16[3,4,8,128]{3,2,1,0:T(8,128)(2,1)S(1)}, bf16[3,4,8,128]{3,2,1,0:T(8,128)(2,1)S(1)}, u32[]{:S(2)}, u32[]{:S(2)}) collective-permute-start(bf16[3,4,8,128]{3,2,1,0:T(8,128)(2,1)S(1)} %pad_maximum_fusion.1), channel_id=1, source_target_pairs={{0,4},{1,9},{4,0},{5,13},{8,12},{9,1},{12,8},{13,5},{2,6},{3,11},{... | collective-permute-start | bytes 73736 | tf_op jit(solution)/shard_map/ppermute | solution.py:80
  12.5 5.6 %collective-permute-start.5 = (bf16[2,4,8,128]{3,2,1,0:T(8,128)(2,1)S(1)}, bf16[2,4,8,128]{3,2,1,0:T(8,128)(2,1)S(1)}, u32[]{:S(2)}, u32[]{:S(2)}) collective-permute-start(bf16[2,4,8,128]{3,2,1,0:T(8,128)(2,1)S(1)} %pad_maximum_fusion.3), channel_id=1, source_target_pairs={{0,12},{1,13},{4,8},{5,9},{8,4},{9,5},{12,0},{13,1},{2,14},{3,15},... | collective-permute-start | bytes 49160 | tf_op jit(solution)/shard_map/ppermute | solution.py:80
  15.0 3.1 %collective-permute-start.4 = (bf16[2,4,8,128]{3,2,1,0:T(8,128)(2,1)S(1)}, bf16[2,4,8,128]{3,2,1,0:T(8,128)(2,1)S(1)}, u32[]{:S(2)}, u32[]{:S(2)}) collective-permute-start(bf16[2,4,8,128]{3,2,1,0:T(8,128)(2,1)S(1)} %slice.4), channel_id=1, source_target_pairs={{0,1},{1,0},{2,3},{3,2},{4,5},{5,4},{6,7},{7,6},{8,9},{9,8},{10,11... | collective-permute-start | bytes 49160 | tf_op jit(solution)/shard_map/ppermute | solution.py:17
  18.5 4.0 %collective-permute-start.6 = (f32[8,256]{1,0:T(8,128)S(1)}, f32[8,256]{1,0:T(8,128)S(1)}, u32[]{:S(2)}, u32[]{:S(2)}) collective-permute-start(f32[8,256]{1,0:T(8,128)S(1)} %get-tuple-element.15), channel_id=1, source_target_pairs={{0,4},{1,9},{2,6},{3,11},{4,0},{5,13},{6,2},{7,15},{8,12},{9,1},{1... | collective-permute-start | bytes 24584 | tf_op jit(solution)/shard_map/ppermute | solution.py:289
  18.6 4.0 %collective-permute-start.7 = (f32[8,256]{1,0:T(8,128)S(1)}, f32[8,256]{1,0:T(8,128)S(1)}, u32[]{:S(2)}, u32[]{:S(2)}) collective-permute-start(f32[8,256]{1,0:T(8,128)S(1)} %get-tuple-element.16), channel_id=1, source_target_pairs={{0,2},{1,13},{2,0},{3,15},{4,6},{5,9},{6,4},{7,11},{8,10},{9,5},{1... | collective-permute-start | bytes 24584 | tf_op jit(solution)/shard_map/ppermute | solution.py:289
  22.6 1.5 %collective-permute-start.8 = (f32[4,1,256]{2,1,0:T(1,128)S(1)}, f32[4,1,256]{2,1,0:T(1,128)S(1)}, u32[]{:S(2)}, u32[]{:S(2)}) collective-permute-start(f32[4,1,256]{2,1,0:T(1,128)S(1)} %dynamic-slice_bitcast_fusion), channel_id=1, source_target_pairs={{0,1},{1,0},{2,3},{3,2},{4,5},{5,4},{6,7},{7,6},{8,9},{9,8},{10,11... | collective-permute-start | bytes 12296 | tf_op jit(solution)/shard_map/ppermute | solution.py:17
